TPU v7x, 256 devices: a whole 4x4x8 slice. The times are simulated.
256 devices in a mesh: orb: 64 (over y_hi, x, z), grid: 4 (over y_lo, core).
Axes of the slice: x: 4, y: 4 (y_hi: 2, y_lo: 2; y = y_hi * 2 + y_lo), z: 8, core: 2. Of those that a mesh axis runs over, the one named last changes fastest.
Arguments:
- orbitals: float32 [64, 373248], P('orb', 'grid'), may hold values from -12 to 12
Outputs:
- residual: float32 [64, 373248], P('orb', 'grid')
- intersection: float32 [64, 1, 1], P('orb')
All inputs are finite; a program needn't handle non-finite values.
Results may differ from a plain program's by a relative error of at most 0.00023.
Values sent between devices are 32-bit elements; how exact they have to be, the bound alone decides.
No kernel may reach another device: no remote copies, remote signals or barrier semaphores. Data moves between devices by JAX's collectives and lax.ppermute only.
A program may use at most 64 MiB of HBM per device.

v0:
```python
import math

import jax
import jax.numpy as jnp
from jax import lax
from jax.sharding import PartitionSpec as P

G = 72
REACH = 4


SCREENING = 0.09
FRACTION = 0.25
HIGHEST_PRECISION = lax.Precision.HIGHEST


def shifted(value, axis, steps):
    count = lax.axis_size(axis)
    pairs = [(source, (source + steps) % count) for source in range(count)]
    return lax.ppermute(value, axis, pairs)


def hartley_table(length):
    indices = jnp.arange(length, dtype=jnp.int32)
    phases = (indices[:, None] * indices[None, :] % length).astype(jnp.float32) * (
        2.0 * math.pi / length
    )
    return jnp.cos(phases) + jnp.sin(phases)


def wavenumber(indices, length):
    return jnp.minimum(indices, length - indices).astype(jnp.float32) * (2.0 * math.pi / length)


def screened(first, second, third):
    squared = first[:, None, None] ** 2 + second[None, :, None] ** 2 + third[None, None, :] ** 2
    scaled = squared / (4.0 * SCREENING * SCREENING)
    guarded = jnp.where(scaled > 0, scaled, 1.0)
    return jnp.where(scaled > 0, (1.0 - jnp.exp(-guarded)) / guarded, 1.0)


def shards(orbitals):
    num_orbitals = orbitals.shape[0]
    slab_planes = G // lax.axis_size("grid")
    pencil_rows = G // lax.axis_size("grid")
    hartley = hartley_table(G)
    all_indices = jnp.arange(G, dtype=jnp.int32)
    local_rows = lax.axis_index("grid") * pencil_rows + jnp.arange(pencil_rows, dtype=jnp.int32)
    kernel = screened(
        wavenumber(all_indices, G), wavenumber(local_rows, G), wavenumber(all_indices, G)
    ) / float(G * G * G)

    def pencil_step(pencil):
        spectral = jnp.einsum("pxyz,kx->pkyz", pencil, hartley, precision=HIGHEST_PRECISION)
        spectral = spectral * kernel[None]
        spectral = jnp.einsum("pxyz,kx->pkyz", spectral, hartley, precision=HIGHEST_PRECISION)
        return lax.all_to_all(spectral, "grid", split_axis=1, concat_axis=2, tiled=True)

    def poisson(density):
        num_pairs = density.shape[0]
        slab = density.reshape(num_pairs, slab_planes, G, G)
        slab = jnp.einsum("pxyz,kz->pxyk", slab, hartley, precision=HIGHEST_PRECISION)
        slab = jnp.einsum("pxyz,ky->pxkz", slab, hartley, precision=HIGHEST_PRECISION)
        slab = pencil_step(lax.all_to_all(slab, "grid", split_axis=2, concat_axis=1, tiled=True))
        slab = jnp.einsum("pxyz,ky->pxkz", slab, hartley, precision=HIGHEST_PRECISION)
        slab = jnp.einsum("pxyz,kz->pxyk", slab, hartley, precision=HIGHEST_PRECISION)
        return slab.reshape(num_pairs, -1)

    def pair_potential(target, source):
        densities = (target[:, None, :] * source[None, :, :]).reshape(
            num_orbitals * source.shape[0], -1
        )
        return poisson(densities).reshape(num_orbitals, source.shape[0], -1)

    potential = pair_potential(orbitals, orbitals)
    exchange = jnp.sum(potential * orbitals[None, :, :], axis=1)
    behind = orbitals
    ahead = orbitals
    for offset in range(REACH):
        behind = shifted(behind, "orb", 1)
        ahead = shifted(ahead, "orb", -1)
        for source in (behind, ahead):
            potential = pair_potential(orbitals, source)
            exchange = exchange + jnp.sum(potential * source[None, :, :], axis=1)
    exchange = -FRACTION * exchange
    partial_value = jnp.einsum(
        "ac,bc->ab", orbitals, exchange, precision=HIGHEST_PRECISION
    ) / float(G * G * G)
    intersection = lax.psum(partial_value, "grid")
    residual = exchange - jnp.einsum(
        "ab,ac->bc", intersection, orbitals, precision=HIGHEST_PRECISION
    )
    return (residual, intersection[None])


def solution(mesh):
    in_specs = (P("orb", "grid"),)
    out_specs = (P("orb", "grid"), P("orb", None, None))
    return jax.shard_map(shards, mesh=mesh, in_specs=in_specs, out_specs=out_specs, check_vma=False)
```

profile of v0, /device:TPU:1, one launch (start us, length us, event | category | flops | bytes accessed | tf_op | source)
XLA Modules:
  0.0 414.8 jit_solution(9782806568735996791)
XLA Ops:
  0.6 2.5 collective-permute-start
  3.2 8.9 %collective-permute-start.1 = (f32[1,93312]{1,0:T(1,128)}, f32[1,93312]{1,0:T(1,128)S(1)}, u32[]{:S(2)}, u32[]{:S(2)}) collective-permute-start(f32[1,93312]{1,0:T(1,128)} %param.1), channel_id=1, source_target_pairs={{0,252},{4,0},{8,4},{12,8},{16,12},{20,16},{24,20},{28,24},{32,28}... | collective-permute-start | bytes 1119752 | tf_op jit(solution)/shard_map/ppermute | solution.py:20
  12.0 8.5 %collective-permute-done = f32[1,93312]{1,0:T(1,128)S(1)} collective-permute-done((f32[1,93312]{1,0:T(1,128)}, f32[1,93312]{1,0:T(1,128)S(1)}, u32[]{:S(2)}, u32[]{:S(2)}) %collective-permute-start) | collective-permute-done | bytes 373280 | tf_op jit(solution)/shard_map/ppermute | solution.py:20
  20.6 7.2 %collective-permute-start.3 = (f32[1,93312]{1,0:T(1,128)S(1)}, f32[1,93312]{1,0:T(1,128)S(1)}, u32[]{:S(2)}, u32[]{:S(2)}) collective-permute-start(f32[1,93312]{1,0:T(1,128)S(1)} %collective-permute-done.1), channel_id=1, source_target_pairs={{0,252},{4,0},{8,4},{12,8},{16,12},{20,16},{24,20},{28,24},{32,28}... | collective-permute-start | bytes 1119752 | tf_op jit(solution)/shard_map/ppermute | solution.py:20
  27.8 7.5 %collective-permute-done.2 = f32[1,93312]{1,0:T(1,128)S(1)} collective-permute-done((f32[1,93312]{1,0:T(1,128)S(1)}, f32[1,93312]{1,0:T(1,128)S(1)}, u32[]{:S(2)}, u32[]{:S(2)}) %collective-permute-start.2) | collective-permute-done | bytes 373280 | tf_op jit(solution)/shard_map/ppermute | solution.py:20
  36.0 6.5 %collective-permute-start.5 = (f32[1,93312]{1,0:T(1,128)S(1)}, f32[1,93312]{1,0:T(1,128)S(1)}, u32[]{:S(2)}, u32[]{:S(2)}) collective-permute-start(f32[1,93312]{1,0:T(1,128)S(1)} %collective-permute-done.3), channel_id=1, source_target_pairs={{0,252},{4,0},{8,4},{12,8},{16,12},{20,16},{24,20},{28,24},{32,28}... | collective-permute-start | bytes 1119752 | tf_op jit(solution)/shard_map/ppermute | solution.py:20
  42.5 6.5 %collective-permute-done.4 = f32[1,93312]{1,0:T(1,128)S(1)} collective-permute-done((f32[1,93312]{1,0:T(1,128)S(1)}, f32[1,93312]{1,0:T(1,128)S(1)}, u32[]{:S(2)}, u32[]{:S(2)}) %collective-permute-start.4) | collective-permute-done | bytes 373280 | tf_op jit(solution)/shard_map/ppermute | solution.py:20
  49.0 7.6 %collective-permute-start.7 = (f32[1,93312]{1,0:T(1,128)S(1)}, f32[1,93312]{1,0:T(1,128)}, u32[]{:S(2)}, u32[]{:S(2)}) collective-permute-start(f32[1,93312]{1,0:T(1,128)S(1)} %collective-permute-done.5), channel_id=1, source_target_pairs={{0,252},{4,0},{8,4},{12,8},{16,12},{20,16},{24,20},{28,24},{32,28}... | collective-permute-start | bytes 1119752 | tf_op jit(solution)/shard_map/ppermute | solution.py:20
  56.7 5.1 %collective-permute-done.6 = f32[1,93312]{1,0:T(1,128)S(1)} collective-permute-done((f32[1,93312]{1,0:T(1,128)S(1)}, f32[1,93312]{1,0:T(1,128)S(1)}, u32[]{:S(2)}, u32[]{:S(2)}) %collective-permute-start.6) | collective-permute-done | bytes 373280 | tf_op jit(solution)/shard_map/ppermute | solution.py:20
  62.6 13.6 %multiply_reduce_fusion.10 = (f32[93312]{0:T(1024)S(1)}, f32[93312]{0:T(1024)}, f32[93312]{0:T(1024)}, f32[93312]{0:T(1024)}, f32[93312]{0:T(1024)S(1)}, /*index...) fusion(f32[1,93312]{1,0:T(1,128)} %param.1, f32[1,93312]{1,0:T(1,128)} %copy-done.9, ...), kind=kLoop, calls=%fused_computation.50 | loop fusion | flops 839808 | bytes 6718464 | tf_op jit(solution)/shard_map/mul | solution.py:70
  80.0 7.6 %all-to-all-start = ((f32[1,18,72,72]{3,0,1,2:T(1,128)}), f32[1,18,72,72]{3,0,1,2:T(1,128)S(1)}, u32[]{:S(2)}, u32[]{:S(2)}) async-start(f32[1,18,72,72]{3,0,1,2:T(1,128)} %copy.84), calls=%async_computation | async-start | bytes 1327104 | tf_op jit(solution)/shard_map/all_to_all | solution.py:64
  121.3 3.9 all-to-all-start.14
  129.4 5.3 %all-to-all-done.14 = f32[1,18,72,72]{3,0,1,2:T(1,128)S(1)} async-done(((f32[1,18,72,72]{3,0,1,2:T(1,128)}), f32[1,18,72,72]{3,0,1,2:T(1,128)S(1)}, u32[]{:S(2)}, u32[]{:S(2)}) %all-to-all-start.14) | async-done | bytes 373280 | tf_op jit(solution)/shard_map/all_to_all | solution.py:64
  134.7 4.3 %all-to-all-start.12 = ((f32[1,18,72,72]{3,0,1,2:T(1,128)}), f32[1,18,72,72]{3,0,1,2:T(1,128)S(1)}, u32[]{:S(2)}, u32[]{:S(2)}) async-start(f32[1,18,72,72]{3,0,1,2:T(1,128)} %copy.114), calls=%async_computation.12 | async-start | bytes 1327104 | tf_op jit(solution)/shard_map/all_to_all | solution.py:64
  143.1 5.4 %all-to-all-done.12 = f32[1,18,72,72]{3,0,1,2:T(1,128)S(1)} async-done(((f32[1,18,72,72]{3,0,1,2:T(1,128)}), f32[1,18,72,72]{3,0,1,2:T(1,128)S(1)}, u32[]{:S(2)}, u32[]{:S(2)}) %all-to-all-start.12) | async-done | bytes 373280 | tf_op jit(solution)/shard_map/all_to_all | solution.py:64
  148.5 4.3 %all-to-all-start.10 = ((f32[1,18,72,72]{3,0,1,2:T(1,128)}), f32[1,18,72,72]{3,0,1,2:T(1,128)S(1)}, u32[]{:S(2)}, u32[]{:S(2)}) async-start(f32[1,18,72,72]{3,0,1,2:T(1,128)} %copy.109), calls=%async_computation.10 | async-start | bytes 1327104 | tf_op jit(solution)/shard_map/all_to_all | solution.py:64
  156.9 5.4 %all-to-all-done.10 = f32[1,18,72,72]{3,0,1,2:T(1,128)S(1)} async-done(((f32[1,18,72,72]{3,0,1,2:T(1,128)}), f32[1,18,72,72]{3,0,1,2:T(1,128)S(1)}, u32[]{:S(2)}, u32[]{:S(2)}) %all-to-all-start.10) | async-done | bytes 373280 | tf_op jit(solution)/shard_map/all_to_all | solution.py:64
  162.3 4.5 %all-to-all-start.8 = ((f32[1,18,72,72]{3,0,1,2:T(1,128)}), f32[1,18,72,72]{3,0,1,2:T(1,128)S(1)}, u32[]{:S(2)}, u32[]{:S(2)}) async-start(f32[1,18,72,72]{3,0,1,2:T(1,128)} %copy.104), calls=%async_computation.8 | async-start | bytes 1327104 | tf_op jit(solution)/shard_map/all_to_all | solution.py:64
  170.9 5.4 %all-to-all-done.8 = f32[1,18,72,72]{3,0,1,2:T(1,128)S(1)} async-done(((f32[1,18,72,72]{3,0,1,2:T(1,128)}), f32[1,18,72,72]{3,0,1,2:T(1,128)S(1)}, u32[]{:S(2)}, u32[]{:S(2)}) %all-to-all-start.8) | async-done | bytes 373280 | tf_op jit(solution)/shard_map/all_to_all | solution.py:64
  176.2 4.3 %all-to-all-start.6 = ((f32[1,18,72,72]{3,0,1,2:T(1,128)}), f32[1,18,72,72]{3,0,1,2:T(1,128)S(1)}, u32[]{:S(2)}, u32[]{:S(2)}) async-start(f32[1,18,72,72]{3,0,1,2:T(1,128)} %copy.99), calls=%async_computation.6 | async-start | bytes 1327104 | tf_op jit(solution)/shard_map/all_to_all | solution.py:64
  184.7 5.3 %all-to-all-done.6 = f32[1,18,72,72]{3,0,1,2:T(1,128)S(1)} async-done(((f32[1,18,72,72]{3,0,1,2:T(1,128)}), f32[1,18,72,72]{3,0,1,2:T(1,128)S(1)}, u32[]{:S(2)}, u32[]{:S(2)}) %all-to-all-start.6) | async-done | bytes 373280 | tf_op jit(solution)/shard_map/all_to_all | solution.py:64
  190.0 4.3 %all-to-all-start.4 = ((f32[1,18,72,72]{3,0,1,2:T(1,128)}), f32[1,18,72,72]{3,0,1,2:T(1,128)S(1)}, u32[]{:S(2)}, u32[]{:S(2)}) async-start(f32[1,18,72,72]{3,0,1,2:T(1,128)} %copy.94), calls=%async_computation.4 | async-start | bytes 1327104 | tf_op jit(solution)/shard_map/all_to_all | solution.py:64
  198.4 5.4 %all-to-all-done.4 = f32[1,18,72,72]{3,0,1,2:T(1,128)S(1)} async-done(((f32[1,18,72,72]{3,0,1,2:T(1,128)}), f32[1,18,72,72]{3,0,1,2:T(1,128)S(1)}, u32[]{:S(2)}, u32[]{:S(2)}) %all-to-all-start.4) | async-done | bytes 373280 | tf_op jit(solution)/shard_map/all_to_all | solution.py:64
  203.8 4.5 %all-to-all-start.2 = ((f32[1,18,72,72]{3,0,1,2:T(1,128)}), f32[1,18,72,72]{3,0,1,2:T(1,128)S(1)}, u32[]{:S(2)}, u32[]{:S(2)}) async-start(f32[1,18,72,72]{3,0,1,2:T(1,128)} %copy.89), calls=%async_computation.2 | async-start | bytes 1327104 | tf_op jit(solution)/shard_map/all_to_all | solution.py:64
  212.4 5.4 %all-to-all-done.2 = f32[1,18,72,72]{3,0,1,2:T(1,128)S(1)} async-done(((f32[1,18,72,72]{3,0,1,2:T(1,128)}), f32[1,18,72,72]{3,0,1,2:T(1,128)S(1)}, u32[]{:S(2)}, u32[]{:S(2)}) %all-to-all-start.2) | async-done | bytes 373280 | tf_op jit(solution)/shard_map/all_to_all | solution.py:64
  217.8 4.3 %all-to-all-start.16 = ((f32[1,18,72,72]{3,0,1,2:T(1,128)}), f32[1,18,72,72]{3,0,1,2:T(1,128)S(1)}, u32[]{:S(2)}, u32[]{:S(2)}) async-start(f32[1,18,72,72]{3,0,1,2:T(1,128)} %copy.124), calls=%async_computation.16 | async-start | bytes 1327104 | tf_op jit(solution)/shard_map/all_to_all | solution.py:64
  226.2 5.4 %all-to-all-done.16 = f32[1,18,72,72]{3,0,1,2:T(1,128)S(1)} async-done(((f32[1,18,72,72]{3,0,1,2:T(1,128)}), f32[1,18,72,72]{3,0,1,2:T(1,128)S(1)}, u32[]{:S(2)}, u32[]{:S(2)}) %all-to-all-start.16) | async-done | bytes 373280 | tf_op jit(solution)/shard_map/all_to_all | solution.py:64
  231.6 4.3 %all-to-all-start.1 = ((f32[1,72,18,72]{3,0,2,1:T(1,128)}), f32[1,72,18,72]{3,0,2,1:T(1,128)S(1)}, u32[]{:S(2)}, u32[]{:S(2)}) async-start(f32[1,72,18,72]{3,0,2,1:T(1,128)} %copy.87), calls=%async_computation.1 | async-start | bytes 1327104 | tf_op jit(solution)/shard_map/all_to_all | solution.py:57
  240.0 5.4 %all-to-all-done.1 = f32[1,72,18,72]{3,0,2,1:T(1,128)S(1)} async-done(((f32[1,72,18,72]{3,0,2,1:T(1,128)}), f32[1,72,18,72]{3,0,2,1:T(1,128)S(1)}, u32[]{:S(2)}, u32[]{:S(2)}) %all-to-all-start.1) | async-done | bytes 373280 | tf_op jit(solution)/shard_map/all_to_all | solution.py:57
  245.4 4.3 %all-to-all-start.15 = ((f32[1,72,18,72]{3,0,2,1:T(1,128)}), f32[1,72,18,72]{3,0,2,1:T(1,128)S(1)}, u32[]{:S(2)}, u32[]{:S(2)}) async-start(f32[1,72,18,72]{3,0,2,1:T(1,128)} %copy.122), calls=%async_computation.15 | async-start | bytes 1327104 | tf_op jit(solution)/shard_map/all_to_all | solution.py:57
  251.6 7.6 %all-to-all-done.15 = f32[1,72,18,72]{3,0,2,1:T(1,128)S(1)} async-done(((f32[1,72,18,72]{3,0,2,1:T(1,128)}), f32[1,72,18,72]{3,0,2,1:T(1,128)S(1)}, u32[]{:S(2)}, u32[]{:S(2)}) %all-to-all-start.15) | async-done | bytes 373280 | tf_op jit(solution)/shard_map/all_to_all | solution.py:57
  259.2 4.7 %all-to-all-start.13 = ((f32[1,72,18,72]{3,0,2,1:T(1,128)}), f32[1,72,18,72]{3,0,2,1:T(1,128)S(1)}, u32[]{:S(2)}, u32[]{:S(2)}) async-start(f32[1,72,18,72]{3,0,2,1:T(1,128)} %copy.117), calls=%async_computation.13 | async-start | bytes 1327104 | tf_op jit(solution)/shard_map/all_to_all | solution.py:57
  265.8 7.6 %all-to-all-done.13 = f32[1,72,18,72]{3,0,2,1:T(1,128)S(1)} async-done(((f32[1,72,18,72]{3,0,2,1:T(1,128)}), f32[1,72,18,72]{3,0,2,1:T(1,128)S(1)}, u32[]{:S(2)}, u32[]{:S(2)}) %all-to-all-start.13) | async-done | bytes 373280 | tf_op jit(solution)/shard_map/all_to_all | solution.py:57
  273.4 4.3 %all-to-all-start.11 = ((f32[1,72,18,72]{3,0,2,1:T(1,128)}), f32[1,72,18,72]{3,0,2,1:T(1,128)S(1)}, u32[]{:S(2)}, u32[]{:S(2)}) async-start(f32[1,72,18,72]{3,0,2,1:T(1,128)} %copy.112), calls=%async_computation.11 | async-start | bytes 1327104 | tf_op jit(solution)/shard_map/all_to_all | solution.py:57
  279.6 7.6 %all-to-all-done.11 = f32[1,72,18,72]{3,0,2,1:T(1,128)S(1)} async-done(((f32[1,72,18,72]{3,0,2,1:T(1,128)}), f32[1,72,18,72]{3,0,2,1:T(1,128)S(1)}, u32[]{:S(2)}, u32[]{:S(2)}) %all-to-all-start.11) | async-done | bytes 373280 | tf_op jit(solution)/shard_map/all_to_all | solution.py:57
  287.2 5.0 %all-to-all-start.9 = ((f32[1,72,18,72]{3,0,2,1:T(1,128)}), f32[1,72,18,72]{3,0,2,1:T(1,128)}, u32[]{:S(2)}, u32[]{:S(2)}) async-start(f32[1,72,18,72]{3,0,2,1:T(1,128)} %copy.107), calls=%async_computation.9 | async-start | bytes 1327104 | tf_op jit(solution)/shard_map/all_to_all | solution.py:57
  294.1 7.7 %all-to-all-done.9 = f32[1,72,18,72]{3,0,2,1:T(1,128)} async-done(((f32[1,72,18,72]{3,0,2,1:T(1,128)}), f32[1,72,18,72]{3,0,2,1:T(1,128)}, u32[]{:S(2)}, u32[]{:S(2)}) %all-to-all-start.9) | async-done | bytes 373280 | tf_op jit(solution)/shard_map/all_to_all | solution.py:57
  301.8 5.0 %all-to-all-start.7 = ((f32[1,72,18,72]{3,0,2,1:T(1,128)}), f32[1,72,18,72]{3,0,2,1:T(1,128)}, u32[]{:S(2)}, u32[]{:S(2)}) async-start(f32[1,72,18,72]{3,0,2,1:T(1,128)} %copy.102), calls=%async_computation.7 | async-start | bytes 1327104 | tf_op jit(solution)/shard_map/all_to_all | solution.py:57
  311.7 4.7 %all-to-all-done.7 = f32[1,72,18,72]{3,0,2,1:T(1,128)} async-done(((f32[1,72,18,72]{3,0,2,1:T(1,128)}), f32[1,72,18,72]{3,0,2,1:T(1,128)}, u32[]{:S(2)}, u32[]{:S(2)}) %all-to-all-start.7) | async-done | bytes 373280 | tf_op jit(solution)/shard_map/all_to_all | solution.py:57
  316.3 5.0 %all-to-all-start.5 = ((f32[1,72,18,72]{3,0,2,1:T(1,128)}), f32[1,72,18,72]{3,0,2,1:T(1,128)}, u32[]{:S(2)}, u32[]{:S(2)}) async-start(f32[1,72,18,72]{3,0,2,1:T(1,128)} %copy.97), calls=%async_computation.5 | async-start | bytes 1327104 | tf_op jit(solution)/shard_map/all_to_all | solution.py:57
  321.3 2.1 copy.103
  330.9 5.0 %all-to-all-start.3 = ((f32[1,72,18,72]{3,0,2,1:T(1,128)}), f32[1,72,18,72]{3,0,2,1:T(1,128)}, u32[]{:S(2)}, u32[]{:S(2)}) async-start(f32[1,72,18,72]{3,0,2,1:T(1,128)} %copy.92), calls=%async_computation.3 | async-start | bytes 1327104 | tf_op jit(solution)/shard_map/all_to_all | solution.py:57
  335.9 2.1 copy.98
  345.5 5.1 %all-to-all-start.17 = ((f32[1,72,18,72]{3,0,2,1:T(1,128)}), f32[1,72,18,72]{3,0,2,1:T(1,128)}, u32[]{:S(2)}, u32[]{:S(2)}) async-start(f32[1,72,18,72]{3,0,2,1:T(1,128)} %copy.127), calls=%async_computation.17 | async-start | bytes 1327104 | tf_op jit(solution)/shard_map/all_to_all | solution.py:57
  354.8 2.8 convolution_bitcast_fusion.21
  388.0 14.9 %multiply_reduce_fusion.1 = (f32[93312]{0:T(1024)S(1)}, f32[93312]{0:T(1024)S(1)}, f32[93312]{0:T(1024)S(1)}, f32[93312]{0:T(1024)S(1)}, f32[93312]{0:T(1024)S(1...) fusion(f32[1,93312]{1,0:T(1,128)} %reshape_reshape.71, ...), kind=kLoop, calls=%fused_computation.41 | loop fusion | flops 1679616 | bytes 10450944 | tf_op jit(solution)/shard_map/mul | solution.py:85
  404.2 6.5 %psum.7 = f32[1,1]{1,0:T(1,128)} all-reduce(f32[1,1]{1,0:T(1,128)} %bitcast.91), channel_id=1, replica_groups=mesh['orb'=64,'grid'=4] {'grid'}, use_global_device_ids=true, to_apply=%region_0.1 | all-reduce | flops 1 | bytes 8 | tf_op jit(solution)/shard_map/psum | solution.py:89
  410.8 2.8 multiply_subtract_fusion
  (177 shorter events, 138.8 us)
Async XLA Ops:
  0.6 19.9 %collective-permute-start = (f32[1,93312]{1,0:T(1,128)}, f32[1,93312]{1,0:T(1,128)S(1)}, u32[]{:S(2)}, u32[]{:S(2)}) collective-permute-start(f32[1,93312]{1,0:T(1,128)} %param.1), channel_id=1, source_target_pairs={{0,4},{4,8},{8,12},{12,16},{16,20},{20,24},{24,28},{28,32},{32,36}... | collective-permute-start | bytes 1119752 | tf_op jit(solution)/shard_map/ppermute | solution.py:20
  3.2 17.4 %collective-permute-start.1 = (f32[1,93312]{1,0:T(1,128)}, f32[1,93312]{1,0:T(1,128)S(1)}, u32[]{:S(2)}, u32[]{:S(2)}) collective-permute-start(f32[1,93312]{1,0:T(1,128)} %param.1), channel_id=1, source_target_pairs={{0,252},{4,0},{8,4},{12,8},{16,12},{20,16},{24,20},{28,24},{32,28}... | collective-permute-start | bytes 1119752 | tf_op jit(solution)/shard_map/ppermute | solution.py:20
  20.6 55.6 %copy-start.3 = (f32[1,93312]{1,0:T(1,128)}, f32[1,93312]{1,0:T(1,128)S(1)}, u32[]{:S(2)}) copy-start(f32[1,93312]{1,0:T(1,128)S(1)} %collective-permute-done) | copy-start | bytes 1119748
  20.6 14.7 %collective-permute-start.2 = (f32[1,93312]{1,0:T(1,128)S(1)}, f32[1,93312]{1,0:T(1,128)S(1)}, u32[]{:S(2)}, u32[]{:S(2)}) collective-permute-start(f32[1,93312]{1,0:T(1,128)S(1)} %collective-permute-done), channel_id=1, source_target_pairs={{0,4},{4,8},{8,12},{12,16},{16,20},{20,24},{24,28},{28,32},{32,36}... | collective-permute-start | bytes 1119752 | tf_op jit(solution)/shard_map/ppermute | solution.py:20
  20.6 14.7 %copy-start.4 = (f32[1,93312]{1,0:T(1,128)}, f32[1,93312]{1,0:T(1,128)S(1)}, u32[]{:S(2)}) copy-start(f32[1,93312]{1,0:T(1,128)S(1)} %collective-permute-done.1) | copy-start | bytes 1119748
  20.6 14.7 %collective-permute-start.3 = (f32[1,93312]{1,0:T(1,128)S(1)}, f32[1,93312]{1,0:T(1,128)S(1)}, u32[]{:S(2)}, u32[]{:S(2)}) collective-permute-start(f32[1,93312]{1,0:T(1,128)S(1)} %collective-permute-done.1), channel_id=1, source_target_pairs={{0,252},{4,0},{8,4},{12,8},{16,12},{20,16},{24,20},{28,24},{32,28}... | collective-permute-start | bytes 1119752 | tf_op jit(solution)/shard_map/ppermute | solution.py:20
  35.2 0.8 copy-start.5
  35.2 13.8 %collective-permute-start.4 = (f32[1,93312]{1,0:T(1,128)S(1)}, f32[1,93312]{1,0:T(1,128)S(1)}, u32[]{:S(2)}, u32[]{:S(2)}) collective-permute-start(f32[1,93312]{1,0:T(1,128)S(1)} %collective-permute-done.2), channel_id=1, source_target_pairs={{0,4},{4,8},{8,12},{12,16},{16,20},{20,24},{24,28},{28,32},{32,36}... | collective-permute-start | bytes 1119752 | tf_op jit(solution)/shard_map/ppermute | solution.py:20
  36.0 13.0 %copy-start.6 = (f32[1,93312]{1,0:T(1,128)}, f32[1,93312]{1,0:T(1,128)S(1)}, u32[]{:S(2)}) copy-start(f32[1,93312]{1,0:T(1,128)S(1)} %collective-permute-done.3) | copy-start | bytes 1119748
  36.0 13.0 %collective-permute-start.5 = (f32[1,93312]{1,0:T(1,128)S(1)}, f32[1,93312]{1,0:T(1,128)S(1)}, u32[]{:S(2)}, u32[]{:S(2)}) collective-permute-start(f32[1,93312]{1,0:T(1,128)S(1)} %collective-permute-done.3), channel_id=1, source_target_pairs={{0,252},{4,0},{8,4},{12,8},{16,12},{20,16},{24,20},{28,24},{32,28}... | collective-permute-start | bytes 1119752 | tf_op jit(solution)/shard_map/ppermute | solution.py:20
  49.0 12.8 %copy-start.7 = (f32[1,93312]{1,0:T(1,128)}, f32[1,93312]{1,0:T(1,128)S(1)}, u32[]{:S(2)}) copy-start(f32[1,93312]{1,0:T(1,128)S(1)} %collective-permute-done.4) | copy-start | bytes 1119748
  49.0 12.8 %collective-permute-start.6 = (f32[1,93312]{1,0:T(1,128)S(1)}, f32[1,93312]{1,0:T(1,128)S(1)}, u32[]{:S(2)}, u32[]{:S(2)}) collective-permute-start(f32[1,93312]{1,0:T(1,128)S(1)} %collective-permute-done.4), channel_id=1, source_target_pairs={{0,4},{4,8},{8,12},{12,16},{16,20},{20,24},{24,28},{28,32},{32,36}... | collective-permute-start | bytes 1119752 | tf_op jit(solution)/shard_map/ppermute | solution.py:20
  49.0 12.8 %copy-start.8 = (f32[1,93312]{1,0:T(1,128)}, f32[1,93312]{1,0:T(1,128)S(1)}, u32[]{:S(2)}) copy-start(f32[1,93312]{1,0:T(1,128)S(1)} %collective-permute-done.5) | copy-start | bytes 1119748
  49.0 13.6 %collective-permute-start.7 = (f32[1,93312]{1,0:T(1,128)S(1)}, f32[1,93312]{1,0:T(1,128)}, u32[]{:S(2)}, u32[]{:S(2)}) collective-permute-start(f32[1,93312]{1,0:T(1,128)S(1)} %collective-permute-done.5), channel_id=1, source_target_pairs={{0,252},{4,0},{8,4},{12,8},{16,12},{20,16},{24,20},{28,24},{32,28}... | collective-permute-start | bytes 1119752 | tf_op jit(solution)/shard_map/ppermute | solution.py:20
  61.8 0.7 copy-start.9
  80.0 41.3 %all-to-all-start = ((f32[1,18,72,72]{3,0,1,2:T(1,128)}), f32[1,18,72,72]{3,0,1,2:T(1,128)S(1)}, u32[]{:S(2)}, u32[]{:S(2)}) async-start(f32[1,18,72,72]{3,0,1,2:T(1,128)} %copy.84), calls=%async_computation | async-start | bytes 1327104 | tf_op jit(solution)/shard_map/all_to_all | solution.py:64
  121.3 13.4 %all-to-all-start.14 = ((f32[1,18,72,72]{3,0,1,2:T(1,128)}), f32[1,18,72,72]{3,0,1,2:T(1,128)S(1)}, u32[]{:S(2)}, u32[]{:S(2)}) async-start(f32[1,18,72,72]{3,0,1,2:T(1,128)} %copy.119), calls=%async_computation.14 | async-start | bytes 1327104 | tf_op jit(solution)/shard_map/all_to_all | solution.py:64
  134.7 13.8 %all-to-all-start.12 = ((f32[1,18,72,72]{3,0,1,2:T(1,128)}), f32[1,18,72,72]{3,0,1,2:T(1,128)S(1)}, u32[]{:S(2)}, u32[]{:S(2)}) async-start(f32[1,18,72,72]{3,0,1,2:T(1,128)} %copy.114), calls=%async_computation.12 | async-start | bytes 1327104 | tf_op jit(solution)/shard_map/all_to_all | solution.py:64
  148.5 13.8 %all-to-all-start.10 = ((f32[1,18,72,72]{3,0,1,2:T(1,128)}), f32[1,18,72,72]{3,0,1,2:T(1,128)S(1)}, u32[]{:S(2)}, u32[]{:S(2)}) async-start(f32[1,18,72,72]{3,0,1,2:T(1,128)} %copy.109), calls=%async_computation.10 | async-start | bytes 1327104 | tf_op jit(solution)/shard_map/all_to_all | solution.py:64
  162.3 13.9 %all-to-all-start.8 = ((f32[1,18,72,72]{3,0,1,2:T(1,128)}), f32[1,18,72,72]{3,0,1,2:T(1,128)S(1)}, u32[]{:S(2)}, u32[]{:S(2)}) async-start(f32[1,18,72,72]{3,0,1,2:T(1,128)} %copy.104), calls=%async_computation.8 | async-start | bytes 1327104 | tf_op jit(solution)/shard_map/all_to_all | solution.py:64
  176.2 13.8 %all-to-all-start.6 = ((f32[1,18,72,72]{3,0,1,2:T(1,128)}), f32[1,18,72,72]{3,0,1,2:T(1,128)S(1)}, u32[]{:S(2)}, u32[]{:S(2)}) async-start(f32[1,18,72,72]{3,0,1,2:T(1,128)} %copy.99), calls=%async_computation.6 | async-start | bytes 1327104 | tf_op jit(solution)/shard_map/all_to_all | solution.py:64
  190.0 13.8 %all-to-all-start.4 = ((f32[1,18,72,72]{3,0,1,2:T(1,128)}), f32[1,18,72,72]{3,0,1,2:T(1,128)S(1)}, u32[]{:S(2)}, u32[]{:S(2)}) async-start(f32[1,18,72,72]{3,0,1,2:T(1,128)} %copy.94), calls=%async_computation.4 | async-start | bytes 1327104 | tf_op jit(solution)/shard_map/all_to_all | solution.py:64
  203.8 14.0 %all-to-all-start.2 = ((f32[1,18,72,72]{3,0,1,2:T(1,128)}), f32[1,18,72,72]{3,0,1,2:T(1,128)S(1)}, u32[]{:S(2)}, u32[]{:S(2)}) async-start(f32[1,18,72,72]{3,0,1,2:T(1,128)} %copy.89), calls=%async_computation.2 | async-start | bytes 1327104 | tf_op jit(solution)/shard_map/all_to_all | solution.py:64
  217.8 13.8 %all-to-all-start.16 = ((f32[1,18,72,72]{3,0,1,2:T(1,128)}), f32[1,18,72,72]{3,0,1,2:T(1,128)S(1)}, u32[]{:S(2)}, u32[]{:S(2)}) async-start(f32[1,18,72,72]{3,0,1,2:T(1,128)} %copy.124), calls=%async_computation.16 | async-start | bytes 1327104 | tf_op jit(solution)/shard_map/all_to_all | solution.py:64
  231.6 13.8 %all-to-all-start.1 = ((f32[1,72,18,72]{3,0,2,1:T(1,128)}), f32[1,72,18,72]{3,0,2,1:T(1,128)S(1)}, u32[]{:S(2)}, u32[]{:S(2)}) async-start(f32[1,72,18,72]{3,0,2,1:T(1,128)} %copy.87), calls=%async_computation.1 | async-start | bytes 1327104 | tf_op jit(solution)/shard_map/all_to_all | solution.py:57
  245.4 13.8 %all-to-all-start.15 = ((f32[1,72,18,72]{3,0,2,1:T(1,128)}), f32[1,72,18,72]{3,0,2,1:T(1,128)S(1)}, u32[]{:S(2)}, u32[]{:S(2)}) async-start(f32[1,72,18,72]{3,0,2,1:T(1,128)} %copy.122), calls=%async_computation.15 | async-start | bytes 1327104 | tf_op jit(solution)/shard_map/all_to_all | solution.py:57
  259.2 14.2 %all-to-all-start.13 = ((f32[1,72,18,72]{3,0,2,1:T(1,128)}), f32[1,72,18,72]{3,0,2,1:T(1,128)S(1)}, u32[]{:S(2)}, u32[]{:S(2)}) async-start(f32[1,72,18,72]{3,0,2,1:T(1,128)} %copy.117), calls=%async_computation.13 | async-start | bytes 1327104 | tf_op jit(solution)/shard_map/all_to_all | solution.py:57
  273.4 13.8 %all-to-all-start.11 = ((f32[1,72,18,72]{3,0,2,1:T(1,128)}), f32[1,72,18,72]{3,0,2,1:T(1,128)S(1)}, u32[]{:S(2)}, u32[]{:S(2)}) async-start(f32[1,72,18,72]{3,0,2,1:T(1,128)} %copy.112), calls=%async_computation.11 | async-start | bytes 1327104 | tf_op jit(solution)/shard_map/all_to_all | solution.py:57
  287.2 14.6 %all-to-all-start.9 = ((f32[1,72,18,72]{3,0,2,1:T(1,128)}), f32[1,72,18,72]{3,0,2,1:T(1,128)}, u32[]{:S(2)}, u32[]{:S(2)}) async-start(f32[1,72,18,72]{3,0,2,1:T(1,128)} %copy.107), calls=%async_computation.9 | async-start | bytes 1327104 | tf_op jit(solution)/shard_map/all_to_all | solution.py:57
  301.8 14.6 %all-to-all-start.7 = ((f32[1,72,18,72]{3,0,2,1:T(1,128)}), f32[1,72,18,72]{3,0,2,1:T(1,128)}, u32[]{:S(2)}, u32[]{:S(2)}) async-start(f32[1,72,18,72]{3,0,2,1:T(1,128)} %copy.102), calls=%async_computation.7 | async-start | bytes 1327104 | tf_op jit(solution)/shard_map/all_to_all | solution.py:57
  316.3 14.6 %all-to-all-start.5 = ((f32[1,72,18,72]{3,0,2,1:T(1,128)}), f32[1,72,18,72]{3,0,2,1:T(1,128)}, u32[]{:S(2)}, u32[]{:S(2)}) async-start(f32[1,72,18,72]{3,0,2,1:T(1,128)} %copy.97), calls=%async_computation.5 | async-start | bytes 1327104 | tf_op jit(solution)/shard_map/all_to_all | solution.py:57
  330.9 14.6 %all-to-all-start.3 = ((f32[1,72,18,72]{3,0,2,1:T(1,128)}), f32[1,72,18,72]{3,0,2,1:T(1,128)}, u32[]{:S(2)}, u32[]{:S(2)}) async-start(f32[1,72,18,72]{3,0,2,1:T(1,128)} %copy.92), calls=%async_computation.3 | async-start | bytes 1327104 | tf_op jit(solution)/shard_map/all_to_all | solution.py:57
  345.5 36.7 %all-to-all-start.17 = ((f32[1,72,18,72]{3,0,2,1:T(1,128)}), f32[1,72,18,72]{3,0,2,1:T(1,128)}, u32[]{:S(2)}, u32[]{:S(2)}) async-start(f32[1,72,18,72]{3,0,2,1:T(1,128)} %copy.127), calls=%async_computation.17 | async-start | bytes 1327104 | tf_op jit(solution)/shard_map/all_to_all | solution.py:57
  371.0 1.3 copy-start
  373.9 1.3 copy-start.1
  376.9 1.3 copy-start.2
where the time goes:
time: 421 us; the launch traced here: 415 us
  starting transfers between devices  118 us (28%)
  waiting for transfers between devices  115 us (27%)
  local copies, waits for them, and re-layouts  87.2 us (21%)
  matrix products  54.3 us (13%)
  other arithmetic  32.1 us (8%)
  blocking collectives  6.54 us (2%)
    all_to_all x9, waiting for transfers between devices, pencil_step(): lax.all_to_all(spectral, 'grid', split_axis=1, concat_axis=2, tiled=True)  44 us
    all_to_all x9, waiting for transfers between devices, poisson(): lax.all_to_all(slab, 'grid', split_axis=2, concat_axis=1, tiled=True)  43 us
    all_to_all x9, starting transfers between devices, pencil_step(): lax.all_to_all(spectral, 'grid', split_axis=1, concat_axis=2, tiled=True)  42.8 us
    all_to_all x9, starting transfers between devices, poisson(): lax.all_to_all(slab, 'grid', split_axis=2, concat_axis=1, tiled=True)  42.2 us
    ppermute x8, starting transfers between devices, shifted(): return lax.ppermute(value, axis, pairs)  32.7 us
    ppermute x8, waiting for transfers between devices, shifted(): return lax.ppermute(value, axis, pairs)  27.6 us
    another operation x18, local copies, waits for them, and re-layouts, pair_potential(): return poisson(densities).reshape(num_orbitals, source.shape[0], -1)  26.4 us
    dot_general x18, matrix products, poisson(): jnp.einsum('pxyz,ky->pxkz', slab, hartley, precision=HIGHEST_PRECISION)  20.6 us
  transfers between devices with their start and end apart: 26, of which 20 were waited for; matrix products, arithmetic and copies ran while one was open for 31% of the time, Pallas kernels for 0%

commit v1 on v0

v1 whole, which is shorter than its diff:
```python
import math

import jax
import jax.numpy as jnp
import numpy as np
from jax import lax
from jax.experimental import pallas as pl
from jax.experimental.pallas import tpu as pltpu
from jax.sharding import PartitionSpec as P

G = 72
LANES = 128
DEVICES = 4
STEPS = (0, 2, 3, 1)
PLANES = G // DEVICES
LINES = PLANES * G
ROWS = LINES * G // LANES
PAD_ROWS = 736
GROUPS = ROWS // 9
TILES = 11
PAIR_ROWS = 200
STEP = 24
SCREENING = 0.09
FRACTION = 0.25
CELLS = float(G * G * G)


def hartley_halves():
    indices = np.arange(G)
    phases = 2.0 * np.pi * (indices[:, None] * indices[None, :] % G) / G
    table = np.cos(phases) + np.sin(phases)
    high = table.astype(jnp.bfloat16)
    low = (table - high.astype(np.float64)).astype(jnp.bfloat16)
    return high, low


def line_weights():
    high, low = hartley_halves()
    weights = np.zeros((2 * LANES, 2 * LANES), jnp.bfloat16)
    weights[:G, :G] = high
    weights[:G, LANES : LANES + G] = low
    weights[LANES : LANES + G, :G] = high
    return weights


def column_weights():
    return np.concatenate(hartley_halves(), axis=0)


def spread(table):
    wide = np.zeros((G, DEVICES * STEP), jnp.bfloat16)
    for device in range(DEVICES):
        wide[:, device * STEP : device * STEP + PLANES] = table[:, device * PLANES : (device + 1) * PLANES]
    return wide


def in_order(table, device):
    blocks = np.split(table, DEVICES, axis=1)
    return np.concatenate([blocks[device ^ step] for step in STEPS], axis=1)


def forward_weights(device):
    return np.concatenate([spread(in_order(half, device)) for half in hartley_halves()], axis=0)


def backward_weights(device):
    return np.concatenate([spread(in_order(half, device)).T for half in hartley_halves()], axis=0)


def wavenumber(indices):
    return jnp.minimum(indices, G - indices).astype(jnp.float32) * (2.0 * math.pi / G)


def screened(device):
    lanes = jnp.arange(TILES * LANES, dtype=jnp.int32)
    first = wavenumber(jnp.arange(G, dtype=jnp.int32))
    second = wavenumber(jnp.minimum(device * PLANES + lanes // G, G - 1))
    third = wavenumber(lanes % G)
    squared = first[:, None] ** 2 + (second**2)[None, :] + (third**2)[None, :]
    scaled = squared / (4.0 * SCREENING * SCREENING)
    guarded = jnp.where(scaled > 0, scaled, 1.0)
    return jnp.where(scaled > 0, (1.0 - jnp.exp(-guarded)) / guarded, 1.0) / CELLS


def halves(value):
    high = value.astype(jnp.bfloat16)
    return high, (value - high.astype(jnp.float32)).astype(jnp.bfloat16)


def product(left, right):
    return jnp.dot(left, right, preferred_element_type=jnp.float32)


def along_lines(value, weights):
    result = product(jnp.concatenate(halves(value), axis=1), weights)
    return result[:, :LANES] + result[:, LANES:]


def along_columns(values, weights):
    rows = weights.shape[0] // 2
    high, low = halves(jnp.concatenate(values, axis=1) if len(values) > 1 else values[0])
    result = product(weights, high)
    result = result[:rows] + result[rows:] + product(weights[:rows], low)
    return [result[:, index * LANES : (index + 1) * LANES] for index in range(len(values))]


def unpack(lines, load, store, lane):
    tiles = {}

    def tile_at(tile):
        if tile not in tiles:
            tiles.pop(tile - 2, None)
            tiles[tile] = load(tile)
        return tiles[tile]

    for line in range(lines):
        tile, shift = divmod(line * G, LANES)
        value = tile_at(tile)
        if shift:
            value = pltpu.roll(value, LANES - shift, 1)
        if shift + G > LANES:
            tail = pltpu.roll(tile_at(tile + 1), LANES - shift, 1)
            value = jnp.where(lane < LANES - shift, value, tail)
        store(line, jnp.where(lane < G, value, 0.0))


def pack(lines, load, store, lane):
    filled = jnp.zeros(lane.shape, jnp.float32)
    for line in range(lines):
        tile, shift = divmod(line * G, LANES)
        value = load(line)
        if shift:
            value = pltpu.roll(value, shift, 1)
        if shift + G < LANES:
            filled = filled + value
            if line == lines - 1:
                store(tile, filled)
            continue
        store(tile, filled + jnp.where(lane >= shift, value, 0.0))
        filled = jnp.where(lane < shift, value, 0.0)
        if line == lines - 1 and shift + G > LANES:
            store(tile + 1, filled)


def lane_index(rows):
    return lax.broadcasted_iota(jnp.int32, (rows, LANES), 1)


def line_passes(work, weights, count):
    rows = 6 * G

    def some_lines(index, carry):
        block = pl.ds(pl.multiple_of(index * rows, 8), rows)
        work[block, :] = along_lines(work[block, :], weights[...])
        return carry

    lax.fori_loop(0, count * LINES // rows, some_lines, 0, unroll=True)


def column_passes(work, weights, count):
    def planes(index, carry):
        blocks = [pl.ds(pl.multiple_of((2 * index + half) * G, 8), G) for half in range(2)]
        values = along_columns([work[block, :] for block in blocks], weights[...])
        for block, value in zip(blocks, values):
            work[block, :] = value
        return carry

    lax.fori_loop(0, count * PLANES // 2, planes, 0, unroll=3)


def device_row(chunks, place, device, row):
    value = chunks[0][row : row + 1, :]
    for chunk, step in zip(chunks[1:], STEPS[1:]):
        value = jnp.where(place[1] ^ step == device, chunk[row : row + 1, :], value)
    return value


def orbital_at(refs, names, place, rows):
    def read(distance):
        if distance in names:
            return refs[names.index(distance)][rows, :]
        step = abs(distance)
        first = refs[names.index((step, 0))][rows, :]
        second = refs[names.index((step, 1))][rows, :]
        upward = place[0] == (0 if step == 1 else 1)
        return jnp.where(upward if distance > 0 else jnp.logical_not(upward), first, second)

    return read


def product_at(refs, names, place, pair, rows):
    first, second = pair
    if first == -second != 0:
        return refs[names.index((second, 0))][rows, :] * refs[names.index((second, 1))][rows, :]
    read = orbital_at(refs, names, place, rows)
    value = read(first)
    return value * (value if first == second else read(second))


def views(refs, place):
    if len(refs) > 1:
        return refs
    return [refs[0].at[place[1] ^ step] for step in STEPS]


def spread_kernel(pairs, names, place, *refs):
    orbitals, (lines, columns), outs = refs[: len(names)], refs[len(names) : len(names) + 2], refs[len(names) + 2 : -1]
    outs, work = views(outs, place), refs[-1]
    lane = lane_index(GROUPS)
    for index, pair in enumerate(pairs):

        def load(tile, pair=pair):
            return product_at(orbitals, names, place, pair, pl.ds(tile, GROUPS, stride=9))

        def store(line, value, index=index):
            work[pl.ds(index * LINES + line, GROUPS, stride=16), :] = value

        unpack(16, load, store, lane)
    line_passes(work, lines, len(pairs))
    column_passes(work, columns, len(pairs))
    lane = lane_index(PLANES)
    for index in range(len(pairs)):
        for out, step in zip(outs, STEPS):
            first = (place[1] ^ step) * PLANES + index * LINES

            def load(line, first=first):
                return work[pl.ds(first + line, PLANES, stride=G), :]

            def store(tile, value, start=index * PAIR_ROWS, out=out):
                out[start + tile * PLANES : start + (tile + 1) * PLANES, :] = value

            pack(PLANES, load, store, lane)
            start = index * PAIR_ROWS + TILES * PLANES
            out[start : start + 2, :] = jnp.zeros((2, LANES), jnp.float32)


def pencil_kernel(count, parts, place, *refs):
    chunks, (kernel, forward, backward), outs = refs[:parts], refs[parts : parts + 3], refs[parts + 3 :]
    chunks = views(chunks, place)
    forward, backward = forward.at[place[1]], backward.at[place[1]]
    lane = lane_index(G)
    gap = jnp.zeros((STEP - PLANES, LANES), jnp.float32)
    energies = [jnp.zeros((G, LANES), jnp.float32) for _ in range(count)]
    places = [(pair, tile) for tile in range(TILES) for pair in range(count)]
    for group in range(0, len(places), 2):
        now = places[group : group + 2]
        values = []
        for pair, tile in now:
            start = pair * PAIR_ROWS + tile * PLANES
            pieces = []
            for chunk in chunks:
                pieces += [chunk[start : start + PLANES, :], gap]
            values.append(jnp.concatenate(pieces, axis=0))
        solved = []
        for (pair, tile), spectral in zip(now, along_columns(values, forward[...])):
            solved.append(spectral * kernel[:, tile * LANES : (tile + 1) * LANES])
            if tile == TILES - 1:
                spectral = jnp.where(lane < PLANES * G - tile * LANES, spectral, 0.0)
            energies[pair] = energies[pair] + spectral * solved[-1]
        for (pair, tile), value in zip(now, along_columns(solved, backward[...])):
            start = pair * PAIR_ROWS + tile * PLANES
            for index, out in enumerate(outs):
                out[start : start + PLANES, :] = value[index * STEP : index * STEP + PLANES]
    for pair in range(count):
        total = jnp.full((2, LANES), jnp.sum(energies[pair]), jnp.float32)
        start = pair * PAIR_ROWS + TILES * PLANES
        for out in outs:
            out[start : start + 2, :] = total


def gather_kernel(count, parts, names, shares, place, *refs):
    chunks, (lines, columns), refs = views(refs[:parts], place), refs[parts : parts + 2], refs[parts + 2 :]
    orbitals = refs[: len(names)]
    outs, work = refs[-1 - len(shares) : -1], refs[-1]
    outs = dict(zip(shares, outs))
    added = dict(zip((2, -2), refs[len(names) : -1 - len(shares)]))
    upward = place[0] == 0
    lane = lane_index(PLANES)
    for pair in range(count):
        for chunk, step in zip(chunks, STEPS):
            first = pair * LINES + (place[1] ^ step) * PLANES

            def load(tile, start=pair * PAIR_ROWS, chunk=chunk):
                return chunk[start + tile * PLANES : start + (tile + 1) * PLANES, :]

            def store(line, value, first=first):
                work[pl.ds(first + line, PLANES, stride=G), :] = value

            unpack(PLANES, load, store, lane)
    column_passes(work, columns, count)
    line_passes(work, lines, count)
    lane = lane_index(GROUPS)

    def write(rows, terms, begun):
        shape = next(iter(terms.values())).shape
        for name in (1, 2):
            if name in terms or -name in terms:
                ahead = terms.get(name, jnp.zeros(shape, jnp.float32))
                behind = terms.get(-name, jnp.zeros(shape, jnp.float32))
                terms[name] = jnp.where(upward, ahead, behind)
                terms[-name] = jnp.where(upward, behind, ahead)
        for name, term in terms.items():
            if name in begun:
                term = term + outs[name][rows, :]
            elif name in added:
                term = term + added[name][rows, :]
            outs[name][rows, :] = term
        return set(terms)

    begun = set()
    for pair in range(count):

        def load(line, start=pair * LINES):
            return work[pl.ds(start + line, GROUPS, stride=16), :]

        written = set()

        def store(tile, value, pair=pair, written=written):
            rows = pl.ds(tile, GROUPS, stride=9)
            read = orbital_at(orbitals, names, place, rows)
            terms = {}
            for name, share in shares.items():
                for other, distance in share:
                    if other == pair:
                        terms[name] = value * read(distance)
            written |= write(rows, terms, begun)

        pack(16, load, store, lane)
        begun |= written
    totals = {}
    for name, share in shares.items():
        total = jnp.zeros((1, LANES), jnp.float32)
        for pair, _ in share:
            start = pair * PAIR_ROWS + TILES * PLANES
            for device in range(DEVICES):
                total = total + device_row(chunks, place, device, start)
        totals[name] = jnp.broadcast_to(total, (PAD_ROWS - ROWS, LANES))
    write(slice(ROWS, PAD_ROWS), totals, set())


def enter_kernel(cells, out):
    whole = ROWS // 8 * 8
    for row in range(0, whole, 8):
        out[row : row + 8, :] = cells[:, row * LANES : (row + 8) * LANES].reshape(8, LANES)
    out[whole:ROWS, :] = cells[:, whole * LANES :]
    out[ROWS:, :] = jnp.ones((PAD_ROWS - ROWS, LANES), jnp.float32)


def leave_kernel(own, *refs):
    parts, (residual, intersection) = refs[:-2], refs[-2:]

    def exchange(rows):
        return -FRACTION * sum(part[rows, :] for part in parts)

    mean = exchange(slice(ROWS, ROWS + 1)) * (1.0 / CELLS)
    intersection[...] = mean[:, :1]
    whole = ROWS // 8 * 8
    for row in range(0, whole, 8):
        rows = slice(row, row + 8)
        value = exchange(rows) - mean * own[rows, :]
        residual[:, row * LANES : (row + 8) * LANES] = value.reshape(1, 8 * LANES)
    rows = slice(whole, ROWS)
    residual[:, whole * LANES :] = exchange(rows) - mean * own[rows, :]


VMEM = pl.BlockSpec(memory_space=pltpu.VMEM)
SMEM = pl.BlockSpec(memory_space=pltpu.SMEM)
PARAMS = pltpu.CompilerParams(vmem_limit_bytes=8 * 1024 * 1024)


def chunks_of(count, parts):
    rows = count * PAIR_ROWS
    if parts == 1:
        return [jax.ShapeDtypeStruct((DEVICES, rows, LANES), jnp.float32)]
    return [jax.ShapeDtypeStruct((rows, LANES), jnp.float32)] * parts


def work_of(count):
    return [pltpu.VMEM((count * LINES, LANES), jnp.float32)]


def spread_pairs(orbitals, pairs, tables, parts=DEVICES):
    return pl.pallas_call(
        lambda *refs: spread_kernel(pairs, list(orbitals), *refs),
        out_shape=chunks_of(len(pairs), parts),
        in_specs=[SMEM] + [VMEM] * (len(orbitals) + 2),
        out_specs=[VMEM] * parts,
        scratch_shapes=work_of(len(pairs)),
        compiler_params=PARAMS,
        name="spread",
    )(tables["place"], *orbitals.values(), tables["lines"], tables["columns"])


def solve_pencils(chunks, count, tables):
    parts = len(chunks)
    return pl.pallas_call(
        lambda *refs: pencil_kernel(count, parts, *refs),
        out_shape=chunks_of(count, DEVICES),
        in_specs=[SMEM] + [VMEM] * (parts + 3),
        out_specs=[VMEM] * DEVICES,
        compiler_params=PARAMS,
        name="pencils",
    )(tables["place"], *chunks, tables["kernel"], tables["forward"], tables["backward"])


def gather_shares(chunks, count, orbitals, shares, tables, added=()):
    parts = len(chunks)
    return pl.pallas_call(
        lambda *refs: gather_kernel(count, parts, list(orbitals), shares, *refs),
        out_shape=[jax.ShapeDtypeStruct((PAD_ROWS, LANES), jnp.float32)] * len(shares),
        in_specs=[SMEM] + [VMEM] * (parts + 2 + len(orbitals) + len(added)),
        out_specs=[VMEM] * len(shares),
        scratch_shapes=work_of(count),
        compiler_params=PARAMS,
        name="gather",
    )(tables["place"], *chunks, tables["lines"], tables["columns"], *orbitals.values(), *added)


def enter(cells):
    return pl.pallas_call(
        enter_kernel,
        out_shape=jax.ShapeDtypeStruct((PAD_ROWS, LANES), jnp.float32),
        in_specs=[VMEM],
        out_specs=VMEM,
        compiler_params=PARAMS,
        name="enter",
    )(cells)


def leave(own, *parts):
    return pl.pallas_call(
        leave_kernel,
        out_shape=[jax.ShapeDtypeStruct((1, ROWS * LANES), jnp.float32), jax.ShapeDtypeStruct((1, 1), jnp.float32)],
        in_specs=[VMEM] * (1 + len(parts)),
        out_specs=[VMEM] * 2,
        compiler_params=PARAMS,
        name="leave",
    )(own, *parts)


def exchanged(chunks):
    if len(chunks) == 1:
        return [lax.all_to_all(chunks[0], "grid", split_axis=0, concat_axis=0)]
    received = [chunks[0]]
    for chunk, step in zip(chunks[1:], STEPS[1:]):
        pairs = [(device, device ^ step) for device in range(DEVICES)]
        received.append(lax.ppermute(chunk, "grid", pairs))
    return received


def after(values, *others):
    return lax.optimization_barrier((values, others))[0]


def swapped(value, step, phase):
    count = lax.axis_size("orb")
    pairs = []
    for source in range(count):
        upward = source // step % 2 == phase
        pairs.append((source, (source + (step if upward else -step)) % count))
    return lax.ppermute(value, "orb", pairs)


def shards(orbitals):
    device = lax.axis_index("grid")
    block = lax.axis_index("orb")
    tables = {
        "place": jnp.stack([block % 2, device]).astype(jnp.int32),
        "kernel": screened(device),
        "lines": jnp.asarray(line_weights()),
        "columns": jnp.asarray(column_weights()),
        "forward": jnp.asarray(np.stack([forward_weights(d) for d in range(DEVICES)])),
        "backward": jnp.asarray(np.stack([backward_weights(d) for d in range(DEVICES)])),
    }
    own = enter(orbitals)
    second = swapped(own, 1, 1)
    first = swapped(own, 1, 0)
    third = swapped(first, 1, 1)
    fourth = swapped(second, 1, 0)
    close = {0: own, (1, 0): first, (1, 1): second}
    near = spread_pairs(close, [(0, 1), (-1, 1)], tables)
    third, fourth = after((third, fourth), near)
    wide = {(1, 0): first, (1, 1): second, (2, 0): third, (2, 1): fourth}
    far = spread_pairs(wide, [(-1, 2), (-2, 2)], tables)
    none = spread_pairs({0: after(own, far)}, [(0, 0)], tables)
    near = solve_pencils(exchanged(near), 2, tables)
    far = solve_pencils(after(exchanged(far), near, none), 2, tables)
    near = exchanged(near)
    far = exchanged(far)
    shares = {1: [(0, 0), (1, -1)], -1: [(1, 1)], 0: [(0, 1)]}
    three, four, kept = gather_shares(near, 2, close, shares, tables)
    none = exchanged(after(none, kept))
    far = after(far, kept)
    shares = {1: [(0, -1), (1, -2)], -1: [(1, 2)], 2: [], -2: [(0, 2)]}
    one, two, three, four = gather_shares(far, 2, wide, shares, tables, [three, four])
    one = swapped(after(one, none), 1, 0)
    two = swapped(two, 1, 1)
    none = solve_pencils(none, 1, tables)
    four = swapped(one + four, 1, 1)
    three = swapped(two + after(three, none), 1, 0)
    none = exchanged(none)
    kept = kept + four
    (self_share,) = gather_shares(none, 1, {0: own}, {0: [(0, 0)]}, tables)
    residual, intersection = leave(own, self_share, kept, three)
    return residual, intersection.reshape(1, 1, 1)


def solution(mesh):
    in_specs = (P("orb", "grid"),)
    out_specs = (P("orb", "grid"), P("orb", None, None))
    return jax.shard_map(shards, mesh=mesh, in_specs=in_specs, out_specs=out_specs, check_vma=False)
```

time: 421 us -> 104 us (0.25); the launches traced: 415 us -> 104 us
  waiting for transfers between devices: 115 us -> 22.4 us
  local copies, waits for them, and re-layouts: 87.2 us -> 1.23 us
  starting transfers between devices: 118 us -> 53.9 us
  matrix products: 54.3 us -> 0 us
  other arithmetic: 32.1 us -> 0.48 us
  Pallas kernels: 0 us -> 25 us
  blocking collectives: 6.54 us -> 0 us
    all_to_all x18 -> x0, waiting for transfers between devices: 87 us -> none  [the longest x9 44 us: pencil_step(): lax.all_to_all(spectral, 'grid', split_axis=1, concat_axis=2, tiled=True)]
    all_to_all x18 -> x0, starting transfers between devices: 85 us -> none  [the longest x9 42.8 us: pencil_step(): lax.all_to_all(spectral, 'grid', split_axis=1, concat_axis=2, tiled=True)]
    dot_general x54 -> x0, matrix products: 54.3 us -> none  [the longest x18 20.6 us: poisson(): jnp.einsum('pxyz,ky->pxkz', slab, hartley, precision=HIGHEST_PRECISION)]
    another operation x36 -> x0, local copies, waits for them, and re-layouts: 34.4 us -> none  [the longest x18 26.4 us: pair_potential(): return poisson(densities).reshape(num_orbitals, source.shape[0], -1)]
    mul x2 -> x0, other arithmetic: 28.5 us -> none  [the longest x1 14.9 us: shards(): exchange = -FRACTION * exchange]
    transpose x18 -> x0, local copies, waits for them, and re-layouts: 27.7 us -> none  [the longest x9 13.9 us: pencil_step(): jnp.einsum('pxyz,kx->pkyz', spectral, hartley, precision=HIGHEST_PRECISION)]
    pallas_call x0 -> x11, Pallas kernels: none -> 25 us  [the longest x3 9.61 us: gather_shares(): pl.pallas_call(lambda *refs: gather_kernel(count, parts, list(orbitals),...]
    ppermute x8 -> x26, starting transfers between devices: 32.7 us -> 53.9 us  [the longest x8 35.3 us: swapped(): return lax.ppermute(value, 'orb', pairs)]
  transfers between devices with their start and end apart: 26 -> 26, of which waited for: 20 -> 9; matrix products, arithmetic and copies ran while one was open for 31% -> 0% of each run, Pallas kernels for 0% -> 23%
where the time goes in v1:
time: 104 us
  starting transfers between devices  53.9 us (52%)
  Pallas kernels  25 us (24%)
  waiting for transfers between devices  22.4 us (22%)
  local copies, waits for them, and re-layouts  1.23 us (1%)
    ppermute x8, starting transfers between devices, swapped(): return lax.ppermute(value, 'orb', pairs)  35.3 us
    ppermute x18, waiting for transfers between devices, exchanged(): received.append(lax.ppermute(chunk, 'grid', pairs))  19.6 us
    ppermute x18, starting transfers between devices, exchanged(): received.append(lax.ppermute(chunk, 'grid', pairs))  18.6 us
    pallas_call x3, Pallas kernels, gather_shares(): pl.pallas_call(lambda *refs: gather_kernel(count, parts, list(orbitals),...  9.61 us
    pallas_call x3, Pallas kernels, spread_pairs(): pl.pallas_call(lambda *refs: spread_kernel(pairs, list(orbitals), *refs),...  8.67 us
    pallas_call x3, Pallas kernels, solve_pencils(): pl.pallas_call(lambda *refs: pencil_kernel(count, parts, *refs), out_shap...  5.87 us
    ppermute x8, waiting for transfers between devices, swapped(): return lax.ppermute(value, 'orb', pairs)  2.79 us
  transfers between devices with their start and end apart: 26, of which 9 were waited for; matrix products, arithmetic and copies ran while one was open for 0% of the time, Pallas kernels for 23%

profile of v1, /device:TPU:1, one launch (start us, length us, event | category | flops | bytes accessed | tf_op | source)
XLA Modules:
  0.0 103.8 jit_solution(4390926192018984662)
XLA Ops:
  0.6 1.0 copy-done.4
  1.7 2.6 %collective-permute-start = (f32[736,128]{1,0:T(8,128)S(1)}, f32[736,128]{1,0:T(8,128)S(1)}, u32[]{:S(2)}, u32[]{:S(2)}) collective-permute-start(f32[736,128]{1,0:T(8,128)S(1)} %enter.1.refs_1_.refs_7_.own), channel_id=1, source_target_pairs={{0,4},{4,0},{8,12},{12,8},{16,20},{20,16},{24,28},{28,24},{32,36},... | collective-permute-start | bytes 1130504 | tf_op jit(solution)/shard_map/ppermute | solution.py:461
  4.2 9.5 %collective-permute-start.1 = (f32[736,128]{1,0:T(8,128)S(1)}, f32[736,128]{1,0:T(8,128)S(1)}, u32[]{:S(2)}, u32[]{:S(2)}) collective-permute-start(f32[736,128]{1,0:T(8,128)S(1)} %enter.1.refs_1_.refs_7_.own), channel_id=1, source_target_pairs={{0,252},{4,8},{8,4},{12,16},{16,12},{20,24},{24,20},{28,32},{32,28... | collective-permute-start | bytes 1130504 | tf_op jit(solution)/shard_map/ppermute | solution.py:461
  13.7 8.9 %collective-permute-start.2 = (f32[736,128]{1,0:T(8,128)S(1)}, f32[736,128]{1,0:T(8,128)S(1)}, u32[]{:S(2)}, u32[]{:S(2)}) collective-permute-start(f32[736,128]{1,0:T(8,128)S(1)} %collective-permute-done.refs_2_.refs_1_.refs_8_.refs_7_), channel_id=1, source_target_pairs={{0,252},{4,8},{8,4},{12,16},{16,12},{20,24},{24,20},{28,32},{32,28... | collective-permute-start | bytes 1130504 | tf_op jit(solution)/shard_map/ppermute | solution.py:461
  22.6 0.1 pad_add_fusion.refs_0_
  22.7 3.3 %spread.3 = (f32[400,128]{1,0:T(8,128)S(1)}, f32[400,128]{1,0:T(8,128)S(1)}, f32[400,128]{1,0:T(8,128)S(1)}, f32[400,128]{1,0:T(8,128)S(1)}) custom-call(s32[2]{0:T(128)S(1)} %pad_add_fusion.refs_0_, f32[736,128]{1,0:T(8,128)S(1)} %enter.1.refs_1_.refs_7_.own, f32[736,128]{1,0:T(8,128)S(1)} %collective-permute-done.refs_2_.refs_1_.refs_8_.refs_7_, ...), custom_call_target="tpu_custom_call" | custom-call | tf_op jit(solution)/shard_map/spread/pallas_call | solution.py:383
  26.0 0.5 collective-permute-start.4
  26.5 3.1 %collective-permute-start.5 = (f32[400,128]{1,0:T(8,128)S(1)}, f32[400,128]{1,0:T(8,128)S(1)}, u32[]{:S(2)}, u32[]{:S(2)}) collective-permute-start(f32[400,128]{1,0:T(8,128)S(1)} %get-tuple-element.54), channel_id=1, source_target_pairs={{0,3},{1,2},{2,1},{3,0},{4,7},{5,6},{6,5},{7,4},{8,11},{9,10},{10,... | collective-permute-start | bytes 614408 | tf_op jit(solution)/shard_map/ppermute | solution.py:447
  29.7 0.5 collective-permute-done.2.refs_3_.refs_9_
  30.1 0.9 collective-permute-done.3.refs_4_.refs_10_
  31.0 3.3 %spread.4 = (f32[400,128]{1,0:T(8,128)S(1)}, f32[400,128]{1,0:T(8,128)S(1)}, f32[400,128]{1,0:T(8,128)S(1)}, f32[400,128]{1,0:T(8,128)S(1)}) custom-call(s32[2]{0:T(128)S(1)} %pad_add_fusion.refs_0_, f32[736,128]{1,0:T(8,128)S(1)} %collective-permute-done.refs_2_.refs_1_.refs_8_.refs_7_, ...), custom_call_target="tpu_custom_call" | custom-call | tf_op jit(solution)/shard_map/spread/pallas_call | solution.py:383
  34.4 0.5 collective-permute-start.16
  34.9 4.0 %collective-permute-start.17 = (f32[400,128]{1,0:T(8,128)S(1)}, f32[400,128]{1,0:T(8,128)S(1)}, u32[]{:S(2)}, u32[]{:S(2)}) collective-permute-start(f32[400,128]{1,0:T(8,128)S(1)} %get-tuple-element.60), channel_id=1, source_target_pairs={{0,3},{1,2},{2,1},{3,0},{4,7},{5,6},{6,5},{7,4},{8,11},{9,10},{10,... | collective-permute-start | bytes 614408 | tf_op jit(solution)/shard_map/ppermute | solution.py:447
  38.9 0.2 fusion.refs_5_
  39.1 0.5 collective-permute-done.5.refs_3_
  39.6 0.1 copy-done.1
  39.8 0.1 copy-done.2
  39.9 2.2 %pencils.3 = (f32[400,128]{1,0:T(8,128)S(1)}, f32[400,128]{1,0:T(8,128)S(1)}, f32[400,128]{1,0:T(8,128)S(1)}, f32[400,128]{1,0:T(8,128)S(1)}) custom-call(s32[2]{0:T(128)S(1)} %pad_add_fusion.refs_0_, f32[400,128]{1,0:T(8,128)S(1)} %get-tuple-element.52.refs_1_, f32[400,128]{1,0:T(8,128)S(1)} %collective-permute-done.4.refs_2_, ...), custom_call_target="tpu_custom_call" | custom-call | tf_op jit(solution)/shard_map/pencils/pallas_call | solution.py:396
  42.1 0.5 collective-permute-start.7
  42.6 1.7 %collective-permute-start.8 = (f32[400,128]{1,0:T(8,128)S(1)}, f32[400,128]{1,0:T(8,128)S(1)}, u32[]{:S(2)}, u32[]{:S(2)}) collective-permute-start(f32[400,128]{1,0:T(8,128)S(1)} %get-tuple-element.69), channel_id=1, source_target_pairs={{0,3},{1,2},{2,1},{3,0},{4,7},{5,6},{6,5},{7,4},{8,11},{9,10},{10,... | collective-permute-start | bytes 614408 | tf_op jit(solution)/shard_map/ppermute | solution.py:447
  44.3 2.0 %spread.5 = (f32[200,128]{1,0:T(8,128)S(1)}, f32[200,128]{1,0:T(8,128)S(1)}, f32[200,128]{1,0:T(8,128)S(1)}, f32[200,128]{1,0:T(8,128)S(1)}) custom-call(s32[2]{0:T(128)S(1)} %pad_add_fusion.refs_0_, f32[736,128]{1,0:T(8,128)S(1)} %enter.1.refs_1_.refs_7_.own, bf16[256,256]{1,0:T(8,128)(2,1)S(1)} %copy-done, bf16[144,72]{1,0:T(8,128)(2,1)S(1)} %copy-done.3), custom_call_target="tpu_custom_call" | custom-call | tf_op jit(solution)/shard_map/spread/pallas_call | solution.py:383
  46.3 0.3 collective-permute-start.9
  46.6 2.3 %collective-permute-done.17.refs_3_ = f32[400,128]{1,0:T(8,128)S(1)} collective-permute-done((f32[400,128]{1,0:T(8,128)S(1)}, f32[400,128]{1,0:T(8,128)S(1)}, u32[]{:S(2)}, u32[]{:S(2)}) %collective-permute-start.17) | collective-permute-done | bytes 204832 | tf_op jit(solution)/shard_map/ppermute | solution.py:447
  48.9 2.2 %pencils.5 = (f32[400,128]{1,0:T(8,128)S(1)}, f32[400,128]{1,0:T(8,128)S(1)}, f32[400,128]{1,0:T(8,128)S(1)}, f32[400,128]{1,0:T(8,128)S(1)}) custom-call(s32[2]{0:T(128)S(1)} %pad_add_fusion.refs_0_, f32[400,128]{1,0:T(8,128)S(1)} %get-tuple-element.80.refs_1_, f32[400,128]{1,0:T(8,128)S(1)} %collective-permute-done.16.refs_2_, ...), custom_call_target="tpu_custom_call" | custom-call | tf_op jit(solution)/shard_map/pencils/pallas_call | solution.py:396
  51.2 0.5 collective-permute-start.19
  51.6 0.1 collective-permute-start.20
  51.8 2.3 %collective-permute-start.21 = (f32[400,128]{1,0:T(8,128)S(1)}, f32[400,128]{1,0:T(8,128)S(1)}, u32[]{:S(2)}, u32[]{:S(2)}) collective-permute-start(f32[400,128]{1,0:T(8,128)S(1)} %get-tuple-element.87), channel_id=1, source_target_pairs={{0,1},{1,0},{2,3},{3,2},{4,5},{5,4},{6,7},{7,6},{8,9},{9,8},{10,11... | collective-permute-start | bytes 614408 | tf_op jit(solution)/shard_map/ppermute | solution.py:447
  54.0 3.7 %collective-permute-done.8.refs_3_ = f32[400,128]{1,0:T(8,128)S(1)} collective-permute-done((f32[400,128]{1,0:T(8,128)S(1)}, f32[400,128]{1,0:T(8,128)S(1)}, u32[]{:S(2)}, u32[]{:S(2)}) %collective-permute-start.8) | collective-permute-done | bytes 204832 | tf_op jit(solution)/shard_map/ppermute | solution.py:447
  57.7 3.6 %gather.3 = (f32[736,128]{1,0:T(8,128)S(1)}, f32[736,128]{1,0:T(8,128)S(1)}, f32[736,128]{1,0:T(8,128)S(1)}) custom-call(s32[2]{0:T(128)S(1)} %pad_add_fusion.refs_0_, f32[400,128]{1,0:T(8,128)S(1)} %get-tuple-element.67.refs_1_, f32[400,128]{1,0:T(8,128)S(1)} %collective-permute-done.7.refs_2_, f32[400,128]{1,0:T(8,128)S(1)} %collective-permute-done.8.refs_3_, ...), custom_call_target="tpu_custom_call" | custom-call | tf_op jit(solution)/shard_map/gather/pallas_call | solution.py:408
  61.4 0.5 collective-permute-start.10
  61.9 0.1 collective-permute-start.11
  62.0 1.3 %collective-permute-start.12 = (f32[200,128]{1,0:T(8,128)S(1)}, f32[200,128]{1,0:T(8,128)S(1)}, u32[]{:S(2)}, u32[]{:S(2)}) collective-permute-start(f32[200,128]{1,0:T(8,128)S(1)} %get-tuple-element.75), channel_id=1, source_target_pairs={{0,1},{1,0},{2,3},{3,2},{4,5},{5,4},{6,7},{7,6},{8,9},{9,8},{10,11... | collective-permute-start | bytes 307208 | tf_op jit(solution)/shard_map/ppermute | solution.py:447
  63.3 3.3 %collective-permute-done.20.refs_3_ = f32[400,128]{1,0:T(8,128)S(1)} collective-permute-done((f32[400,128]{1,0:T(8,128)S(1)}, f32[400,128]{1,0:T(8,128)S(1)}, u32[]{:S(2)}, u32[]{:S(2)}) %collective-permute-start.20) | collective-permute-done | bytes 204832 | tf_op jit(solution)/shard_map/ppermute | solution.py:447
  66.6 3.8 %gather.5 = (f32[736,128]{1,0:T(8,128)S(1)}, f32[736,128]{1,0:T(8,128)S(1)}, f32[736,128]{1,0:T(8,128)S(1)}, f32[736,128]{1,0:T(8,128)S(1)}) custom-call(s32[2]{0:T(128)S(1)} %pad_add_fusion.refs_0_, f32[400,128]{1,0:T(8,128)S(1)} %get-tuple-element.88.refs_1_, f32[400,128]{1,0:T(8,128)S(1)} %collective-permute-done.19.refs_2_, ...), custom_call_target="tpu_custom_call" | custom-call | tf_op jit(solution)/shard_map/gather/pallas_call | solution.py:408
  70.5 0.1 collective-permute-start.22
  70.6 6.9 %collective-permute-start.24 = (f32[736,128]{1,0:T(8,128)S(1)}, f32[736,128]{1,0:T(8,128)S(1)}, u32[]{:S(2)}, u32[]{:S(2)}) collective-permute-start(f32[736,128]{1,0:T(8,128)S(1)} %get-tuple-element.97), channel_id=1, source_target_pairs={{0,252},{4,8},{8,4},{12,16},{16,12},{20,24},{24,20},{28,32},{32,28... | collective-permute-start | bytes 1130504 | tf_op jit(solution)/shard_map/ppermute | solution.py:461
  77.5 1.4 %pencils.4 = (f32[200,128]{1,0:T(8,128)S(1)}, f32[200,128]{1,0:T(8,128)S(1)}, f32[200,128]{1,0:T(8,128)S(1)}, f32[200,128]{1,0:T(8,128)S(1)}) custom-call(s32[2]{0:T(128)S(1)} %pad_add_fusion.refs_0_, f32[200,128]{1,0:T(8,128)S(1)} %get-tuple-element.72.refs_1_, f32[200,128]{1,0:T(8,128)S(1)} %collective-permute-done.10.refs_2_, ...), custom_call_target="tpu_custom_call" | custom-call | tf_op jit(solution)/shard_map/pencils/pallas_call | solution.py:396
  79.0 1.4 %collective-permute-done.22 = f32[736,128]{1,0:T(8,128)S(1)} collective-permute-done((f32[736,128]{1,0:T(8,128)S(1)}, f32[736,128]{1,0:T(8,128)S(1)}, u32[]{:S(2)}, u32[]{:S(2)}) %collective-permute-start.22) | collective-permute-done | bytes 376864 | tf_op jit(solution)/shard_map/ppermute | solution.py:461
  80.4 7.2 %collective-permute-start.23 = (f32[736,128]{1,0:T(8,128)S(1)}, f32[736,128]{1,0:T(8,128)S(1)}, u32[]{:S(2)}, u32[]{:S(2)}) collective-permute-start(f32[736,128]{1,0:T(8,128)S(1)} %add.68), channel_id=1, source_target_pairs={{0,252},{4,8},{8,4},{12,16},{16,12},{20,24},{24,20},{28,32},{32,28... | collective-permute-start | bytes 1130504 | tf_op jit(solution)/shard_map/ppermute | solution.py:461
  87.6 0.1 add.70
  87.7 0.1 collective-permute-start.25
  87.8 0.5 collective-permute-start.13
  88.3 2.7 %collective-permute-start.14 = (f32[200,128]{1,0:T(8,128)S(1)}, f32[200,128]{1,0:T(8,128)S(1)}, u32[]{:S(2)}, u32[]{:S(2)}) collective-permute-start(f32[200,128]{1,0:T(8,128)S(1)} %get-tuple-element.78), channel_id=1, source_target_pairs={{0,3},{1,2},{2,1},{3,0},{4,7},{5,6},{6,5},{7,4},{8,11},{9,10},{10,... | collective-permute-start | bytes 307208 | tf_op jit(solution)/shard_map/ppermute | solution.py:447
  91.0 7.5 %collective-permute-done.13.refs_2_ = f32[200,128]{1,0:T(8,128)S(1)} collective-permute-done((f32[200,128]{1,0:T(8,128)S(1)}, f32[200,128]{1,0:T(8,128)S(1)}, u32[]{:S(2)}, u32[]{:S(2)}) %collective-permute-start.13) | collective-permute-done | bytes 102432 | tf_op jit(solution)/shard_map/ppermute | solution.py:447
  98.5 2.2 %collective-permute-done.14.refs_3_ = f32[200,128]{1,0:T(8,128)S(1)} collective-permute-done((f32[200,128]{1,0:T(8,128)S(1)}, f32[200,128]{1,0:T(8,128)S(1)}, u32[]{:S(2)}, u32[]{:S(2)}) %collective-permute-start.14) | collective-permute-done | bytes 102432 | tf_op jit(solution)/shard_map/ppermute | solution.py:447
  100.7 2.2 %gather.4.refs_0_ = f32[736,128]{1,0:T(8,128)S(1)} custom-call(s32[2]{0:T(128)S(1)} %pad_add_fusion.refs_0_, f32[200,128]{1,0:T(8,128)S(1)} %get-tuple-element.76.refs_1_, f32[200,128]{1,0:T(8,128)S(1)} %collective-permute-done.13.refs_2_, f32[200,128]{1,0:T(8,128)S(1)} %collective-permute-done.14.refs_3_, f32[200,128]{1,0:T(8,128)S(1)} %collective-permute-done.15.refs_4_, ...), custom_call_target="tpu_custom_call" | custom-call | tf_op jit(solution)/shard_map/gather/pallas_call | solution.py:408
  102.9 0.1 add.69.refs_1_
  103.0 0.8 leave.1
  (32 shorter events, 0.2 us)
Async XLA Ops:
  0.6 1.0 copy-start.4
  1.6 21.1 %copy-start = (bf16[256,256]{1,0:T(8,128)(2,1)S(1)}, bf16[256,256]{1,0:T(8,128)(2,1)}, u32[]{:S(2)}) copy-start(bf16[256,256]{1,0:T(8,128)(2,1)} %constant.68.clone.refs_4_.refs_5_.refs_2_) | copy-start | bytes 393220
  1.6 21.0 %copy-start.3 = (bf16[144,72]{1,0:T(8,128)(2,1)S(1)}, bf16[144,72]{1,0:T(8,128)(2,1)}, u32[]{:S(2)}) copy-start(bf16[144,72]{1,0:T(8,128)(2,1)} %constant.69.clone.refs_5_.refs_6_.refs_3_) | copy-start | bytes 62212
  1.7 12.0 %collective-permute-start = (f32[736,128]{1,0:T(8,128)S(1)}, f32[736,128]{1,0:T(8,128)S(1)}, u32[]{:S(2)}, u32[]{:S(2)}) collective-permute-start(f32[736,128]{1,0:T(8,128)S(1)} %enter.1.refs_1_.refs_7_.own), channel_id=1, source_target_pairs={{0,4},{4,0},{8,12},{12,8},{16,20},{20,16},{24,28},{28,24},{32,36},... | collective-permute-start | bytes 1130504 | tf_op jit(solution)/shard_map/ppermute | solution.py:461
  4.2 18.4 %collective-permute-start.1 = (f32[736,128]{1,0:T(8,128)S(1)}, f32[736,128]{1,0:T(8,128)S(1)}, u32[]{:S(2)}, u32[]{:S(2)}) collective-permute-start(f32[736,128]{1,0:T(8,128)S(1)} %enter.1.refs_1_.refs_7_.own), channel_id=1, source_target_pairs={{0,252},{4,8},{8,4},{12,16},{16,12},{20,24},{24,20},{28,32},{32,28... | collective-permute-start | bytes 1130504 | tf_op jit(solution)/shard_map/ppermute | solution.py:461
  13.7 16.4 %collective-permute-start.2 = (f32[736,128]{1,0:T(8,128)S(1)}, f32[736,128]{1,0:T(8,128)S(1)}, u32[]{:S(2)}, u32[]{:S(2)}) collective-permute-start(f32[736,128]{1,0:T(8,128)S(1)} %collective-permute-done.refs_2_.refs_1_.refs_8_.refs_7_), channel_id=1, source_target_pairs={{0,252},{4,8},{8,4},{12,16},{16,12},{20,24},{24,20},{28,32},{32,28... | collective-permute-start | bytes 1130504 | tf_op jit(solution)/shard_map/ppermute | solution.py:461
  22.6 8.4 %collective-permute-start.3 = (f32[736,128]{1,0:T(8,128)S(1)}, f32[736,128]{1,0:T(8,128)S(1)}, u32[]{:S(2)}, u32[]{:S(2)}) collective-permute-start(f32[736,128]{1,0:T(8,128)S(1)} %collective-permute-done.1.refs_3_.refs_2_.refs_9_.refs_8_), channel_id=1, source_target_pairs={{0,4},{4,0},{8,12},{12,8},{16,20},{20,16},{24,28},{28,24},{32,36},... | collective-permute-start | bytes 1130504 | tf_op jit(solution)/shard_map/ppermute | solution.py:461
  26.0 12.8 %collective-permute-start.4 = (f32[400,128]{1,0:T(8,128)S(1)}, f32[400,128]{1,0:T(8,128)S(1)}, u32[]{:S(2)}, u32[]{:S(2)}) collective-permute-start(f32[400,128]{1,0:T(8,128)S(1)} %get-tuple-element.53), channel_id=1, source_target_pairs={{0,2},{1,3},{2,0},{3,1},{4,6},{5,7},{6,4},{7,5},{8,10},{9,11},{10,... | collective-permute-start | bytes 614408 | tf_op jit(solution)/shard_map/ppermute | solution.py:447
  26.5 13.1 %collective-permute-start.5 = (f32[400,128]{1,0:T(8,128)S(1)}, f32[400,128]{1,0:T(8,128)S(1)}, u32[]{:S(2)}, u32[]{:S(2)}) collective-permute-start(f32[400,128]{1,0:T(8,128)S(1)} %get-tuple-element.54), channel_id=1, source_target_pairs={{0,3},{1,2},{2,1},{3,0},{4,7},{5,6},{6,5},{7,4},{8,11},{9,10},{10,... | collective-permute-start | bytes 614408 | tf_op jit(solution)/shard_map/ppermute | solution.py:447
  29.7 10.0 %collective-permute-start.6 = (f32[400,128]{1,0:T(8,128)S(1)}, f32[400,128]{1,0:T(8,128)S(1)}, u32[]{:S(2)}, u32[]{:S(2)}) collective-permute-start(f32[400,128]{1,0:T(8,128)S(1)} %get-tuple-element.55), channel_id=1, source_target_pairs={{0,1},{1,0},{2,3},{3,2},{4,5},{5,4},{6,7},{7,6},{8,9},{9,8},{10,11... | collective-permute-start | bytes 614408 | tf_op jit(solution)/shard_map/ppermute | solution.py:447
  34.4 12.0 %collective-permute-start.16 = (f32[400,128]{1,0:T(8,128)S(1)}, f32[400,128]{1,0:T(8,128)S(1)}, u32[]{:S(2)}, u32[]{:S(2)}) collective-permute-start(f32[400,128]{1,0:T(8,128)S(1)} %get-tuple-element.59), channel_id=1, source_target_pairs={{0,2},{1,3},{2,0},{3,1},{4,6},{5,7},{6,4},{7,5},{8,10},{9,11},{10,... | collective-permute-start | bytes 614408 | tf_op jit(solution)/shard_map/ppermute | solution.py:447
  34.9 14.1 %collective-permute-start.17 = (f32[400,128]{1,0:T(8,128)S(1)}, f32[400,128]{1,0:T(8,128)S(1)}, u32[]{:S(2)}, u32[]{:S(2)}) collective-permute-start(f32[400,128]{1,0:T(8,128)S(1)} %get-tuple-element.60), channel_id=1, source_target_pairs={{0,3},{1,2},{2,1},{3,0},{4,7},{5,6},{6,5},{7,4},{8,11},{9,10},{10,... | collective-permute-start | bytes 614408 | tf_op jit(solution)/shard_map/ppermute | solution.py:447
  38.9 10.1 %collective-permute-start.18 = (f32[400,128]{1,0:T(8,128)S(1)}, f32[400,128]{1,0:T(8,128)S(1)}, u32[]{:S(2)}, u32[]{:S(2)}) collective-permute-start(f32[400,128]{1,0:T(8,128)S(1)} %get-tuple-element.61), channel_id=1, source_target_pairs={{0,1},{1,0},{2,3},{3,2},{4,5},{5,4},{6,7},{7,6},{8,9},{9,8},{10,11... | collective-permute-start | bytes 614408 | tf_op jit(solution)/shard_map/ppermute | solution.py:447
  38.9 0.9 copy-start.1
  38.9 1.0 copy-start.2
  42.1 9.7 %collective-permute-start.7 = (f32[400,128]{1,0:T(8,128)S(1)}, f32[400,128]{1,0:T(8,128)S(1)}, u32[]{:S(2)}, u32[]{:S(2)}) collective-permute-start(f32[400,128]{1,0:T(8,128)S(1)} %get-tuple-element.68), channel_id=1, source_target_pairs={{0,2},{1,3},{2,0},{3,1},{4,6},{5,7},{6,4},{7,5},{8,10},{9,11},{10,... | collective-permute-start | bytes 614408 | tf_op jit(solution)/shard_map/ppermute | solution.py:447
  42.6 15.2 %collective-permute-start.8 = (f32[400,128]{1,0:T(8,128)S(1)}, f32[400,128]{1,0:T(8,128)S(1)}, u32[]{:S(2)}, u32[]{:S(2)}) collective-permute-start(f32[400,128]{1,0:T(8,128)S(1)} %get-tuple-element.69), channel_id=1, source_target_pairs={{0,3},{1,2},{2,1},{3,0},{4,7},{5,6},{6,5},{7,4},{8,11},{9,10},{10,... | collective-permute-start | bytes 614408 | tf_op jit(solution)/shard_map/ppermute | solution.py:447
  46.3 11.4 %collective-permute-start.9 = (f32[400,128]{1,0:T(8,128)S(1)}, f32[400,128]{1,0:T(8,128)S(1)}, u32[]{:S(2)}, u32[]{:S(2)}) collective-permute-start(f32[400,128]{1,0:T(8,128)S(1)} %get-tuple-element.70), channel_id=1, source_target_pairs={{0,1},{1,0},{2,3},{3,2},{4,5},{5,4},{6,7},{7,6},{8,9},{9,8},{10,11... | collective-permute-start | bytes 614408 | tf_op jit(solution)/shard_map/ppermute | solution.py:447
  51.2 10.8 %collective-permute-start.19 = (f32[400,128]{1,0:T(8,128)S(1)}, f32[400,128]{1,0:T(8,128)S(1)}, u32[]{:S(2)}, u32[]{:S(2)}) collective-permute-start(f32[400,128]{1,0:T(8,128)S(1)} %get-tuple-element.85), channel_id=1, source_target_pairs={{0,2},{1,3},{2,0},{3,1},{4,6},{5,7},{6,4},{7,5},{8,10},{9,11},{10,... | collective-permute-start | bytes 614408 | tf_op jit(solution)/shard_map/ppermute | solution.py:447
  51.6 15.0 %collective-permute-start.20 = (f32[400,128]{1,0:T(8,128)S(1)}, f32[400,128]{1,0:T(8,128)S(1)}, u32[]{:S(2)}, u32[]{:S(2)}) collective-permute-start(f32[400,128]{1,0:T(8,128)S(1)} %get-tuple-element.86), channel_id=1, source_target_pairs={{0,3},{1,2},{2,1},{3,0},{4,7},{5,6},{6,5},{7,4},{8,11},{9,10},{10,... | collective-permute-start | bytes 614408 | tf_op jit(solution)/shard_map/ppermute | solution.py:447
  51.8 14.9 %collective-permute-start.21 = (f32[400,128]{1,0:T(8,128)S(1)}, f32[400,128]{1,0:T(8,128)S(1)}, u32[]{:S(2)}, u32[]{:S(2)}) collective-permute-start(f32[400,128]{1,0:T(8,128)S(1)} %get-tuple-element.87), channel_id=1, source_target_pairs={{0,1},{1,0},{2,3},{3,2},{4,5},{5,4},{6,7},{7,6},{8,9},{9,8},{10,11... | collective-permute-start | bytes 614408 | tf_op jit(solution)/shard_map/ppermute | solution.py:447
  61.4 9.1 %collective-permute-start.10 = (f32[200,128]{1,0:T(8,128)S(1)}, f32[200,128]{1,0:T(8,128)S(1)}, u32[]{:S(2)}, u32[]{:S(2)}) collective-permute-start(f32[200,128]{1,0:T(8,128)S(1)} %get-tuple-element.73), channel_id=1, source_target_pairs={{0,2},{1,3},{2,0},{3,1},{4,6},{5,7},{6,4},{7,5},{8,10},{9,11},{10,... | collective-permute-start | bytes 307208 | tf_op jit(solution)/shard_map/ppermute | solution.py:447
  61.9 8.6 %collective-permute-start.11 = (f32[200,128]{1,0:T(8,128)S(1)}, f32[200,128]{1,0:T(8,128)S(1)}, u32[]{:S(2)}, u32[]{:S(2)}) collective-permute-start(f32[200,128]{1,0:T(8,128)S(1)} %get-tuple-element.74), channel_id=1, source_target_pairs={{0,3},{1,2},{2,1},{3,0},{4,7},{5,6},{6,5},{7,4},{8,11},{9,10},{10,... | collective-permute-start | bytes 307208 | tf_op jit(solution)/shard_map/ppermute | solution.py:447
  62.0 8.5 %collective-permute-start.12 = (f32[200,128]{1,0:T(8,128)S(1)}, f32[200,128]{1,0:T(8,128)S(1)}, u32[]{:S(2)}, u32[]{:S(2)}) collective-permute-start(f32[200,128]{1,0:T(8,128)S(1)} %get-tuple-element.75), channel_id=1, source_target_pairs={{0,1},{1,0},{2,3},{3,2},{4,5},{5,4},{6,7},{7,6},{8,9},{9,8},{10,11... | collective-permute-start | bytes 307208 | tf_op jit(solution)/shard_map/ppermute | solution.py:447
  70.5 9.9 %collective-permute-start.22 = (f32[736,128]{1,0:T(8,128)S(1)}, f32[736,128]{1,0:T(8,128)S(1)}, u32[]{:S(2)}, u32[]{:S(2)}) collective-permute-start(f32[736,128]{1,0:T(8,128)S(1)} %get-tuple-element.95), channel_id=1, source_target_pairs={{0,4},{4,0},{8,12},{12,8},{16,20},{20,16},{24,28},{28,24},{32,36},... | collective-permute-start | bytes 1130504 | tf_op jit(solution)/shard_map/ppermute | solution.py:461
  70.6 17.0 %collective-permute-start.24 = (f32[736,128]{1,0:T(8,128)S(1)}, f32[736,128]{1,0:T(8,128)S(1)}, u32[]{:S(2)}, u32[]{:S(2)}) collective-permute-start(f32[736,128]{1,0:T(8,128)S(1)} %get-tuple-element.97), channel_id=1, source_target_pairs={{0,252},{4,8},{8,4},{12,16},{16,12},{20,24},{24,20},{28,32},{32,28... | collective-permute-start | bytes 1130504 | tf_op jit(solution)/shard_map/ppermute | solution.py:461
  80.4 22.5 %collective-permute-start.23 = (f32[736,128]{1,0:T(8,128)S(1)}, f32[736,128]{1,0:T(8,128)S(1)}, u32[]{:S(2)}, u32[]{:S(2)}) collective-permute-start(f32[736,128]{1,0:T(8,128)S(1)} %add.68), channel_id=1, source_target_pairs={{0,252},{4,8},{8,4},{12,16},{16,12},{20,24},{24,20},{28,32},{32,28... | collective-permute-start | bytes 1130504 | tf_op jit(solution)/shard_map/ppermute | solution.py:461
  87.7 15.3 %collective-permute-start.25 = (f32[736,128]{1,0:T(8,128)S(1)}, f32[736,128]{1,0:T(8,128)S(1)}, u32[]{:S(2)}, u32[]{:S(2)}) collective-permute-start(f32[736,128]{1,0:T(8,128)S(1)} %add.70), channel_id=1, source_target_pairs={{0,4},{4,0},{8,12},{12,8},{16,20},{20,16},{24,28},{28,24},{32,36},... | collective-permute-start | bytes 1130504 | tf_op jit(solution)/shard_map/ppermute | solution.py:461
  87.8 10.8 %collective-permute-start.13 = (f32[200,128]{1,0:T(8,128)S(1)}, f32[200,128]{1,0:T(8,128)S(1)}, u32[]{:S(2)}, u32[]{:S(2)}) collective-permute-start(f32[200,128]{1,0:T(8,128)S(1)} %get-tuple-element.77), channel_id=1, source_target_pairs={{0,2},{1,3},{2,0},{3,1},{4,6},{5,7},{6,4},{7,5},{8,10},{9,11},{10,... | collective-permute-start | bytes 307208 | tf_op jit(solution)/shard_map/ppermute | solution.py:447
  88.3 12.4 %collective-permute-start.14 = (f32[200,128]{1,0:T(8,128)S(1)}, f32[200,128]{1,0:T(8,128)S(1)}, u32[]{:S(2)}, u32[]{:S(2)}) collective-permute-start(f32[200,128]{1,0:T(8,128)S(1)} %get-tuple-element.78), channel_id=1, source_target_pairs={{0,3},{1,2},{2,1},{3,0},{4,7},{5,6},{6,5},{7,4},{8,11},{9,10},{10,... | collective-permute-start | bytes 307208 | tf_op jit(solution)/shard_map/ppermute | solution.py:447
  91.0 9.7 %collective-permute-start.15 = (f32[200,128]{1,0:T(8,128)S(1)}, f32[200,128]{1,0:T(8,128)S(1)}, u32[]{:S(2)}, u32[]{:S(2)}) collective-permute-start(f32[200,128]{1,0:T(8,128)S(1)} %get-tuple-element.79), channel_id=1, source_target_pairs={{0,1},{1,0},{2,3},{3,2},{4,5},{5,4},{6,7},{7,6},{8,9},{9,8},{10,11... | collective-permute-start | bytes 307208 | tf_op jit(solution)/shard_map/ppermute | solution.py:447

commit v2 on v1

--- a/solution.py
+++ b/solution.py
@@ -157,15 +157,23 @@
     lax.fori_loop(0, count * LINES // rows, some_lines, 0, unroll=True)
 
 
-def column_passes(work, weights, count):
+def column_passes(source, target, count, weights):
     def planes(index, carry):
-        blocks = [pl.ds(pl.multiple_of((2 * index + half) * G, 8), G) for half in range(2)]
-        values = along_columns([work[block, :] for block in blocks], weights[...])
-        for block, value in zip(blocks, values):
-            work[block, :] = value
+        blocks = [2 * index + half for half in range(2)]
+        values = along_columns([source[0][source[1](plane), :] for plane in blocks], weights[...])
+        for plane, value in zip(blocks, values):
+            target[0][target[1](plane), :] = value
         return carry
 
     lax.fori_loop(0, count * PLANES // 2, planes, 0, unroll=3)
+
+
+def whole_plane(plane):
+    return pl.ds(pl.multiple_of(plane * G, 8), G)
+
+
+def spread_plane(count):
+    return lambda plane: pl.ds(plane, G, stride=count * PLANES + 1)
 
 
 def device_row(chunks, place, device, row):
@@ -205,7 +213,8 @@
 
 def spread_kernel(pairs, names, place, *refs):
     orbitals, (lines, columns), outs = refs[: len(names)], refs[len(names) : len(names) + 2], refs[len(names) + 2 : -1]
-    outs, work = views(outs, place), refs[-1]
+    outs, work, turned = views(outs[:-1], place), refs[-2], refs[-1]
+    wide = len(pairs) * PLANES + 1
     lane = lane_index(GROUPS)
     for index, pair in enumerate(pairs):
 
@@ -217,14 +226,14 @@
 
         unpack(16, load, store, lane)
     line_passes(work, lines, len(pairs))
-    column_passes(work, columns, len(pairs))
+    column_passes((work, whole_plane), (turned, spread_plane(len(pairs))), len(pairs), columns)
     lane = lane_index(PLANES)
     for index in range(len(pairs)):
         for out, step in zip(outs, STEPS):
-            first = (place[1] ^ step) * PLANES + index * LINES
+            first = (place[1] ^ step) * PLANES * wide + index * PLANES
 
             def load(line, first=first):
-                return work[pl.ds(first + line, PLANES, stride=G), :]
+                return turned[pl.ds(first + line * wide, PLANES), :]
 
             def store(tile, value, start=index * PAIR_ROWS, out=out):
                 out[start + tile * PLANES : start + (tile + 1) * PLANES, :] = value
@@ -271,23 +280,24 @@
 def gather_kernel(count, parts, names, shares, place, *refs):
     chunks, (lines, columns), refs = views(refs[:parts], place), refs[parts : parts + 2], refs[parts + 2 :]
     orbitals = refs[: len(names)]
-    outs, work = refs[-1 - len(shares) : -1], refs[-1]
+    outs, work, turned = refs[-2 - len(shares) : -2], refs[-2], refs[-1]
     outs = dict(zip(shares, outs))
-    added = dict(zip((2, -2), refs[len(names) : -1 - len(shares)]))
+    added = dict(zip((2, -2), refs[len(names) : -2 - len(shares)]))
+    wide = count * PLANES + 1
     upward = place[0] == 0
     lane = lane_index(PLANES)
     for pair in range(count):
         for chunk, step in zip(chunks, STEPS):
-            first = pair * LINES + (place[1] ^ step) * PLANES
+            first = (place[1] ^ step) * PLANES * wide + pair * PLANES
 
             def load(tile, start=pair * PAIR_ROWS, chunk=chunk):
                 return chunk[start + tile * PLANES : start + (tile + 1) * PLANES, :]
 
             def store(line, value, first=first):
-                work[pl.ds(first + line, PLANES, stride=G), :] = value
+                turned[pl.ds(first + line * wide, PLANES), :] = value
 
             unpack(PLANES, load, store, lane)
-    column_passes(work, columns, count)
+    column_passes((turned, spread_plane(count)), (work, whole_plane), count, columns)
     line_passes(work, lines, count)
     lane = lane_index(GROUPS)
 
@@ -376,7 +386,8 @@
 
 
 def work_of(count):
-    return [pltpu.VMEM((count * LINES, LANES), jnp.float32)]
+    turned = G * (count * PLANES + 1) + 7
+    return [pltpu.VMEM((rows, LANES), jnp.float32) for rows in (count * LINES, turned)]
 
 
 def spread_pairs(orbitals, pairs, tables, parts=DEVICES):

time: 104 us -> 104 us (level)
  no operation moved by 1% of the time
where the time goes in v2:
time: 104 us
  starting transfers between devices  53.9 us (52%)
  Pallas kernels  25 us (24%)
  waiting for transfers between devices  22.4 us (22%)
  local copies, waits for them, and re-layouts  1.23 us (1%)
    ppermute x8, starting transfers between devices, swapped(): return lax.ppermute(value, 'orb', pairs)  35.3 us
    ppermute x18, waiting for transfers between devices, exchanged(): received.append(lax.ppermute(chunk, 'grid', pairs))  19.6 us
    ppermute x18, starting transfers between devices, exchanged(): received.append(lax.ppermute(chunk, 'grid', pairs))  18.6 us
    pallas_call x3, Pallas kernels, gather_shares(): pl.pallas_call(lambda *refs: gather_kernel(count, parts, list(orbitals),...  9.58 us
    pallas_call x3, Pallas kernels, spread_pairs(): pl.pallas_call(lambda *refs: spread_kernel(pairs, list(orbitals), *refs),...  8.66 us
    pallas_call x3, Pallas kernels, solve_pencils(): pl.pallas_call(lambda *refs: pencil_kernel(count, parts, *refs), out_shap...  5.88 us
    ppermute x8, waiting for transfers between devices, swapped(): return lax.ppermute(value, 'orb', pairs)  2.8 us
  transfers between devices with their start and end apart: 26, of which 9 were waited for; matrix products, arithmetic and copies ran while one was open for 0% of the time, Pallas kernels for 23%

profile of v2, /device:TPU:1, one launch (start us, length us, event | category | flops | bytes accessed | tf_op | source)
XLA Modules:
  0.0 103.8 jit_solution(17648025416868624617)
XLA Ops:
  0.6 1.0 copy-done.4
  1.7 2.6 %collective-permute-start = (f32[736,128]{1,0:T(8,128)S(1)}, f32[736,128]{1,0:T(8,128)S(1)}, u32[]{:S(2)}, u32[]{:S(2)}) collective-permute-start(f32[736,128]{1,0:T(8,128)S(1)} %enter.1.refs_1_.refs_7_.own), channel_id=1, source_target_pairs={{0,4},{4,0},{8,12},{12,8},{16,20},{20,16},{24,28},{28,24},{32,36},... | collective-permute-start | bytes 1130504 | tf_op jit(solution)/shard_map/ppermute | solution.py:472
  4.2 9.5 %collective-permute-start.1 = (f32[736,128]{1,0:T(8,128)S(1)}, f32[736,128]{1,0:T(8,128)S(1)}, u32[]{:S(2)}, u32[]{:S(2)}) collective-permute-start(f32[736,128]{1,0:T(8,128)S(1)} %enter.1.refs_1_.refs_7_.own), channel_id=1, source_target_pairs={{0,252},{4,8},{8,4},{12,16},{16,12},{20,24},{24,20},{28,32},{32,28... | collective-permute-start | bytes 1130504 | tf_op jit(solution)/shard_map/ppermute | solution.py:472
  13.7 8.9 %collective-permute-start.2 = (f32[736,128]{1,0:T(8,128)S(1)}, f32[736,128]{1,0:T(8,128)S(1)}, u32[]{:S(2)}, u32[]{:S(2)}) collective-permute-start(f32[736,128]{1,0:T(8,128)S(1)} %collective-permute-done.refs_2_.refs_1_.refs_8_.refs_7_), channel_id=1, source_target_pairs={{0,252},{4,8},{8,4},{12,16},{16,12},{20,24},{24,20},{28,32},{32,28... | collective-permute-start | bytes 1130504 | tf_op jit(solution)/shard_map/ppermute | solution.py:472
  22.6 0.1 pad_add_fusion.refs_0_
  22.7 3.3 %spread.3 = (f32[400,128]{1,0:T(8,128)S(1)}, f32[400,128]{1,0:T(8,128)S(1)}, f32[400,128]{1,0:T(8,128)S(1)}, f32[400,128]{1,0:T(8,128)S(1)}) custom-call(s32[2]{0:T(128)S(1)} %pad_add_fusion.refs_0_, f32[736,128]{1,0:T(8,128)S(1)} %enter.1.refs_1_.refs_7_.own, f32[736,128]{1,0:T(8,128)S(1)} %collective-permute-done.refs_2_.refs_1_.refs_8_.refs_7_, ...), custom_call_target="tpu_custom_call" | custom-call | tf_op jit(solution)/shard_map/spread/pallas_call | solution.py:394
  26.0 0.5 collective-permute-start.4
  26.5 3.1 %collective-permute-start.5 = (f32[400,128]{1,0:T(8,128)S(1)}, f32[400,128]{1,0:T(8,128)S(1)}, u32[]{:S(2)}, u32[]{:S(2)}) collective-permute-start(f32[400,128]{1,0:T(8,128)S(1)} %get-tuple-element.54), channel_id=1, source_target_pairs={{0,3},{1,2},{2,1},{3,0},{4,7},{5,6},{6,5},{7,4},{8,11},{9,10},{10,... | collective-permute-start | bytes 614408 | tf_op jit(solution)/shard_map/ppermute | solution.py:458
  29.7 0.5 collective-permute-done.2.refs_3_.refs_9_
  30.1 0.9 collective-permute-done.3.refs_4_.refs_10_
  31.0 3.3 %spread.4 = (f32[400,128]{1,0:T(8,128)S(1)}, f32[400,128]{1,0:T(8,128)S(1)}, f32[400,128]{1,0:T(8,128)S(1)}, f32[400,128]{1,0:T(8,128)S(1)}) custom-call(s32[2]{0:T(128)S(1)} %pad_add_fusion.refs_0_, f32[736,128]{1,0:T(8,128)S(1)} %collective-permute-done.refs_2_.refs_1_.refs_8_.refs_7_, ...), custom_call_target="tpu_custom_call" | custom-call | tf_op jit(solution)/shard_map/spread/pallas_call | solution.py:394
  34.4 0.5 collective-permute-start.16
  34.9 4.0 %collective-permute-start.17 = (f32[400,128]{1,0:T(8,128)S(1)}, f32[400,128]{1,0:T(8,128)S(1)}, u32[]{:S(2)}, u32[]{:S(2)}) collective-permute-start(f32[400,128]{1,0:T(8,128)S(1)} %get-tuple-element.60), channel_id=1, source_target_pairs={{0,3},{1,2},{2,1},{3,0},{4,7},{5,6},{6,5},{7,4},{8,11},{9,10},{10,... | collective-permute-start | bytes 614408 | tf_op jit(solution)/shard_map/ppermute | solution.py:458
  38.9 0.2 fusion.refs_5_
  39.1 0.5 collective-permute-done.5.refs_3_
  39.6 0.1 copy-done.1
  39.8 0.1 copy-done.2
  39.9 2.2 %pencils.3 = (f32[400,128]{1,0:T(8,128)S(1)}, f32[400,128]{1,0:T(8,128)S(1)}, f32[400,128]{1,0:T(8,128)S(1)}, f32[400,128]{1,0:T(8,128)S(1)}) custom-call(s32[2]{0:T(128)S(1)} %pad_add_fusion.refs_0_, f32[400,128]{1,0:T(8,128)S(1)} %get-tuple-element.52.refs_1_, f32[400,128]{1,0:T(8,128)S(1)} %collective-permute-done.4.refs_2_, ...), custom_call_target="tpu_custom_call" | custom-call | tf_op jit(solution)/shard_map/pencils/pallas_call | solution.py:407
  42.1 0.5 collective-permute-start.7
  42.6 1.7 %collective-permute-start.8 = (f32[400,128]{1,0:T(8,128)S(1)}, f32[400,128]{1,0:T(8,128)S(1)}, u32[]{:S(2)}, u32[]{:S(2)}) collective-permute-start(f32[400,128]{1,0:T(8,128)S(1)} %get-tuple-element.69), channel_id=1, source_target_pairs={{0,3},{1,2},{2,1},{3,0},{4,7},{5,6},{6,5},{7,4},{8,11},{9,10},{10,... | collective-permute-start | bytes 614408 | tf_op jit(solution)/shard_map/ppermute | solution.py:458
  44.3 2.0 %spread.5 = (f32[200,128]{1,0:T(8,128)S(1)}, f32[200,128]{1,0:T(8,128)S(1)}, f32[200,128]{1,0:T(8,128)S(1)}, f32[200,128]{1,0:T(8,128)S(1)}) custom-call(s32[2]{0:T(128)S(1)} %pad_add_fusion.refs_0_, f32[736,128]{1,0:T(8,128)S(1)} %enter.1.refs_1_.refs_7_.own, bf16[256,256]{1,0:T(8,128)(2,1)S(1)} %copy-done, bf16[144,72]{1,0:T(8,128)(2,1)S(1)} %copy-done.3), custom_call_target="tpu_custom_call" | custom-call | tf_op jit(solution)/shard_map/spread/pallas_call | solution.py:394
  46.3 0.3 collective-permute-start.9
  46.6 2.3 %collective-permute-done.17.refs_3_ = f32[400,128]{1,0:T(8,128)S(1)} collective-permute-done((f32[400,128]{1,0:T(8,128)S(1)}, f32[400,128]{1,0:T(8,128)S(1)}, u32[]{:S(2)}, u32[]{:S(2)}) %collective-permute-start.17) | collective-permute-done | bytes 204832 | tf_op jit(solution)/shard_map/ppermute | solution.py:458
  48.9 2.2 %pencils.5 = (f32[400,128]{1,0:T(8,128)S(1)}, f32[400,128]{1,0:T(8,128)S(1)}, f32[400,128]{1,0:T(8,128)S(1)}, f32[400,128]{1,0:T(8,128)S(1)}) custom-call(s32[2]{0:T(128)S(1)} %pad_add_fusion.refs_0_, f32[400,128]{1,0:T(8,128)S(1)} %get-tuple-element.80.refs_1_, f32[400,128]{1,0:T(8,128)S(1)} %collective-permute-done.16.refs_2_, ...), custom_call_target="tpu_custom_call" | custom-call | tf_op jit(solution)/shard_map/pencils/pallas_call | solution.py:407
  51.2 0.5 collective-permute-start.19
  51.6 0.1 collective-permute-start.20
  51.8 2.3 %collective-permute-start.21 = (f32[400,128]{1,0:T(8,128)S(1)}, f32[400,128]{1,0:T(8,128)S(1)}, u32[]{:S(2)}, u32[]{:S(2)}) collective-permute-start(f32[400,128]{1,0:T(8,128)S(1)} %get-tuple-element.87), channel_id=1, source_target_pairs={{0,1},{1,0},{2,3},{3,2},{4,5},{5,4},{6,7},{7,6},{8,9},{9,8},{10,11... | collective-permute-start | bytes 614408 | tf_op jit(solution)/shard_map/ppermute | solution.py:458
  54.0 3.7 %collective-permute-done.8.refs_3_ = f32[400,128]{1,0:T(8,128)S(1)} collective-permute-done((f32[400,128]{1,0:T(8,128)S(1)}, f32[400,128]{1,0:T(8,128)S(1)}, u32[]{:S(2)}, u32[]{:S(2)}) %collective-permute-start.8) | collective-permute-done | bytes 204832 | tf_op jit(solution)/shard_map/ppermute | solution.py:458
  57.7 3.6 %gather.3 = (f32[736,128]{1,0:T(8,128)S(1)}, f32[736,128]{1,0:T(8,128)S(1)}, f32[736,128]{1,0:T(8,128)S(1)}) custom-call(s32[2]{0:T(128)S(1)} %pad_add_fusion.refs_0_, f32[400,128]{1,0:T(8,128)S(1)} %get-tuple-element.67.refs_1_, f32[400,128]{1,0:T(8,128)S(1)} %collective-permute-done.7.refs_2_, f32[400,128]{1,0:T(8,128)S(1)} %collective-permute-done.8.refs_3_, ...), custom_call_target="tpu_custom_call" | custom-call | tf_op jit(solution)/shard_map/gather/pallas_call | solution.py:419
  61.4 0.5 collective-permute-start.10
  61.8 0.1 collective-permute-start.11
  62.0 1.3 %collective-permute-start.12 = (f32[200,128]{1,0:T(8,128)S(1)}, f32[200,128]{1,0:T(8,128)S(1)}, u32[]{:S(2)}, u32[]{:S(2)}) collective-permute-start(f32[200,128]{1,0:T(8,128)S(1)} %get-tuple-element.75), channel_id=1, source_target_pairs={{0,1},{1,0},{2,3},{3,2},{4,5},{5,4},{6,7},{7,6},{8,9},{9,8},{10,11... | collective-permute-start | bytes 307208 | tf_op jit(solution)/shard_map/ppermute | solution.py:458
  63.3 3.3 %collective-permute-done.20.refs_3_ = f32[400,128]{1,0:T(8,128)S(1)} collective-permute-done((f32[400,128]{1,0:T(8,128)S(1)}, f32[400,128]{1,0:T(8,128)S(1)}, u32[]{:S(2)}, u32[]{:S(2)}) %collective-permute-start.20) | collective-permute-done | bytes 204832 | tf_op jit(solution)/shard_map/ppermute | solution.py:458
  66.6 3.8 %gather.5 = (f32[736,128]{1,0:T(8,128)S(1)}, f32[736,128]{1,0:T(8,128)S(1)}, f32[736,128]{1,0:T(8,128)S(1)}, f32[736,128]{1,0:T(8,128)S(1)}) custom-call(s32[2]{0:T(128)S(1)} %pad_add_fusion.refs_0_, f32[400,128]{1,0:T(8,128)S(1)} %get-tuple-element.88.refs_1_, f32[400,128]{1,0:T(8,128)S(1)} %collective-permute-done.19.refs_2_, ...), custom_call_target="tpu_custom_call" | custom-call | tf_op jit(solution)/shard_map/gather/pallas_call | solution.py:419
  70.5 0.1 collective-permute-start.22
  70.6 6.9 %collective-permute-start.24 = (f32[736,128]{1,0:T(8,128)S(1)}, f32[736,128]{1,0:T(8,128)S(1)}, u32[]{:S(2)}, u32[]{:S(2)}) collective-permute-start(f32[736,128]{1,0:T(8,128)S(1)} %get-tuple-element.97), channel_id=1, source_target_pairs={{0,252},{4,8},{8,4},{12,16},{16,12},{20,24},{24,20},{28,32},{32,28... | collective-permute-start | bytes 1130504 | tf_op jit(solution)/shard_map/ppermute | solution.py:472
  77.5 1.4 %pencils.4 = (f32[200,128]{1,0:T(8,128)S(1)}, f32[200,128]{1,0:T(8,128)S(1)}, f32[200,128]{1,0:T(8,128)S(1)}, f32[200,128]{1,0:T(8,128)S(1)}) custom-call(s32[2]{0:T(128)S(1)} %pad_add_fusion.refs_0_, f32[200,128]{1,0:T(8,128)S(1)} %get-tuple-element.72.refs_1_, f32[200,128]{1,0:T(8,128)S(1)} %collective-permute-done.10.refs_2_, ...), custom_call_target="tpu_custom_call" | custom-call | tf_op jit(solution)/shard_map/pencils/pallas_call | solution.py:407
  79.0 1.4 %collective-permute-done.22 = f32[736,128]{1,0:T(8,128)S(1)} collective-permute-done((f32[736,128]{1,0:T(8,128)S(1)}, f32[736,128]{1,0:T(8,128)S(1)}, u32[]{:S(2)}, u32[]{:S(2)}) %collective-permute-start.22) | collective-permute-done | bytes 376864 | tf_op jit(solution)/shard_map/ppermute | solution.py:472
  80.4 7.2 %collective-permute-start.23 = (f32[736,128]{1,0:T(8,128)S(1)}, f32[736,128]{1,0:T(8,128)S(1)}, u32[]{:S(2)}, u32[]{:S(2)}) collective-permute-start(f32[736,128]{1,0:T(8,128)S(1)} %add.68), channel_id=1, source_target_pairs={{0,252},{4,8},{8,4},{12,16},{16,12},{20,24},{24,20},{28,32},{32,28... | collective-permute-start | bytes 1130504 | tf_op jit(solution)/shard_map/ppermute | solution.py:472
  87.6 0.1 add.70
  87.7 0.1 collective-permute-start.25
  87.8 0.5 collective-permute-start.13
  88.3 2.7 %collective-permute-start.14 = (f32[200,128]{1,0:T(8,128)S(1)}, f32[200,128]{1,0:T(8,128)S(1)}, u32[]{:S(2)}, u32[]{:S(2)}) collective-permute-start(f32[200,128]{1,0:T(8,128)S(1)} %get-tuple-element.78), channel_id=1, source_target_pairs={{0,3},{1,2},{2,1},{3,0},{4,7},{5,6},{6,5},{7,4},{8,11},{9,10},{10,... | collective-permute-start | bytes 307208 | tf_op jit(solution)/shard_map/ppermute | solution.py:458
  91.0 7.5 %collective-permute-done.13.refs_2_ = f32[200,128]{1,0:T(8,128)S(1)} collective-permute-done((f32[200,128]{1,0:T(8,128)S(1)}, f32[200,128]{1,0:T(8,128)S(1)}, u32[]{:S(2)}, u32[]{:S(2)}) %collective-permute-start.13) | collective-permute-done | bytes 102432 | tf_op jit(solution)/shard_map/ppermute | solution.py:458
  98.5 2.2 %collective-permute-done.14.refs_3_ = f32[200,128]{1,0:T(8,128)S(1)} collective-permute-done((f32[200,128]{1,0:T(8,128)S(1)}, f32[200,128]{1,0:T(8,128)S(1)}, u32[]{:S(2)}, u32[]{:S(2)}) %collective-permute-start.14) | collective-permute-done | bytes 102432 | tf_op jit(solution)/shard_map/ppermute | solution.py:458
  100.7 2.1 %gather.4.refs_0_ = f32[736,128]{1,0:T(8,128)S(1)} custom-call(s32[2]{0:T(128)S(1)} %pad_add_fusion.refs_0_, f32[200,128]{1,0:T(8,128)S(1)} %get-tuple-element.76.refs_1_, f32[200,128]{1,0:T(8,128)S(1)} %collective-permute-done.13.refs_2_, f32[200,128]{1,0:T(8,128)S(1)} %collective-permute-done.14.refs_3_, f32[200,128]{1,0:T(8,128)S(1)} %collective-permute-done.15.refs_4_, ...), custom_call_target="tpu_custom_call" | custom-call | tf_op jit(solution)/shard_map/gather/pallas_call | solution.py:419
  102.9 0.1 add.69.refs_1_
  103.0 0.8 leave.1
  (32 shorter events, 0.2 us)
Async XLA Ops:
  0.6 1.0 copy-start.4
  1.6 21.1 %copy-start = (bf16[256,256]{1,0:T(8,128)(2,1)S(1)}, bf16[256,256]{1,0:T(8,128)(2,1)}, u32[]{:S(2)}) copy-start(bf16[256,256]{1,0:T(8,128)(2,1)} %constant.68.clone.refs_4_.refs_5_.refs_2_) | copy-start | bytes 393220
  1.6 21.0 %copy-start.3 = (bf16[144,72]{1,0:T(8,128)(2,1)S(1)}, bf16[144,72]{1,0:T(8,128)(2,1)}, u32[]{:S(2)}) copy-start(bf16[144,72]{1,0:T(8,128)(2,1)} %constant.69.clone.refs_5_.refs_6_.refs_3_) | copy-start | bytes 62212
  1.7 12.0 %collective-permute-start = (f32[736,128]{1,0:T(8,128)S(1)}, f32[736,128]{1,0:T(8,128)S(1)}, u32[]{:S(2)}, u32[]{:S(2)}) collective-permute-start(f32[736,128]{1,0:T(8,128)S(1)} %enter.1.refs_1_.refs_7_.own), channel_id=1, source_target_pairs={{0,4},{4,0},{8,12},{12,8},{16,20},{20,16},{24,28},{28,24},{32,36},... | collective-permute-start | bytes 1130504 | tf_op jit(solution)/shard_map/ppermute | solution.py:472
  4.2 18.4 %collective-permute-start.1 = (f32[736,128]{1,0:T(8,128)S(1)}, f32[736,128]{1,0:T(8,128)S(1)}, u32[]{:S(2)}, u32[]{:S(2)}) collective-permute-start(f32[736,128]{1,0:T(8,128)S(1)} %enter.1.refs_1_.refs_7_.own), channel_id=1, source_target_pairs={{0,252},{4,8},{8,4},{12,16},{16,12},{20,24},{24,20},{28,32},{32,28... | collective-permute-start | bytes 1130504 | tf_op jit(solution)/shard_map/ppermute | solution.py:472
  13.7 16.4 %collective-permute-start.2 = (f32[736,128]{1,0:T(8,128)S(1)}, f32[736,128]{1,0:T(8,128)S(1)}, u32[]{:S(2)}, u32[]{:S(2)}) collective-permute-start(f32[736,128]{1,0:T(8,128)S(1)} %collective-permute-done.refs_2_.refs_1_.refs_8_.refs_7_), channel_id=1, source_target_pairs={{0,252},{4,8},{8,4},{12,16},{16,12},{20,24},{24,20},{28,32},{32,28... | collective-permute-start | bytes 1130504 | tf_op jit(solution)/shard_map/ppermute | solution.py:472
  22.6 8.4 %collective-permute-start.3 = (f32[736,128]{1,0:T(8,128)S(1)}, f32[736,128]{1,0:T(8,128)S(1)}, u32[]{:S(2)}, u32[]{:S(2)}) collective-permute-start(f32[736,128]{1,0:T(8,128)S(1)} %collective-permute-done.1.refs_3_.refs_2_.refs_9_.refs_8_), channel_id=1, source_target_pairs={{0,4},{4,0},{8,12},{12,8},{16,20},{20,16},{24,28},{28,24},{32,36},... | collective-permute-start | bytes 1130504 | tf_op jit(solution)/shard_map/ppermute | solution.py:472
  26.0 12.8 %collective-permute-start.4 = (f32[400,128]{1,0:T(8,128)S(1)}, f32[400,128]{1,0:T(8,128)S(1)}, u32[]{:S(2)}, u32[]{:S(2)}) collective-permute-start(f32[400,128]{1,0:T(8,128)S(1)} %get-tuple-element.53), channel_id=1, source_target_pairs={{0,2},{1,3},{2,0},{3,1},{4,6},{5,7},{6,4},{7,5},{8,10},{9,11},{10,... | collective-permute-start | bytes 614408 | tf_op jit(solution)/shard_map/ppermute | solution.py:458
  26.5 13.1 %collective-permute-start.5 = (f32[400,128]{1,0:T(8,128)S(1)}, f32[400,128]{1,0:T(8,128)S(1)}, u32[]{:S(2)}, u32[]{:S(2)}) collective-permute-start(f32[400,128]{1,0:T(8,128)S(1)} %get-tuple-element.54), channel_id=1, source_target_pairs={{0,3},{1,2},{2,1},{3,0},{4,7},{5,6},{6,5},{7,4},{8,11},{9,10},{10,... | collective-permute-start | bytes 614408 | tf_op jit(solution)/shard_map/ppermute | solution.py:458
  29.7 10.0 %collective-permute-start.6 = (f32[400,128]{1,0:T(8,128)S(1)}, f32[400,128]{1,0:T(8,128)S(1)}, u32[]{:S(2)}, u32[]{:S(2)}) collective-permute-start(f32[400,128]{1,0:T(8,128)S(1)} %get-tuple-element.55), channel_id=1, source_target_pairs={{0,1},{1,0},{2,3},{3,2},{4,5},{5,4},{6,7},{7,6},{8,9},{9,8},{10,11... | collective-permute-start | bytes 614408 | tf_op jit(solution)/shard_map/ppermute | solution.py:458
  34.4 12.0 %collective-permute-start.16 = (f32[400,128]{1,0:T(8,128)S(1)}, f32[400,128]{1,0:T(8,128)S(1)}, u32[]{:S(2)}, u32[]{:S(2)}) collective-permute-start(f32[400,128]{1,0:T(8,128)S(1)} %get-tuple-element.59), channel_id=1, source_target_pairs={{0,2},{1,3},{2,0},{3,1},{4,6},{5,7},{6,4},{7,5},{8,10},{9,11},{10,... | collective-permute-start | bytes 614408 | tf_op jit(solution)/shard_map/ppermute | solution.py:458
  34.9 14.1 %collective-permute-start.17 = (f32[400,128]{1,0:T(8,128)S(1)}, f32[400,128]{1,0:T(8,128)S(1)}, u32[]{:S(2)}, u32[]{:S(2)}) collective-permute-start(f32[400,128]{1,0:T(8,128)S(1)} %get-tuple-element.60), channel_id=1, source_target_pairs={{0,3},{1,2},{2,1},{3,0},{4,7},{5,6},{6,5},{7,4},{8,11},{9,10},{10,... | collective-permute-start | bytes 614408 | tf_op jit(solution)/shard_map/ppermute | solution.py:458
  38.9 10.1 %collective-permute-start.18 = (f32[400,128]{1,0:T(8,128)S(1)}, f32[400,128]{1,0:T(8,128)S(1)}, u32[]{:S(2)}, u32[]{:S(2)}) collective-permute-start(f32[400,128]{1,0:T(8,128)S(1)} %get-tuple-element.61), channel_id=1, source_target_pairs={{0,1},{1,0},{2,3},{3,2},{4,5},{5,4},{6,7},{7,6},{8,9},{9,8},{10,11... | collective-permute-start | bytes 614408 | tf_op jit(solution)/shard_map/ppermute | solution.py:458
  38.9 0.9 copy-start.1
  38.9 1.0 copy-start.2
  42.1 9.7 %collective-permute-start.7 = (f32[400,128]{1,0:T(8,128)S(1)}, f32[400,128]{1,0:T(8,128)S(1)}, u32[]{:S(2)}, u32[]{:S(2)}) collective-permute-start(f32[400,128]{1,0:T(8,128)S(1)} %get-tuple-element.68), channel_id=1, source_target_pairs={{0,2},{1,3},{2,0},{3,1},{4,6},{5,7},{6,4},{7,5},{8,10},{9,11},{10,... | collective-permute-start | bytes 614408 | tf_op jit(solution)/shard_map/ppermute | solution.py:458
  42.6 15.1 %collective-permute-start.8 = (f32[400,128]{1,0:T(8,128)S(1)}, f32[400,128]{1,0:T(8,128)S(1)}, u32[]{:S(2)}, u32[]{:S(2)}) collective-permute-start(f32[400,128]{1,0:T(8,128)S(1)} %get-tuple-element.69), channel_id=1, source_target_pairs={{0,3},{1,2},{2,1},{3,0},{4,7},{5,6},{6,5},{7,4},{8,11},{9,10},{10,... | collective-permute-start | bytes 614408 | tf_op jit(solution)/shard_map/ppermute | solution.py:458
  46.3 11.4 %collective-permute-start.9 = (f32[400,128]{1,0:T(8,128)S(1)}, f32[400,128]{1,0:T(8,128)S(1)}, u32[]{:S(2)}, u32[]{:S(2)}) collective-permute-start(f32[400,128]{1,0:T(8,128)S(1)} %get-tuple-element.70), channel_id=1, source_target_pairs={{0,1},{1,0},{2,3},{3,2},{4,5},{5,4},{6,7},{7,6},{8,9},{9,8},{10,11... | collective-permute-start | bytes 614408 | tf_op jit(solution)/shard_map/ppermute | solution.py:458
  51.2 10.8 %collective-permute-start.19 = (f32[400,128]{1,0:T(8,128)S(1)}, f32[400,128]{1,0:T(8,128)S(1)}, u32[]{:S(2)}, u32[]{:S(2)}) collective-permute-start(f32[400,128]{1,0:T(8,128)S(1)} %get-tuple-element.85), channel_id=1, source_target_pairs={{0,2},{1,3},{2,0},{3,1},{4,6},{5,7},{6,4},{7,5},{8,10},{9,11},{10,... | collective-permute-start | bytes 614408 | tf_op jit(solution)/shard_map/ppermute | solution.py:458
  51.6 15.0 %collective-permute-start.20 = (f32[400,128]{1,0:T(8,128)S(1)}, f32[400,128]{1,0:T(8,128)S(1)}, u32[]{:S(2)}, u32[]{:S(2)}) collective-permute-start(f32[400,128]{1,0:T(8,128)S(1)} %get-tuple-element.86), channel_id=1, source_target_pairs={{0,3},{1,2},{2,1},{3,0},{4,7},{5,6},{6,5},{7,4},{8,11},{9,10},{10,... | collective-permute-start | bytes 614408 | tf_op jit(solution)/shard_map/ppermute | solution.py:458
  51.8 14.9 %collective-permute-start.21 = (f32[400,128]{1,0:T(8,128)S(1)}, f32[400,128]{1,0:T(8,128)S(1)}, u32[]{:S(2)}, u32[]{:S(2)}) collective-permute-start(f32[400,128]{1,0:T(8,128)S(1)} %get-tuple-element.87), channel_id=1, source_target_pairs={{0,1},{1,0},{2,3},{3,2},{4,5},{5,4},{6,7},{7,6},{8,9},{9,8},{10,11... | collective-permute-start | bytes 614408 | tf_op jit(solution)/shard_map/ppermute | solution.py:458
  61.4 9.1 %collective-permute-start.10 = (f32[200,128]{1,0:T(8,128)S(1)}, f32[200,128]{1,0:T(8,128)S(1)}, u32[]{:S(2)}, u32[]{:S(2)}) collective-permute-start(f32[200,128]{1,0:T(8,128)S(1)} %get-tuple-element.73), channel_id=1, source_target_pairs={{0,2},{1,3},{2,0},{3,1},{4,6},{5,7},{6,4},{7,5},{8,10},{9,11},{10,... | collective-permute-start | bytes 307208 | tf_op jit(solution)/shard_map/ppermute | solution.py:458
  61.8 8.6 %collective-permute-start.11 = (f32[200,128]{1,0:T(8,128)S(1)}, f32[200,128]{1,0:T(8,128)S(1)}, u32[]{:S(2)}, u32[]{:S(2)}) collective-permute-start(f32[200,128]{1,0:T(8,128)S(1)} %get-tuple-element.74), channel_id=1, source_target_pairs={{0,3},{1,2},{2,1},{3,0},{4,7},{5,6},{6,5},{7,4},{8,11},{9,10},{10,... | collective-permute-start | bytes 307208 | tf_op jit(solution)/shard_map/ppermute | solution.py:458
  62.0 8.5 %collective-permute-start.12 = (f32[200,128]{1,0:T(8,128)S(1)}, f32[200,128]{1,0:T(8,128)S(1)}, u32[]{:S(2)}, u32[]{:S(2)}) collective-permute-start(f32[200,128]{1,0:T(8,128)S(1)} %get-tuple-element.75), channel_id=1, source_target_pairs={{0,1},{1,0},{2,3},{3,2},{4,5},{5,4},{6,7},{7,6},{8,9},{9,8},{10,11... | collective-permute-start | bytes 307208 | tf_op jit(solution)/shard_map/ppermute | solution.py:458
  70.5 9.9 %collective-permute-start.22 = (f32[736,128]{1,0:T(8,128)S(1)}, f32[736,128]{1,0:T(8,128)S(1)}, u32[]{:S(2)}, u32[]{:S(2)}) collective-permute-start(f32[736,128]{1,0:T(8,128)S(1)} %get-tuple-element.95), channel_id=1, source_target_pairs={{0,4},{4,0},{8,12},{12,8},{16,20},{20,16},{24,28},{28,24},{32,36},... | collective-permute-start | bytes 1130504 | tf_op jit(solution)/shard_map/ppermute | solution.py:472
  70.6 17.0 %collective-permute-start.24 = (f32[736,128]{1,0:T(8,128)S(1)}, f32[736,128]{1,0:T(8,128)S(1)}, u32[]{:S(2)}, u32[]{:S(2)}) collective-permute-start(f32[736,128]{1,0:T(8,128)S(1)} %get-tuple-element.97), channel_id=1, source_target_pairs={{0,252},{4,8},{8,4},{12,16},{16,12},{20,24},{24,20},{28,32},{32,28... | collective-permute-start | bytes 1130504 | tf_op jit(solution)/shard_map/ppermute | solution.py:472
  80.4 22.5 %collective-permute-start.23 = (f32[736,128]{1,0:T(8,128)S(1)}, f32[736,128]{1,0:T(8,128)S(1)}, u32[]{:S(2)}, u32[]{:S(2)}) collective-permute-start(f32[736,128]{1,0:T(8,128)S(1)} %add.68), channel_id=1, source_target_pairs={{0,252},{4,8},{8,4},{12,16},{16,12},{20,24},{24,20},{28,32},{32,28... | collective-permute-start | bytes 1130504 | tf_op jit(solution)/shard_map/ppermute | solution.py:472
  87.7 15.3 %collective-permute-start.25 = (f32[736,128]{1,0:T(8,128)S(1)}, f32[736,128]{1,0:T(8,128)S(1)}, u32[]{:S(2)}, u32[]{:S(2)}) collective-permute-start(f32[736,128]{1,0:T(8,128)S(1)} %add.70), channel_id=1, source_target_pairs={{0,4},{4,0},{8,12},{12,8},{16,20},{20,16},{24,28},{28,24},{32,36},... | collective-permute-start | bytes 1130504 | tf_op jit(solution)/shard_map/ppermute | solution.py:472
  87.8 10.8 %collective-permute-start.13 = (f32[200,128]{1,0:T(8,128)S(1)}, f32[200,128]{1,0:T(8,128)S(1)}, u32[]{:S(2)}, u32[]{:S(2)}) collective-permute-start(f32[200,128]{1,0:T(8,128)S(1)} %get-tuple-element.77), channel_id=1, source_target_pairs={{0,2},{1,3},{2,0},{3,1},{4,6},{5,7},{6,4},{7,5},{8,10},{9,11},{10,... | collective-permute-start | bytes 307208 | tf_op jit(solution)/shard_map/ppermute | solution.py:458
  88.3 12.4 %collective-permute-start.14 = (f32[200,128]{1,0:T(8,128)S(1)}, f32[200,128]{1,0:T(8,128)S(1)}, u32[]{:S(2)}, u32[]{:S(2)}) collective-permute-start(f32[200,128]{1,0:T(8,128)S(1)} %get-tuple-element.78), channel_id=1, source_target_pairs={{0,3},{1,2},{2,1},{3,0},{4,7},{5,6},{6,5},{7,4},{8,11},{9,10},{10,... | collective-permute-start | bytes 307208 | tf_op jit(solution)/shard_map/ppermute | solution.py:458
  91.0 9.7 %collective-permute-start.15 = (f32[200,128]{1,0:T(8,128)S(1)}, f32[200,128]{1,0:T(8,128)S(1)}, u32[]{:S(2)}, u32[]{:S(2)}) collective-permute-start(f32[200,128]{1,0:T(8,128)S(1)} %get-tuple-element.79), channel_id=1, source_target_pairs={{0,1},{1,0},{2,3},{3,2},{4,5},{5,4},{6,7},{7,6},{8,9},{9,8},{10,11... | collective-permute-start | bytes 307208 | tf_op jit(solution)/shard_map/ppermute | solution.py:458

commit v3 on v1

--- a/solution.py
+++ b/solution.py
@@ -20,6 +20,7 @@
 TILES = 11
 PAIR_ROWS = 200
 STEP = 24
+DEPTH = 80
 SCREENING = 0.09
 FRACTION = 0.25
 CELLS = float(G * G * G)
@@ -43,28 +44,35 @@
     return weights
 
 
+def stacked(left):
+    gap = np.zeros((left[0].shape[0], DEPTH - G), jnp.bfloat16)
+    high, low = left
+    return np.concatenate([high, gap, low, gap, high, gap], axis=1)
+
+
+def padded(table, rows):
+    return np.concatenate([table, np.zeros((rows - table.shape[0], table.shape[1]), table.dtype)], axis=0)
+
+
 def column_weights():
-    return np.concatenate(hartley_halves(), axis=0)
-
-
-def spread(table):
-    wide = np.zeros((G, DEVICES * STEP), jnp.bfloat16)
-    for device in range(DEVICES):
-        wide[:, device * STEP : device * STEP + PLANES] = table[:, device * PLANES : (device + 1) * PLANES]
-    return wide
+    return padded(stacked(hartley_halves()), DEPTH)
 
 
 def in_order(table, device):
     blocks = np.split(table, DEVICES, axis=1)
-    return np.concatenate([blocks[device ^ step] for step in STEPS], axis=1)
+    return [blocks[device ^ step] for step in STEPS]
 
 
 def forward_weights(device):
-    return np.concatenate([spread(in_order(half, device)) for half in hartley_halves()], axis=0)
+    halves_in_order = [np.concatenate(in_order(half, device), axis=1) for half in hartley_halves()]
+    return padded(stacked(halves_in_order), DEPTH)
 
 
 def backward_weights(device):
-    return np.concatenate([spread(in_order(half, device)).T for half in hartley_halves()], axis=0)
+    spread = []
+    for half in hartley_halves():
+        spread.append(np.concatenate([padded(block.T, STEP) for block in in_order(half, device)], axis=0))
+    return stacked(spread)
 
 
 def wavenumber(indices):
@@ -97,10 +105,10 @@
 
 
 def along_columns(values, weights):
-    rows = weights.shape[0] // 2
-    high, low = halves(jnp.concatenate(values, axis=1) if len(values) > 1 else values[0])
-    result = product(weights, high)
-    result = result[:rows] + result[rows:] + product(weights[:rows], low)
+    value = jnp.concatenate(values, axis=1) if len(values) > 1 else values[0]
+    value = jnp.concatenate([value, jnp.zeros((DEPTH - G, value.shape[1]), jnp.float32)], axis=0)
+    high, low = halves(value)
+    result = product(weights, jnp.concatenate([high, high, low], axis=0))
     return [result[:, index * LANES : (index + 1) * LANES] for index in range(len(values))]
 
 
@@ -162,7 +170,7 @@
         blocks = [pl.ds(pl.multiple_of((2 * index + half) * G, 8), G) for half in range(2)]
         values = along_columns([work[block, :] for block in blocks], weights[...])
         for block, value in zip(blocks, values):
-            work[block, :] = value
+            work[block, :] = value[:G]
         return carry
 
     lax.fori_loop(0, count * PLANES // 2, planes, 0, unroll=3)
@@ -239,7 +247,6 @@
     chunks = views(chunks, place)
     forward, backward = forward.at[place[1]], backward.at[place[1]]
     lane = lane_index(G)
-    gap = jnp.zeros((STEP - PLANES, LANES), jnp.float32)
     energies = [jnp.zeros((G, LANES), jnp.float32) for _ in range(count)]
     places = [(pair, tile) for tile in range(TILES) for pair in range(count)]
     for group in range(0, len(places), 2):
@@ -247,12 +254,10 @@
         values = []
         for pair, tile in now:
             start = pair * PAIR_ROWS + tile * PLANES
-            pieces = []
-            for chunk in chunks:
-                pieces += [chunk[start : start + PLANES, :], gap]
-            values.append(jnp.concatenate(pieces, axis=0))
+            values.append(jnp.concatenate([chunk[start : start + PLANES, :] for chunk in chunks], axis=0))
         solved = []
         for (pair, tile), spectral in zip(now, along_columns(values, forward[...])):
+            spectral = spectral[:G]
             solved.append(spectral * kernel[:, tile * LANES : (tile + 1) * LANES])
             if tile == TILES - 1:
                 spectral = jnp.where(lane < PLANES * G - tile * LANES, spectral, 0.0)

time: 104 us -> 104 us (level)
  Pallas kernels: 25 us -> 21.7 us
  waiting for transfers between devices: 22.4 us -> 24.9 us
    pallas_call x3, Pallas kernels: 5.87 us -> 3.58 us  [solve_pencils(): pl.pallas_call(lambda *refs: pencil_kernel(count, parts, *refs), out_shap...]
    ppermute x18, waiting for transfers between devices: 19.6 us -> 21.5 us  [exchanged(): received.append(lax.ppermute(chunk, 'grid', pairs))]
  transfers between devices with their start and end apart: 26 -> 26, of which waited for: 9 -> 10; matrix products, arithmetic and copies ran while one was open for 0% -> 0% of each run, Pallas kernels for 23% -> 20%
where the time goes in v3:
time: 104 us
  starting transfers between devices  54.6 us (52%)
  waiting for transfers between devices  24.9 us (24%)
  Pallas kernels  21.7 us (21%)
  local copies, waits for them, and re-layouts  1.23 us (1%)
    ppermute x8, starting transfers between devices, swapped(): return lax.ppermute(value, 'orb', pairs)  35.5 us
    ppermute x18, waiting for transfers between devices, exchanged(): received.append(lax.ppermute(chunk, 'grid', pairs))  21.5 us
    ppermute x18, starting transfers between devices, exchanged(): received.append(lax.ppermute(chunk, 'grid', pairs))  19.1 us
    pallas_call x3, Pallas kernels, gather_shares(): pl.pallas_call(lambda *refs: gather_kernel(count, parts, list(orbitals),...  9.04 us
    pallas_call x3, Pallas kernels, spread_pairs(): pl.pallas_call(lambda *refs: spread_kernel(pairs, list(orbitals), *refs),...  8.18 us
    pallas_call x3, Pallas kernels, solve_pencils(): pl.pallas_call(lambda *refs: pencil_kernel(count, parts, *refs), out_shap...  3.58 us
    ppermute x8, waiting for transfers between devices, swapped(): return lax.ppermute(value, 'orb', pairs)  3.39 us
  transfers between devices with their start and end apart: 26, of which 10 were waited for; matrix products, arithmetic and copies ran while one was open for 0% of the time, Pallas kernels for 20%

profile of v3, /device:TPU:1, one launch (start us, length us, event | category | flops | bytes accessed | tf_op | source)
XLA Modules:
  0.0 103.7 jit_solution(5603679245328129990)
XLA Ops:
  0.6 1.0 copy-done.4
  1.7 2.6 %collective-permute-start = (f32[736,128]{1,0:T(8,128)S(1)}, f32[736,128]{1,0:T(8,128)S(1)}, u32[]{:S(2)}, u32[]{:S(2)}) collective-permute-start(f32[736,128]{1,0:T(8,128)S(1)} %enter.1.refs_1_.refs_7_.own), channel_id=1, source_target_pairs={{0,4},{4,0},{8,12},{12,8},{16,20},{20,16},{24,28},{28,24},{32,36},... | collective-permute-start | bytes 1130504 | tf_op jit(solution)/shard_map/ppermute | solution.py:466
  4.2 9.5 %collective-permute-start.1 = (f32[736,128]{1,0:T(8,128)S(1)}, f32[736,128]{1,0:T(8,128)S(1)}, u32[]{:S(2)}, u32[]{:S(2)}) collective-permute-start(f32[736,128]{1,0:T(8,128)S(1)} %enter.1.refs_1_.refs_7_.own), channel_id=1, source_target_pairs={{0,252},{4,8},{8,4},{12,16},{16,12},{20,24},{24,20},{28,32},{32,28... | collective-permute-start | bytes 1130504 | tf_op jit(solution)/shard_map/ppermute | solution.py:466
  13.7 8.9 %collective-permute-start.2 = (f32[736,128]{1,0:T(8,128)S(1)}, f32[736,128]{1,0:T(8,128)S(1)}, u32[]{:S(2)}, u32[]{:S(2)}) collective-permute-start(f32[736,128]{1,0:T(8,128)S(1)} %collective-permute-done.refs_2_.refs_1_.refs_8_.refs_7_), channel_id=1, source_target_pairs={{0,252},{4,8},{8,4},{12,16},{16,12},{20,24},{24,20},{28,32},{32,28... | collective-permute-start | bytes 1130504 | tf_op jit(solution)/shard_map/ppermute | solution.py:466
  22.6 0.1 pad_add_fusion.refs_0_
  22.7 3.1 %spread.3 = (f32[400,128]{1,0:T(8,128)S(1)}, f32[400,128]{1,0:T(8,128)S(1)}, f32[400,128]{1,0:T(8,128)S(1)}, f32[400,128]{1,0:T(8,128)S(1)}) custom-call(s32[2]{0:T(128)S(1)} %pad_add_fusion.refs_0_, f32[736,128]{1,0:T(8,128)S(1)} %enter.1.refs_1_.refs_7_.own, f32[736,128]{1,0:T(8,128)S(1)} %collective-permute-done.refs_2_.refs_1_.refs_8_.refs_7_, ...), custom_call_target="tpu_custom_call" | custom-call | tf_op jit(solution)/shard_map/spread/pallas_call | solution.py:388
  25.8 0.5 collective-permute-start.4
  26.3 3.1 %collective-permute-start.5 = (f32[400,128]{1,0:T(8,128)S(1)}, f32[400,128]{1,0:T(8,128)S(1)}, u32[]{:S(2)}, u32[]{:S(2)}) collective-permute-start(f32[400,128]{1,0:T(8,128)S(1)} %get-tuple-element.54), channel_id=1, source_target_pairs={{0,3},{1,2},{2,1},{3,0},{4,7},{5,6},{6,5},{7,4},{8,11},{9,10},{10,... | collective-permute-start | bytes 614408 | tf_op jit(solution)/shard_map/ppermute | solution.py:452
  29.5 0.7 collective-permute-done.2.refs_3_.refs_9_
  30.1 0.9 collective-permute-done.3.refs_4_.refs_10_
  31.0 3.1 %spread.4 = (f32[400,128]{1,0:T(8,128)S(1)}, f32[400,128]{1,0:T(8,128)S(1)}, f32[400,128]{1,0:T(8,128)S(1)}, f32[400,128]{1,0:T(8,128)S(1)}) custom-call(s32[2]{0:T(128)S(1)} %pad_add_fusion.refs_0_, f32[736,128]{1,0:T(8,128)S(1)} %collective-permute-done.refs_2_.refs_1_.refs_8_.refs_7_, ...), custom_call_target="tpu_custom_call" | custom-call | tf_op jit(solution)/shard_map/spread/pallas_call | solution.py:388
  34.2 0.5 collective-permute-start.16
  34.7 4.0 %collective-permute-start.17 = (f32[400,128]{1,0:T(8,128)S(1)}, f32[400,128]{1,0:T(8,128)S(1)}, u32[]{:S(2)}, u32[]{:S(2)}) collective-permute-start(f32[400,128]{1,0:T(8,128)S(1)} %get-tuple-element.60), channel_id=1, source_target_pairs={{0,3},{1,2},{2,1},{3,0},{4,7},{5,6},{6,5},{7,4},{8,11},{9,10},{10,... | collective-permute-start | bytes 614408 | tf_op jit(solution)/shard_map/ppermute | solution.py:452
  38.7 0.2 fusion.refs_5_
  38.9 0.5 collective-permute-done.5.refs_3_
  39.5 0.1 copy-done.1
  39.6 0.1 copy-done.2
  39.7 1.3 %pencils.3 = (f32[400,128]{1,0:T(8,128)S(1)}, f32[400,128]{1,0:T(8,128)S(1)}, f32[400,128]{1,0:T(8,128)S(1)}, f32[400,128]{1,0:T(8,128)S(1)}) custom-call(s32[2]{0:T(128)S(1)} %pad_add_fusion.refs_0_, f32[400,128]{1,0:T(8,128)S(1)} %get-tuple-element.52.refs_1_, f32[400,128]{1,0:T(8,128)S(1)} %collective-permute-done.4.refs_2_, ...), custom_call_target="tpu_custom_call" | custom-call | tf_op jit(solution)/shard_map/pencils/pallas_call | solution.py:401
  40.9 0.5 collective-permute-start.7
  41.4 1.7 %collective-permute-start.8 = (f32[400,128]{1,0:T(8,128)S(1)}, f32[400,128]{1,0:T(8,128)S(1)}, u32[]{:S(2)}, u32[]{:S(2)}) collective-permute-start(f32[400,128]{1,0:T(8,128)S(1)} %get-tuple-element.69), channel_id=1, source_target_pairs={{0,3},{1,2},{2,1},{3,0},{4,7},{5,6},{6,5},{7,4},{8,11},{9,10},{10,... | collective-permute-start | bytes 614408 | tf_op jit(solution)/shard_map/ppermute | solution.py:452
  43.2 1.9 %spread.5 = (f32[200,128]{1,0:T(8,128)S(1)}, f32[200,128]{1,0:T(8,128)S(1)}, f32[200,128]{1,0:T(8,128)S(1)}, f32[200,128]{1,0:T(8,128)S(1)}) custom-call(s32[2]{0:T(128)S(1)} %pad_add_fusion.refs_0_, f32[736,128]{1,0:T(8,128)S(1)} %enter.1.refs_1_.refs_7_.own, bf16[256,256]{1,0:T(8,128)(2,1)S(1)} %copy-done, bf16[80,240]{1,0:T(8,128)(2,1)S(1)} %copy-done.3), custom_call_target="tpu_custom_call" | custom-call | tf_op jit(solution)/shard_map/spread/pallas_call | solution.py:388
  45.1 0.3 collective-permute-start.9
  45.4 3.3 %collective-permute-done.17.refs_3_ = f32[400,128]{1,0:T(8,128)S(1)} collective-permute-done((f32[400,128]{1,0:T(8,128)S(1)}, f32[400,128]{1,0:T(8,128)S(1)}, u32[]{:S(2)}, u32[]{:S(2)}) %collective-permute-start.17) | collective-permute-done | bytes 204832 | tf_op jit(solution)/shard_map/ppermute | solution.py:452
  48.7 1.3 %pencils.5 = (f32[400,128]{1,0:T(8,128)S(1)}, f32[400,128]{1,0:T(8,128)S(1)}, f32[400,128]{1,0:T(8,128)S(1)}, f32[400,128]{1,0:T(8,128)S(1)}) custom-call(s32[2]{0:T(128)S(1)} %pad_add_fusion.refs_0_, f32[400,128]{1,0:T(8,128)S(1)} %get-tuple-element.80.refs_1_, f32[400,128]{1,0:T(8,128)S(1)} %collective-permute-done.16.refs_2_, ...), custom_call_target="tpu_custom_call" | custom-call | tf_op jit(solution)/shard_map/pencils/pallas_call | solution.py:401
  50.0 0.5 collective-permute-start.19
  50.5 0.1 collective-permute-start.20
  50.6 0.5 collective-permute-done.7.refs_2_
  51.1 2.7 %collective-permute-start.21 = (f32[400,128]{1,0:T(8,128)S(1)}, f32[400,128]{1,0:T(8,128)S(1)}, u32[]{:S(2)}, u32[]{:S(2)}) collective-permute-start(f32[400,128]{1,0:T(8,128)S(1)} %get-tuple-element.87), channel_id=1, source_target_pairs={{0,1},{1,0},{2,3},{3,2},{4,5},{5,4},{6,7},{7,6},{8,9},{9,8},{10,11... | collective-permute-start | bytes 614408 | tf_op jit(solution)/shard_map/ppermute | solution.py:452
  53.8 3.7 %collective-permute-done.8.refs_3_ = f32[400,128]{1,0:T(8,128)S(1)} collective-permute-done((f32[400,128]{1,0:T(8,128)S(1)}, f32[400,128]{1,0:T(8,128)S(1)}, u32[]{:S(2)}, u32[]{:S(2)}) %collective-permute-start.8) | collective-permute-done | bytes 204832 | tf_op jit(solution)/shard_map/ppermute | solution.py:452
  57.5 3.4 %gather.3 = (f32[736,128]{1,0:T(8,128)S(1)}, f32[736,128]{1,0:T(8,128)S(1)}, f32[736,128]{1,0:T(8,128)S(1)}) custom-call(s32[2]{0:T(128)S(1)} %pad_add_fusion.refs_0_, f32[400,128]{1,0:T(8,128)S(1)} %get-tuple-element.67.refs_1_, f32[400,128]{1,0:T(8,128)S(1)} %collective-permute-done.7.refs_2_, f32[400,128]{1,0:T(8,128)S(1)} %collective-permute-done.8.refs_3_, ...), custom_call_target="tpu_custom_call" | custom-call | tf_op jit(solution)/shard_map/gather/pallas_call | solution.py:413
  61.0 0.5 collective-permute-start.10
  61.4 0.1 collective-permute-start.11
  61.6 1.3 %collective-permute-start.12 = (f32[200,128]{1,0:T(8,128)S(1)}, f32[200,128]{1,0:T(8,128)S(1)}, u32[]{:S(2)}, u32[]{:S(2)}) collective-permute-start(f32[200,128]{1,0:T(8,128)S(1)} %get-tuple-element.75), channel_id=1, source_target_pairs={{0,1},{1,0},{2,3},{3,2},{4,5},{5,4},{6,7},{7,6},{8,9},{9,8},{10,11... | collective-permute-start | bytes 307208 | tf_op jit(solution)/shard_map/ppermute | solution.py:452
  62.9 3.7 %collective-permute-done.20.refs_3_ = f32[400,128]{1,0:T(8,128)S(1)} collective-permute-done((f32[400,128]{1,0:T(8,128)S(1)}, f32[400,128]{1,0:T(8,128)S(1)}, u32[]{:S(2)}, u32[]{:S(2)}) %collective-permute-start.20) | collective-permute-done | bytes 204832 | tf_op jit(solution)/shard_map/ppermute | solution.py:452
  66.6 3.6 %gather.5 = (f32[736,128]{1,0:T(8,128)S(1)}, f32[736,128]{1,0:T(8,128)S(1)}, f32[736,128]{1,0:T(8,128)S(1)}, f32[736,128]{1,0:T(8,128)S(1)}) custom-call(s32[2]{0:T(128)S(1)} %pad_add_fusion.refs_0_, f32[400,128]{1,0:T(8,128)S(1)} %get-tuple-element.88.refs_1_, f32[400,128]{1,0:T(8,128)S(1)} %collective-permute-done.19.refs_2_, ...), custom_call_target="tpu_custom_call" | custom-call | tf_op jit(solution)/shard_map/gather/pallas_call | solution.py:413
  70.2 0.1 collective-permute-start.22
  70.3 7.2 %collective-permute-start.24 = (f32[736,128]{1,0:T(8,128)S(1)}, f32[736,128]{1,0:T(8,128)S(1)}, u32[]{:S(2)}, u32[]{:S(2)}) collective-permute-start(f32[736,128]{1,0:T(8,128)S(1)} %get-tuple-element.97), channel_id=1, source_target_pairs={{0,252},{4,8},{8,4},{12,16},{16,12},{20,24},{24,20},{28,32},{32,28... | collective-permute-start | bytes 1130504 | tf_op jit(solution)/shard_map/ppermute | solution.py:466
  77.5 1.0 %pencils.4 = (f32[200,128]{1,0:T(8,128)S(1)}, f32[200,128]{1,0:T(8,128)S(1)}, f32[200,128]{1,0:T(8,128)S(1)}, f32[200,128]{1,0:T(8,128)S(1)}) custom-call(s32[2]{0:T(128)S(1)} %pad_add_fusion.refs_0_, f32[200,128]{1,0:T(8,128)S(1)} %get-tuple-element.72.refs_1_, f32[200,128]{1,0:T(8,128)S(1)} %collective-permute-done.10.refs_2_, ...), custom_call_target="tpu_custom_call" | custom-call | tf_op jit(solution)/shard_map/pencils/pallas_call | solution.py:401
  78.6 1.8 %collective-permute-done.22 = f32[736,128]{1,0:T(8,128)S(1)} collective-permute-done((f32[736,128]{1,0:T(8,128)S(1)}, f32[736,128]{1,0:T(8,128)S(1)}, u32[]{:S(2)}, u32[]{:S(2)}) %collective-permute-start.22) | collective-permute-done | bytes 376864 | tf_op jit(solution)/shard_map/ppermute | solution.py:466
  80.4 0.1 add.68
  80.4 7.2 %collective-permute-start.23 = (f32[736,128]{1,0:T(8,128)S(1)}, f32[736,128]{1,0:T(8,128)S(1)}, u32[]{:S(2)}, u32[]{:S(2)}) collective-permute-start(f32[736,128]{1,0:T(8,128)S(1)} %add.68), channel_id=1, source_target_pairs={{0,252},{4,8},{8,4},{12,16},{16,12},{20,24},{24,20},{28,32},{32,28... | collective-permute-start | bytes 1130504 | tf_op jit(solution)/shard_map/ppermute | solution.py:466
  87.7 0.1 collective-permute-start.25
  87.8 0.1 collective-permute-start.13
  87.9 3.1 %collective-permute-start.14 = (f32[200,128]{1,0:T(8,128)S(1)}, f32[200,128]{1,0:T(8,128)S(1)}, u32[]{:S(2)}, u32[]{:S(2)}) collective-permute-start(f32[200,128]{1,0:T(8,128)S(1)} %get-tuple-element.78), channel_id=1, source_target_pairs={{0,3},{1,2},{2,1},{3,0},{4,7},{5,6},{6,5},{7,4},{8,11},{9,10},{10,... | collective-permute-start | bytes 307208 | tf_op jit(solution)/shard_map/ppermute | solution.py:452
  91.0 7.5 %collective-permute-done.13.refs_2_ = f32[200,128]{1,0:T(8,128)S(1)} collective-permute-done((f32[200,128]{1,0:T(8,128)S(1)}, f32[200,128]{1,0:T(8,128)S(1)}, u32[]{:S(2)}, u32[]{:S(2)}) %collective-permute-start.13) | collective-permute-done | bytes 102432 | tf_op jit(solution)/shard_map/ppermute | solution.py:452
  98.5 2.2 %collective-permute-done.14.refs_3_ = f32[200,128]{1,0:T(8,128)S(1)} collective-permute-done((f32[200,128]{1,0:T(8,128)S(1)}, f32[200,128]{1,0:T(8,128)S(1)}, u32[]{:S(2)}, u32[]{:S(2)}) %collective-permute-start.14) | collective-permute-done | bytes 102432 | tf_op jit(solution)/shard_map/ppermute | solution.py:452
  100.7 2.0 %gather.4.refs_0_ = f32[736,128]{1,0:T(8,128)S(1)} custom-call(s32[2]{0:T(128)S(1)} %pad_add_fusion.refs_0_, f32[200,128]{1,0:T(8,128)S(1)} %get-tuple-element.76.refs_1_, f32[200,128]{1,0:T(8,128)S(1)} %collective-permute-done.13.refs_2_, f32[200,128]{1,0:T(8,128)S(1)} %collective-permute-done.14.refs_3_, f32[200,128]{1,0:T(8,128)S(1)} %collective-permute-done.15.refs_4_, ...), custom_call_target="tpu_custom_call" | custom-call | tf_op jit(solution)/shard_map/gather/pallas_call | solution.py:413
  102.8 0.8 leave.1
  (32 shorter events, 0.2 us)
Async XLA Ops:
  0.6 1.0 copy-start.4
  1.6 21.1 %copy-start = (bf16[256,256]{1,0:T(8,128)(2,1)S(1)}, bf16[256,256]{1,0:T(8,128)(2,1)}, u32[]{:S(2)}) copy-start(bf16[256,256]{1,0:T(8,128)(2,1)} %constant.68.clone.refs_4_.refs_5_.refs_2_) | copy-start | bytes 393220
  1.6 21.0 %copy-start.3 = (bf16[80,240]{1,0:T(8,128)(2,1)S(1)}, bf16[80,240]{1,0:T(8,128)(2,1)}, u32[]{:S(2)}) copy-start(bf16[80,240]{1,0:T(8,128)(2,1)} %constant.69.clone.refs_5_.refs_6_.refs_3_) | copy-start | bytes 115204
  1.7 12.0 %collective-permute-start = (f32[736,128]{1,0:T(8,128)S(1)}, f32[736,128]{1,0:T(8,128)S(1)}, u32[]{:S(2)}, u32[]{:S(2)}) collective-permute-start(f32[736,128]{1,0:T(8,128)S(1)} %enter.1.refs_1_.refs_7_.own), channel_id=1, source_target_pairs={{0,4},{4,0},{8,12},{12,8},{16,20},{20,16},{24,28},{28,24},{32,36},... | collective-permute-start | bytes 1130504 | tf_op jit(solution)/shard_map/ppermute | solution.py:466
  4.2 18.4 %collective-permute-start.1 = (f32[736,128]{1,0:T(8,128)S(1)}, f32[736,128]{1,0:T(8,128)S(1)}, u32[]{:S(2)}, u32[]{:S(2)}) collective-permute-start(f32[736,128]{1,0:T(8,128)S(1)} %enter.1.refs_1_.refs_7_.own), channel_id=1, source_target_pairs={{0,252},{4,8},{8,4},{12,16},{16,12},{20,24},{24,20},{28,32},{32,28... | collective-permute-start | bytes 1130504 | tf_op jit(solution)/shard_map/ppermute | solution.py:466
  13.7 16.4 %collective-permute-start.2 = (f32[736,128]{1,0:T(8,128)S(1)}, f32[736,128]{1,0:T(8,128)S(1)}, u32[]{:S(2)}, u32[]{:S(2)}) collective-permute-start(f32[736,128]{1,0:T(8,128)S(1)} %collective-permute-done.refs_2_.refs_1_.refs_8_.refs_7_), channel_id=1, source_target_pairs={{0,252},{4,8},{8,4},{12,16},{16,12},{20,24},{24,20},{28,32},{32,28... | collective-permute-start | bytes 1130504 | tf_op jit(solution)/shard_map/ppermute | solution.py:466
  22.6 8.4 %collective-permute-start.3 = (f32[736,128]{1,0:T(8,128)S(1)}, f32[736,128]{1,0:T(8,128)S(1)}, u32[]{:S(2)}, u32[]{:S(2)}) collective-permute-start(f32[736,128]{1,0:T(8,128)S(1)} %collective-permute-done.1.refs_3_.refs_2_.refs_9_.refs_8_), channel_id=1, source_target_pairs={{0,4},{4,0},{8,12},{12,8},{16,20},{20,16},{24,28},{28,24},{32,36},... | collective-permute-start | bytes 1130504 | tf_op jit(solution)/shard_map/ppermute | solution.py:466
  25.8 12.8 %collective-permute-start.4 = (f32[400,128]{1,0:T(8,128)S(1)}, f32[400,128]{1,0:T(8,128)S(1)}, u32[]{:S(2)}, u32[]{:S(2)}) collective-permute-start(f32[400,128]{1,0:T(8,128)S(1)} %get-tuple-element.53), channel_id=1, source_target_pairs={{0,2},{1,3},{2,0},{3,1},{4,6},{5,7},{6,4},{7,5},{8,10},{9,11},{10,... | collective-permute-start | bytes 614408 | tf_op jit(solution)/shard_map/ppermute | solution.py:452
  26.3 13.1 %collective-permute-start.5 = (f32[400,128]{1,0:T(8,128)S(1)}, f32[400,128]{1,0:T(8,128)S(1)}, u32[]{:S(2)}, u32[]{:S(2)}) collective-permute-start(f32[400,128]{1,0:T(8,128)S(1)} %get-tuple-element.54), channel_id=1, source_target_pairs={{0,3},{1,2},{2,1},{3,0},{4,7},{5,6},{6,5},{7,4},{8,11},{9,10},{10,... | collective-permute-start | bytes 614408 | tf_op jit(solution)/shard_map/ppermute | solution.py:452
  29.5 10.0 %collective-permute-start.6 = (f32[400,128]{1,0:T(8,128)S(1)}, f32[400,128]{1,0:T(8,128)S(1)}, u32[]{:S(2)}, u32[]{:S(2)}) collective-permute-start(f32[400,128]{1,0:T(8,128)S(1)} %get-tuple-element.55), channel_id=1, source_target_pairs={{0,1},{1,0},{2,3},{3,2},{4,5},{5,4},{6,7},{7,6},{8,9},{9,8},{10,11... | collective-permute-start | bytes 614408 | tf_op jit(solution)/shard_map/ppermute | solution.py:452
  34.2 10.9 %collective-permute-start.16 = (f32[400,128]{1,0:T(8,128)S(1)}, f32[400,128]{1,0:T(8,128)S(1)}, u32[]{:S(2)}, u32[]{:S(2)}) collective-permute-start(f32[400,128]{1,0:T(8,128)S(1)} %get-tuple-element.59), channel_id=1, source_target_pairs={{0,2},{1,3},{2,0},{3,1},{4,6},{5,7},{6,4},{7,5},{8,10},{9,11},{10,... | collective-permute-start | bytes 614408 | tf_op jit(solution)/shard_map/ppermute | solution.py:452
  34.7 14.1 %collective-permute-start.17 = (f32[400,128]{1,0:T(8,128)S(1)}, f32[400,128]{1,0:T(8,128)S(1)}, u32[]{:S(2)}, u32[]{:S(2)}) collective-permute-start(f32[400,128]{1,0:T(8,128)S(1)} %get-tuple-element.60), channel_id=1, source_target_pairs={{0,3},{1,2},{2,1},{3,0},{4,7},{5,6},{6,5},{7,4},{8,11},{9,10},{10,... | collective-permute-start | bytes 614408 | tf_op jit(solution)/shard_map/ppermute | solution.py:452
  38.7 10.1 %collective-permute-start.18 = (f32[400,128]{1,0:T(8,128)S(1)}, f32[400,128]{1,0:T(8,128)S(1)}, u32[]{:S(2)}, u32[]{:S(2)}) collective-permute-start(f32[400,128]{1,0:T(8,128)S(1)} %get-tuple-element.61), channel_id=1, source_target_pairs={{0,1},{1,0},{2,3},{3,2},{4,5},{5,4},{6,7},{7,6},{8,9},{9,8},{10,11... | collective-permute-start | bytes 614408 | tf_op jit(solution)/shard_map/ppermute | solution.py:452
  38.7 0.9 copy-start.1
  38.7 1.0 copy-start.2
  40.9 10.1 %collective-permute-start.7 = (f32[400,128]{1,0:T(8,128)S(1)}, f32[400,128]{1,0:T(8,128)S(1)}, u32[]{:S(2)}, u32[]{:S(2)}) collective-permute-start(f32[400,128]{1,0:T(8,128)S(1)} %get-tuple-element.68), channel_id=1, source_target_pairs={{0,2},{1,3},{2,0},{3,1},{4,6},{5,7},{6,4},{7,5},{8,10},{9,11},{10,... | collective-permute-start | bytes 614408 | tf_op jit(solution)/shard_map/ppermute | solution.py:452
  41.4 16.1 %collective-permute-start.8 = (f32[400,128]{1,0:T(8,128)S(1)}, f32[400,128]{1,0:T(8,128)S(1)}, u32[]{:S(2)}, u32[]{:S(2)}) collective-permute-start(f32[400,128]{1,0:T(8,128)S(1)} %get-tuple-element.69), channel_id=1, source_target_pairs={{0,3},{1,2},{2,1},{3,0},{4,7},{5,6},{6,5},{7,4},{8,11},{9,10},{10,... | collective-permute-start | bytes 614408 | tf_op jit(solution)/shard_map/ppermute | solution.py:452
  45.1 12.4 %collective-permute-start.9 = (f32[400,128]{1,0:T(8,128)S(1)}, f32[400,128]{1,0:T(8,128)S(1)}, u32[]{:S(2)}, u32[]{:S(2)}) collective-permute-start(f32[400,128]{1,0:T(8,128)S(1)} %get-tuple-element.70), channel_id=1, source_target_pairs={{0,1},{1,0},{2,3},{3,2},{4,5},{5,4},{6,7},{7,6},{8,9},{9,8},{10,11... | collective-permute-start | bytes 614408 | tf_op jit(solution)/shard_map/ppermute | solution.py:452
  50.0 11.5 %collective-permute-start.19 = (f32[400,128]{1,0:T(8,128)S(1)}, f32[400,128]{1,0:T(8,128)S(1)}, u32[]{:S(2)}, u32[]{:S(2)}) collective-permute-start(f32[400,128]{1,0:T(8,128)S(1)} %get-tuple-element.85), channel_id=1, source_target_pairs={{0,2},{1,3},{2,0},{3,1},{4,6},{5,7},{6,4},{7,5},{8,10},{9,11},{10,... | collective-permute-start | bytes 614408 | tf_op jit(solution)/shard_map/ppermute | solution.py:452
  50.5 16.1 %collective-permute-start.20 = (f32[400,128]{1,0:T(8,128)S(1)}, f32[400,128]{1,0:T(8,128)S(1)}, u32[]{:S(2)}, u32[]{:S(2)}) collective-permute-start(f32[400,128]{1,0:T(8,128)S(1)} %get-tuple-element.86), channel_id=1, source_target_pairs={{0,3},{1,2},{2,1},{3,0},{4,7},{5,6},{6,5},{7,4},{8,11},{9,10},{10,... | collective-permute-start | bytes 614408 | tf_op jit(solution)/shard_map/ppermute | solution.py:452
  51.1 15.5 %collective-permute-start.21 = (f32[400,128]{1,0:T(8,128)S(1)}, f32[400,128]{1,0:T(8,128)S(1)}, u32[]{:S(2)}, u32[]{:S(2)}) collective-permute-start(f32[400,128]{1,0:T(8,128)S(1)} %get-tuple-element.87), channel_id=1, source_target_pairs={{0,1},{1,0},{2,3},{3,2},{4,5},{5,4},{6,7},{7,6},{8,9},{9,8},{10,11... | collective-permute-start | bytes 614408 | tf_op jit(solution)/shard_map/ppermute | solution.py:452
  61.0 9.2 %collective-permute-start.10 = (f32[200,128]{1,0:T(8,128)S(1)}, f32[200,128]{1,0:T(8,128)S(1)}, u32[]{:S(2)}, u32[]{:S(2)}) collective-permute-start(f32[200,128]{1,0:T(8,128)S(1)} %get-tuple-element.73), channel_id=1, source_target_pairs={{0,2},{1,3},{2,0},{3,1},{4,6},{5,7},{6,4},{7,5},{8,10},{9,11},{10,... | collective-permute-start | bytes 307208 | tf_op jit(solution)/shard_map/ppermute | solution.py:452
  61.4 8.8 %collective-permute-start.11 = (f32[200,128]{1,0:T(8,128)S(1)}, f32[200,128]{1,0:T(8,128)S(1)}, u32[]{:S(2)}, u32[]{:S(2)}) collective-permute-start(f32[200,128]{1,0:T(8,128)S(1)} %get-tuple-element.74), channel_id=1, source_target_pairs={{0,3},{1,2},{2,1},{3,0},{4,7},{5,6},{6,5},{7,4},{8,11},{9,10},{10,... | collective-permute-start | bytes 307208 | tf_op jit(solution)/shard_map/ppermute | solution.py:452
  61.6 8.7 %collective-permute-start.12 = (f32[200,128]{1,0:T(8,128)S(1)}, f32[200,128]{1,0:T(8,128)S(1)}, u32[]{:S(2)}, u32[]{:S(2)}) collective-permute-start(f32[200,128]{1,0:T(8,128)S(1)} %get-tuple-element.75), channel_id=1, source_target_pairs={{0,1},{1,0},{2,3},{3,2},{4,5},{5,4},{6,7},{7,6},{8,9},{9,8},{10,11... | collective-permute-start | bytes 307208 | tf_op jit(solution)/shard_map/ppermute | solution.py:452
  70.2 10.1 %collective-permute-start.22 = (f32[736,128]{1,0:T(8,128)S(1)}, f32[736,128]{1,0:T(8,128)S(1)}, u32[]{:S(2)}, u32[]{:S(2)}) collective-permute-start(f32[736,128]{1,0:T(8,128)S(1)} %get-tuple-element.95), channel_id=1, source_target_pairs={{0,4},{4,0},{8,12},{12,8},{16,20},{20,16},{24,28},{28,24},{32,36},... | collective-permute-start | bytes 1130504 | tf_op jit(solution)/shard_map/ppermute | solution.py:466
  70.3 17.3 %collective-permute-start.24 = (f32[736,128]{1,0:T(8,128)S(1)}, f32[736,128]{1,0:T(8,128)S(1)}, u32[]{:S(2)}, u32[]{:S(2)}) collective-permute-start(f32[736,128]{1,0:T(8,128)S(1)} %get-tuple-element.97), channel_id=1, source_target_pairs={{0,252},{4,8},{8,4},{12,16},{16,12},{20,24},{24,20},{28,32},{32,28... | collective-permute-start | bytes 1130504 | tf_op jit(solution)/shard_map/ppermute | solution.py:466
  80.4 22.3 %collective-permute-start.23 = (f32[736,128]{1,0:T(8,128)S(1)}, f32[736,128]{1,0:T(8,128)S(1)}, u32[]{:S(2)}, u32[]{:S(2)}) collective-permute-start(f32[736,128]{1,0:T(8,128)S(1)} %add.68), channel_id=1, source_target_pairs={{0,252},{4,8},{8,4},{12,16},{16,12},{20,24},{24,20},{28,32},{32,28... | collective-permute-start | bytes 1130504 | tf_op jit(solution)/shard_map/ppermute | solution.py:466
  87.7 15.2 %collective-permute-start.25 = (f32[736,128]{1,0:T(8,128)S(1)}, f32[736,128]{1,0:T(8,128)S(1)}, u32[]{:S(2)}, u32[]{:S(2)}) collective-permute-start(f32[736,128]{1,0:T(8,128)S(1)} %add.70), channel_id=1, source_target_pairs={{0,4},{4,0},{8,12},{12,8},{16,20},{20,16},{24,28},{28,24},{32,36},... | collective-permute-start | bytes 1130504 | tf_op jit(solution)/shard_map/ppermute | solution.py:466
  87.8 10.8 %collective-permute-start.13 = (f32[200,128]{1,0:T(8,128)S(1)}, f32[200,128]{1,0:T(8,128)S(1)}, u32[]{:S(2)}, u32[]{:S(2)}) collective-permute-start(f32[200,128]{1,0:T(8,128)S(1)} %get-tuple-element.77), channel_id=1, source_target_pairs={{0,2},{1,3},{2,0},{3,1},{4,6},{5,7},{6,4},{7,5},{8,10},{9,11},{10,... | collective-permute-start | bytes 307208 | tf_op jit(solution)/shard_map/ppermute | solution.py:452
  87.9 12.9 %collective-permute-start.14 = (f32[200,128]{1,0:T(8,128)S(1)}, f32[200,128]{1,0:T(8,128)S(1)}, u32[]{:S(2)}, u32[]{:S(2)}) collective-permute-start(f32[200,128]{1,0:T(8,128)S(1)} %get-tuple-element.78), channel_id=1, source_target_pairs={{0,3},{1,2},{2,1},{3,0},{4,7},{5,6},{6,5},{7,4},{8,11},{9,10},{10,... | collective-permute-start | bytes 307208 | tf_op jit(solution)/shard_map/ppermute | solution.py:452
  91.0 9.7 %collective-permute-start.15 = (f32[200,128]{1,0:T(8,128)S(1)}, f32[200,128]{1,0:T(8,128)S(1)}, u32[]{:S(2)}, u32[]{:S(2)}) collective-permute-start(f32[200,128]{1,0:T(8,128)S(1)} %get-tuple-element.79), channel_id=1, source_target_pairs={{0,1},{1,0},{2,3},{3,2},{4,5},{5,4},{6,7},{7,6},{8,9},{9,8},{10,11... | collective-permute-start | bytes 307208 | tf_op jit(solution)/shard_map/ppermute | solution.py:452

commit v4 on v3

--- a/solution.py
+++ b/solution.py
@@ -501,9 +501,9 @@
     one = swapped(after(one, none), 1, 0)
     two = swapped(two, 1, 1)
     none = solve_pencils(none, 1, tables)
+    none = exchanged(after(none, one))
     four = swapped(one + four, 1, 1)
     three = swapped(two + after(three, none), 1, 0)
-    none = exchanged(none)
     kept = kept + four
     (self_share,) = gather_shares(none, 1, {0: own}, {0: [(0, 0)]}, tables)
     residual, intersection = leave(own, self_share, kept, three)

time: 104 us -> 102 us (0.981)
  waiting for transfers between devices: 24.9 us -> 23.1 us
    ppermute x18, waiting for transfers between devices: 21.5 us -> 12 us  [exchanged(): received.append(lax.ppermute(chunk, 'grid', pairs))]
    ppermute x8, waiting for transfers between devices: 3.39 us -> 11.1 us  [swapped(): return lax.ppermute(value, 'orb', pairs)]
    ppermute x18, starting transfers between devices: 19.1 us -> 17.7 us  [exchanged(): received.append(lax.ppermute(chunk, 'grid', pairs))]
  transfers between devices with their start and end apart: 26 -> 26, of which waited for: 10 -> 11; matrix products, arithmetic and copies ran while one was open for 0% -> 0% of each run, Pallas kernels for 20% -> 20%
where the time goes in v4:
time: 102 us; the launch traced here: 101 us
  starting transfers between devices  54.3 us (53%)
  waiting for transfers between devices  23.1 us (23%)
  Pallas kernels  21.7 us (21%)
  local copies, waits for them, and re-layouts  1.23 us (1%)
    ppermute x8, starting transfers between devices, swapped(): return lax.ppermute(value, 'orb', pairs)  36.5 us
    ppermute x18, starting transfers between devices, exchanged(): received.append(lax.ppermute(chunk, 'grid', pairs))  17.7 us
    ppermute x18, waiting for transfers between devices, exchanged(): received.append(lax.ppermute(chunk, 'grid', pairs))  12 us
    ppermute x8, waiting for transfers between devices, swapped(): return lax.ppermute(value, 'orb', pairs)  11.1 us
    pallas_call x3, Pallas kernels, gather_shares(): pl.pallas_call(lambda *refs: gather_kernel(count, parts, list(orbitals),...  9.04 us
    pallas_call x3, Pallas kernels, spread_pairs(): pl.pallas_call(lambda *refs: spread_kernel(pairs, list(orbitals), *refs),...  8.18 us
    pallas_call x3, Pallas kernels, solve_pencils(): pl.pallas_call(lambda *refs: pencil_kernel(count, parts, *refs), out_shap...  3.58 us
  transfers between devices with their start and end apart: 26, of which 11 were waited for; matrix products, arithmetic and copies ran while one was open for 0% of the time, Pallas kernels for 20%

profile of v4, /device:TPU:1, one launch (start us, length us, event | category | flops | bytes accessed | tf_op | source)
XLA Modules:
  0.0 101.5 jit_solution(4844441274754163767)
XLA Ops:
  0.6 1.0 copy-done.4
  1.7 2.6 %collective-permute-start = (f32[736,128]{1,0:T(8,128)S(1)}, f32[736,128]{1,0:T(8,128)S(1)}, u32[]{:S(2)}, u32[]{:S(2)}) collective-permute-start(f32[736,128]{1,0:T(8,128)S(1)} %enter.1.refs_1_.refs_7_.own), channel_id=1, source_target_pairs={{0,4},{4,0},{8,12},{12,8},{16,20},{20,16},{24,28},{28,24},{32,36},... | collective-permute-start | bytes 1130504 | tf_op jit(solution)/shard_map/ppermute | solution.py:466
  4.2 9.5 %collective-permute-start.1 = (f32[736,128]{1,0:T(8,128)S(1)}, f32[736,128]{1,0:T(8,128)S(1)}, u32[]{:S(2)}, u32[]{:S(2)}) collective-permute-start(f32[736,128]{1,0:T(8,128)S(1)} %enter.1.refs_1_.refs_7_.own), channel_id=1, source_target_pairs={{0,252},{4,8},{8,4},{12,16},{16,12},{20,24},{24,20},{28,32},{32,28... | collective-permute-start | bytes 1130504 | tf_op jit(solution)/shard_map/ppermute | solution.py:466
  13.7 8.9 %collective-permute-start.2 = (f32[736,128]{1,0:T(8,128)S(1)}, f32[736,128]{1,0:T(8,128)S(1)}, u32[]{:S(2)}, u32[]{:S(2)}) collective-permute-start(f32[736,128]{1,0:T(8,128)S(1)} %collective-permute-done.refs_2_.refs_1_.refs_8_.refs_7_), channel_id=1, source_target_pairs={{0,252},{4,8},{8,4},{12,16},{16,12},{20,24},{24,20},{28,32},{32,28... | collective-permute-start | bytes 1130504 | tf_op jit(solution)/shard_map/ppermute | solution.py:466
  22.7 3.1 %spread.3 = (f32[400,128]{1,0:T(8,128)S(1)}, f32[400,128]{1,0:T(8,128)S(1)}, f32[400,128]{1,0:T(8,128)S(1)}, f32[400,128]{1,0:T(8,128)S(1)}) custom-call(s32[2]{0:T(128)S(1)} %pad_add_fusion.refs_0_, f32[736,128]{1,0:T(8,128)S(1)} %enter.1.refs_1_.refs_7_.own, f32[736,128]{1,0:T(8,128)S(1)} %collective-permute-done.refs_2_.refs_1_.refs_8_.refs_7_, ...), custom_call_target="tpu_custom_call" | custom-call | tf_op jit(solution)/shard_map/spread/pallas_call | solution.py:388
  25.8 0.5 collective-permute-start.4
  26.3 3.1 %collective-permute-start.5 = (f32[400,128]{1,0:T(8,128)S(1)}, f32[400,128]{1,0:T(8,128)S(1)}, u32[]{:S(2)}, u32[]{:S(2)}) collective-permute-start(f32[400,128]{1,0:T(8,128)S(1)} %get-tuple-element.58), channel_id=1, source_target_pairs={{0,3},{1,2},{2,1},{3,0},{4,7},{5,6},{6,5},{7,4},{8,11},{9,10},{10,... | collective-permute-start | bytes 614408 | tf_op jit(solution)/shard_map/ppermute | solution.py:452
  29.5 0.7 collective-permute-done.2.refs_3_.refs_9_
  30.1 0.9 collective-permute-done.3.refs_4_.refs_10_
  31.0 3.1 %spread.4 = (f32[400,128]{1,0:T(8,128)S(1)}, f32[400,128]{1,0:T(8,128)S(1)}, f32[400,128]{1,0:T(8,128)S(1)}, f32[400,128]{1,0:T(8,128)S(1)}) custom-call(s32[2]{0:T(128)S(1)} %pad_add_fusion.refs_0_, f32[736,128]{1,0:T(8,128)S(1)} %collective-permute-done.refs_2_.refs_1_.refs_8_.refs_7_, ...), custom_call_target="tpu_custom_call" | custom-call | tf_op jit(solution)/shard_map/spread/pallas_call | solution.py:388
  34.2 0.5 collective-permute-start.13
  34.7 4.0 %collective-permute-start.14 = (f32[400,128]{1,0:T(8,128)S(1)}, f32[400,128]{1,0:T(8,128)S(1)}, u32[]{:S(2)}, u32[]{:S(2)}) collective-permute-start(f32[400,128]{1,0:T(8,128)S(1)} %get-tuple-element.64), channel_id=1, source_target_pairs={{0,3},{1,2},{2,1},{3,0},{4,7},{5,6},{6,5},{7,4},{8,11},{9,10},{10,... | collective-permute-start | bytes 614408 | tf_op jit(solution)/shard_map/ppermute | solution.py:452
  38.7 0.2 fusion.refs_5_
  38.9 0.5 collective-permute-done.5.refs_3_
  39.5 0.1 copy-done.1
  39.6 0.1 copy-done.2
  39.7 1.3 %pencils.3 = (f32[400,128]{1,0:T(8,128)S(1)}, f32[400,128]{1,0:T(8,128)S(1)}, f32[400,128]{1,0:T(8,128)S(1)}, f32[400,128]{1,0:T(8,128)S(1)}) custom-call(s32[2]{0:T(128)S(1)} %pad_add_fusion.refs_0_, f32[400,128]{1,0:T(8,128)S(1)} %get-tuple-element.56.refs_1_, f32[400,128]{1,0:T(8,128)S(1)} %collective-permute-done.4.refs_2_, ...), custom_call_target="tpu_custom_call" | custom-call | tf_op jit(solution)/shard_map/pencils/pallas_call | solution.py:401
  40.9 0.5 collective-permute-start.7
  41.4 1.7 %collective-permute-start.8 = (f32[400,128]{1,0:T(8,128)S(1)}, f32[400,128]{1,0:T(8,128)S(1)}, u32[]{:S(2)}, u32[]{:S(2)}) collective-permute-start(f32[400,128]{1,0:T(8,128)S(1)} %get-tuple-element.73), channel_id=1, source_target_pairs={{0,3},{1,2},{2,1},{3,0},{4,7},{5,6},{6,5},{7,4},{8,11},{9,10},{10,... | collective-permute-start | bytes 614408 | tf_op jit(solution)/shard_map/ppermute | solution.py:452
  43.2 1.9 %spread.5 = (f32[200,128]{1,0:T(8,128)S(1)}, f32[200,128]{1,0:T(8,128)S(1)}, f32[200,128]{1,0:T(8,128)S(1)}, f32[200,128]{1,0:T(8,128)S(1)}) custom-call(s32[2]{0:T(128)S(1)} %pad_add_fusion.refs_0_, f32[736,128]{1,0:T(8,128)S(1)} %enter.1.refs_1_.refs_7_.own, bf16[256,256]{1,0:T(8,128)(2,1)S(1)} %copy-done, bf16[80,240]{1,0:T(8,128)(2,1)S(1)} %copy-done.3), custom_call_target="tpu_custom_call" | custom-call | tf_op jit(solution)/shard_map/spread/pallas_call | solution.py:388
  45.1 0.3 collective-permute-start.9
  45.4 3.3 %collective-permute-done.14.refs_3_ = f32[400,128]{1,0:T(8,128)S(1)} collective-permute-done((f32[400,128]{1,0:T(8,128)S(1)}, f32[400,128]{1,0:T(8,128)S(1)}, u32[]{:S(2)}, u32[]{:S(2)}) %collective-permute-start.14) | collective-permute-done | bytes 204832 | tf_op jit(solution)/shard_map/ppermute | solution.py:452
  48.7 1.3 %pencils.5 = (f32[400,128]{1,0:T(8,128)S(1)}, f32[400,128]{1,0:T(8,128)S(1)}, f32[400,128]{1,0:T(8,128)S(1)}, f32[400,128]{1,0:T(8,128)S(1)}) custom-call(s32[2]{0:T(128)S(1)} %pad_add_fusion.refs_0_, f32[400,128]{1,0:T(8,128)S(1)} %get-tuple-element.84.refs_1_, f32[400,128]{1,0:T(8,128)S(1)} %collective-permute-done.13.refs_2_, ...), custom_call_target="tpu_custom_call" | custom-call | tf_op jit(solution)/shard_map/pencils/pallas_call | solution.py:401
  50.0 0.5 collective-permute-start.16
  50.5 0.1 collective-permute-start.17
  50.6 0.5 collective-permute-done.7.refs_2_
  51.1 2.7 %collective-permute-start.18 = (f32[400,128]{1,0:T(8,128)S(1)}, f32[400,128]{1,0:T(8,128)S(1)}, u32[]{:S(2)}, u32[]{:S(2)}) collective-permute-start(f32[400,128]{1,0:T(8,128)S(1)} %get-tuple-element.91), channel_id=1, source_target_pairs={{0,1},{1,0},{2,3},{3,2},{4,5},{5,4},{6,7},{7,6},{8,9},{9,8},{10,11... | collective-permute-start | bytes 614408 | tf_op jit(solution)/shard_map/ppermute | solution.py:452
  53.8 3.7 %collective-permute-done.8.refs_3_ = f32[400,128]{1,0:T(8,128)S(1)} collective-permute-done((f32[400,128]{1,0:T(8,128)S(1)}, f32[400,128]{1,0:T(8,128)S(1)}, u32[]{:S(2)}, u32[]{:S(2)}) %collective-permute-start.8) | collective-permute-done | bytes 204832 | tf_op jit(solution)/shard_map/ppermute | solution.py:452
  57.5 3.4 %gather.3 = (f32[736,128]{1,0:T(8,128)S(1)}, f32[736,128]{1,0:T(8,128)S(1)}, f32[736,128]{1,0:T(8,128)S(1)}) custom-call(s32[2]{0:T(128)S(1)} %pad_add_fusion.refs_0_, f32[400,128]{1,0:T(8,128)S(1)} %get-tuple-element.71.refs_1_, f32[400,128]{1,0:T(8,128)S(1)} %collective-permute-done.7.refs_2_, f32[400,128]{1,0:T(8,128)S(1)} %collective-permute-done.8.refs_3_, ...), custom_call_target="tpu_custom_call" | custom-call | tf_op jit(solution)/shard_map/gather/pallas_call | solution.py:413
  61.0 0.5 collective-permute-start.10
  61.4 0.1 collective-permute-start.11
  61.6 1.3 %collective-permute-start.12 = (f32[200,128]{1,0:T(8,128)S(1)}, f32[200,128]{1,0:T(8,128)S(1)}, u32[]{:S(2)}, u32[]{:S(2)}) collective-permute-start(f32[200,128]{1,0:T(8,128)S(1)} %get-tuple-element.79), channel_id=1, source_target_pairs={{0,1},{1,0},{2,3},{3,2},{4,5},{5,4},{6,7},{7,6},{8,9},{9,8},{10,11... | collective-permute-start | bytes 307208 | tf_op jit(solution)/shard_map/ppermute | solution.py:452
  62.9 3.7 %collective-permute-done.17.refs_3_ = f32[400,128]{1,0:T(8,128)S(1)} collective-permute-done((f32[400,128]{1,0:T(8,128)S(1)}, f32[400,128]{1,0:T(8,128)S(1)}, u32[]{:S(2)}, u32[]{:S(2)}) %collective-permute-start.17) | collective-permute-done | bytes 204832 | tf_op jit(solution)/shard_map/ppermute | solution.py:452
  66.6 3.6 %gather.4 = (f32[736,128]{1,0:T(8,128)S(1)}, f32[736,128]{1,0:T(8,128)S(1)}, f32[736,128]{1,0:T(8,128)S(1)}, f32[736,128]{1,0:T(8,128)S(1)}) custom-call(s32[2]{0:T(128)S(1)} %pad_add_fusion.refs_0_, f32[400,128]{1,0:T(8,128)S(1)} %get-tuple-element.92.refs_1_, f32[400,128]{1,0:T(8,128)S(1)} %collective-permute-done.16.refs_2_, ...), custom_call_target="tpu_custom_call" | custom-call | tf_op jit(solution)/shard_map/gather/pallas_call | solution.py:413
  70.2 0.1 collective-permute-start.19
  70.3 7.2 %collective-permute-start.24 = (f32[736,128]{1,0:T(8,128)S(1)}, f32[736,128]{1,0:T(8,128)S(1)}, u32[]{:S(2)}, u32[]{:S(2)}) collective-permute-start(f32[736,128]{1,0:T(8,128)S(1)} %get-tuple-element.105), channel_id=1, source_target_pairs={{0,252},{4,8},{8,4},{12,16},{16,12},{20,24},{24,20},{28,32},{32,28... | collective-permute-start | bytes 1130504 | tf_op jit(solution)/shard_map/ppermute | solution.py:466
  77.5 1.0 %pencils.4 = (f32[200,128]{1,0:T(8,128)S(1)}, f32[200,128]{1,0:T(8,128)S(1)}, f32[200,128]{1,0:T(8,128)S(1)}, f32[200,128]{1,0:T(8,128)S(1)}) custom-call(s32[2]{0:T(128)S(1)} %pad_add_fusion.refs_0_, f32[200,128]{1,0:T(8,128)S(1)} %get-tuple-element.76.refs_1_, f32[200,128]{1,0:T(8,128)S(1)} %collective-permute-done.10.refs_2_, ...), custom_call_target="tpu_custom_call" | custom-call | tf_op jit(solution)/shard_map/pencils/pallas_call | solution.py:401
  78.6 1.8 %collective-permute-done.19 = f32[736,128]{1,0:T(8,128)S(1)} collective-permute-done((f32[736,128]{1,0:T(8,128)S(1)}, f32[736,128]{1,0:T(8,128)S(1)}, u32[]{:S(2)}, u32[]{:S(2)}) %collective-permute-start.19) | collective-permute-done | bytes 376864 | tf_op jit(solution)/shard_map/ppermute | solution.py:466
  80.4 0.9 collective-permute-start.20
  81.2 0.4 collective-permute-start.21
  81.7 0.5 collective-permute-start.22
  82.3 8.2 %collective-permute-start.23 = (f32[736,128]{1,0:T(8,128)S(1)}, f32[736,128]{1,0:T(8,128)S(1)}, u32[]{:S(2)}, u32[]{:S(2)}) collective-permute-start(f32[736,128]{1,0:T(8,128)S(1)} %add.68), channel_id=1, source_target_pairs={{0,252},{4,8},{8,4},{12,16},{16,12},{20,24},{24,20},{28,32},{32,28... | collective-permute-start | bytes 1130504 | tf_op jit(solution)/shard_map/ppermute | solution.py:466
  90.5 0.2 collective-permute-done.21.refs_3_
  90.8 0.1 collective-permute-start.25
  90.9 2.0 %gather.5.refs_0_ = f32[736,128]{1,0:T(8,128)S(1)} custom-call(s32[2]{0:T(128)S(1)} %pad_add_fusion.refs_0_, f32[200,128]{1,0:T(8,128)S(1)} %get-tuple-element.100.refs_1_, f32[200,128]{1,0:T(8,128)S(1)} %collective-permute-done.20.refs_2_, f32[200,128]{1,0:T(8,128)S(1)} %collective-permute-done.21.refs_3_, f32[200,128]{1,0:T(8,128)S(1)} %collective-permute-done.22.refs_4_, ...), custom_call_target="tpu_custom_call" | custom-call | tf_op jit(solution)/shard_map/gather/pallas_call | solution.py:413
  92.9 6.2 %collective-permute-done.23 = f32[736,128]{1,0:T(8,128)S(1)} collective-permute-done((f32[736,128]{1,0:T(8,128)S(1)}, f32[736,128]{1,0:T(8,128)S(1)}, u32[]{:S(2)}, u32[]{:S(2)}) %collective-permute-start.23) | collective-permute-done | bytes 376864 | tf_op jit(solution)/shard_map/ppermute | solution.py:466
  99.2 1.5 %collective-permute-done.25.refs_2_ = f32[736,128]{1,0:T(8,128)S(1)} collective-permute-done((f32[736,128]{1,0:T(8,128)S(1)}, f32[736,128]{1,0:T(8,128)S(1)}, u32[]{:S(2)}, u32[]{:S(2)}) %collective-permute-start.25) | collective-permute-done | bytes 376864 | tf_op jit(solution)/shard_map/ppermute | solution.py:466
  100.6 0.8 leave.1
  (32 shorter events, 0.3 us)
Async XLA Ops:
  0.6 1.0 copy-start.4
  1.6 21.1 %copy-start = (bf16[256,256]{1,0:T(8,128)(2,1)S(1)}, bf16[256,256]{1,0:T(8,128)(2,1)}, u32[]{:S(2)}) copy-start(bf16[256,256]{1,0:T(8,128)(2,1)} %constant.68.clone.refs_4_.refs_5_.refs_2_) | copy-start | bytes 393220
  1.6 21.0 %copy-start.3 = (bf16[80,240]{1,0:T(8,128)(2,1)S(1)}, bf16[80,240]{1,0:T(8,128)(2,1)}, u32[]{:S(2)}) copy-start(bf16[80,240]{1,0:T(8,128)(2,1)} %constant.69.clone.refs_5_.refs_6_.refs_3_) | copy-start | bytes 115204
  1.7 12.0 %collective-permute-start = (f32[736,128]{1,0:T(8,128)S(1)}, f32[736,128]{1,0:T(8,128)S(1)}, u32[]{:S(2)}, u32[]{:S(2)}) collective-permute-start(f32[736,128]{1,0:T(8,128)S(1)} %enter.1.refs_1_.refs_7_.own), channel_id=1, source_target_pairs={{0,4},{4,0},{8,12},{12,8},{16,20},{20,16},{24,28},{28,24},{32,36},... | collective-permute-start | bytes 1130504 | tf_op jit(solution)/shard_map/ppermute | solution.py:466
  4.2 18.4 %collective-permute-start.1 = (f32[736,128]{1,0:T(8,128)S(1)}, f32[736,128]{1,0:T(8,128)S(1)}, u32[]{:S(2)}, u32[]{:S(2)}) collective-permute-start(f32[736,128]{1,0:T(8,128)S(1)} %enter.1.refs_1_.refs_7_.own), channel_id=1, source_target_pairs={{0,252},{4,8},{8,4},{12,16},{16,12},{20,24},{24,20},{28,32},{32,28... | collective-permute-start | bytes 1130504 | tf_op jit(solution)/shard_map/ppermute | solution.py:466
  13.7 16.4 %collective-permute-start.2 = (f32[736,128]{1,0:T(8,128)S(1)}, f32[736,128]{1,0:T(8,128)S(1)}, u32[]{:S(2)}, u32[]{:S(2)}) collective-permute-start(f32[736,128]{1,0:T(8,128)S(1)} %collective-permute-done.refs_2_.refs_1_.refs_8_.refs_7_), channel_id=1, source_target_pairs={{0,252},{4,8},{8,4},{12,16},{16,12},{20,24},{24,20},{28,32},{32,28... | collective-permute-start | bytes 1130504 | tf_op jit(solution)/shard_map/ppermute | solution.py:466
  22.6 8.4 %collective-permute-start.3 = (f32[736,128]{1,0:T(8,128)S(1)}, f32[736,128]{1,0:T(8,128)S(1)}, u32[]{:S(2)}, u32[]{:S(2)}) collective-permute-start(f32[736,128]{1,0:T(8,128)S(1)} %collective-permute-done.1.refs_3_.refs_2_.refs_9_.refs_8_), channel_id=1, source_target_pairs={{0,4},{4,0},{8,12},{12,8},{16,20},{20,16},{24,28},{28,24},{32,36},... | collective-permute-start | bytes 1130504 | tf_op jit(solution)/shard_map/ppermute | solution.py:466
  25.8 12.8 %collective-permute-start.4 = (f32[400,128]{1,0:T(8,128)S(1)}, f32[400,128]{1,0:T(8,128)S(1)}, u32[]{:S(2)}, u32[]{:S(2)}) collective-permute-start(f32[400,128]{1,0:T(8,128)S(1)} %get-tuple-element.57), channel_id=1, source_target_pairs={{0,2},{1,3},{2,0},{3,1},{4,6},{5,7},{6,4},{7,5},{8,10},{9,11},{10,... | collective-permute-start | bytes 614408 | tf_op jit(solution)/shard_map/ppermute | solution.py:452
  26.3 13.1 %collective-permute-start.5 = (f32[400,128]{1,0:T(8,128)S(1)}, f32[400,128]{1,0:T(8,128)S(1)}, u32[]{:S(2)}, u32[]{:S(2)}) collective-permute-start(f32[400,128]{1,0:T(8,128)S(1)} %get-tuple-element.58), channel_id=1, source_target_pairs={{0,3},{1,2},{2,1},{3,0},{4,7},{5,6},{6,5},{7,4},{8,11},{9,10},{10,... | collective-permute-start | bytes 614408 | tf_op jit(solution)/shard_map/ppermute | solution.py:452
  29.5 10.0 %collective-permute-start.6 = (f32[400,128]{1,0:T(8,128)S(1)}, f32[400,128]{1,0:T(8,128)S(1)}, u32[]{:S(2)}, u32[]{:S(2)}) collective-permute-start(f32[400,128]{1,0:T(8,128)S(1)} %get-tuple-element.59), channel_id=1, source_target_pairs={{0,1},{1,0},{2,3},{3,2},{4,5},{5,4},{6,7},{7,6},{8,9},{9,8},{10,11... | collective-permute-start | bytes 614408 | tf_op jit(solution)/shard_map/ppermute | solution.py:452
  34.2 10.9 %collective-permute-start.13 = (f32[400,128]{1,0:T(8,128)S(1)}, f32[400,128]{1,0:T(8,128)S(1)}, u32[]{:S(2)}, u32[]{:S(2)}) collective-permute-start(f32[400,128]{1,0:T(8,128)S(1)} %get-tuple-element.63), channel_id=1, source_target_pairs={{0,2},{1,3},{2,0},{3,1},{4,6},{5,7},{6,4},{7,5},{8,10},{9,11},{10,... | collective-permute-start | bytes 614408 | tf_op jit(solution)/shard_map/ppermute | solution.py:452
  34.7 14.1 %collective-permute-start.14 = (f32[400,128]{1,0:T(8,128)S(1)}, f32[400,128]{1,0:T(8,128)S(1)}, u32[]{:S(2)}, u32[]{:S(2)}) collective-permute-start(f32[400,128]{1,0:T(8,128)S(1)} %get-tuple-element.64), channel_id=1, source_target_pairs={{0,3},{1,2},{2,1},{3,0},{4,7},{5,6},{6,5},{7,4},{8,11},{9,10},{10,... | collective-permute-start | bytes 614408 | tf_op jit(solution)/shard_map/ppermute | solution.py:452
  38.7 10.1 %collective-permute-start.15 = (f32[400,128]{1,0:T(8,128)S(1)}, f32[400,128]{1,0:T(8,128)S(1)}, u32[]{:S(2)}, u32[]{:S(2)}) collective-permute-start(f32[400,128]{1,0:T(8,128)S(1)} %get-tuple-element.65), channel_id=1, source_target_pairs={{0,1},{1,0},{2,3},{3,2},{4,5},{5,4},{6,7},{7,6},{8,9},{9,8},{10,11... | collective-permute-start | bytes 614408 | tf_op jit(solution)/shard_map/ppermute | solution.py:452
  38.7 0.9 copy-start.1
  38.7 1.0 copy-start.2
  40.9 10.1 %collective-permute-start.7 = (f32[400,128]{1,0:T(8,128)S(1)}, f32[400,128]{1,0:T(8,128)S(1)}, u32[]{:S(2)}, u32[]{:S(2)}) collective-permute-start(f32[400,128]{1,0:T(8,128)S(1)} %get-tuple-element.72), channel_id=1, source_target_pairs={{0,2},{1,3},{2,0},{3,1},{4,6},{5,7},{6,4},{7,5},{8,10},{9,11},{10,... | collective-permute-start | bytes 614408 | tf_op jit(solution)/shard_map/ppermute | solution.py:452
  41.4 16.1 %collective-permute-start.8 = (f32[400,128]{1,0:T(8,128)S(1)}, f32[400,128]{1,0:T(8,128)S(1)}, u32[]{:S(2)}, u32[]{:S(2)}) collective-permute-start(f32[400,128]{1,0:T(8,128)S(1)} %get-tuple-element.73), channel_id=1, source_target_pairs={{0,3},{1,2},{2,1},{3,0},{4,7},{5,6},{6,5},{7,4},{8,11},{9,10},{10,... | collective-permute-start | bytes 614408 | tf_op jit(solution)/shard_map/ppermute | solution.py:452
  45.1 12.4 %collective-permute-start.9 = (f32[400,128]{1,0:T(8,128)S(1)}, f32[400,128]{1,0:T(8,128)S(1)}, u32[]{:S(2)}, u32[]{:S(2)}) collective-permute-start(f32[400,128]{1,0:T(8,128)S(1)} %get-tuple-element.74), channel_id=1, source_target_pairs={{0,1},{1,0},{2,3},{3,2},{4,5},{5,4},{6,7},{7,6},{8,9},{9,8},{10,11... | collective-permute-start | bytes 614408 | tf_op jit(solution)/shard_map/ppermute | solution.py:452
  50.0 11.5 %collective-permute-start.16 = (f32[400,128]{1,0:T(8,128)S(1)}, f32[400,128]{1,0:T(8,128)S(1)}, u32[]{:S(2)}, u32[]{:S(2)}) collective-permute-start(f32[400,128]{1,0:T(8,128)S(1)} %get-tuple-element.89), channel_id=1, source_target_pairs={{0,2},{1,3},{2,0},{3,1},{4,6},{5,7},{6,4},{7,5},{8,10},{9,11},{10,... | collective-permute-start | bytes 614408 | tf_op jit(solution)/shard_map/ppermute | solution.py:452
  50.5 16.1 %collective-permute-start.17 = (f32[400,128]{1,0:T(8,128)S(1)}, f32[400,128]{1,0:T(8,128)S(1)}, u32[]{:S(2)}, u32[]{:S(2)}) collective-permute-start(f32[400,128]{1,0:T(8,128)S(1)} %get-tuple-element.90), channel_id=1, source_target_pairs={{0,3},{1,2},{2,1},{3,0},{4,7},{5,6},{6,5},{7,4},{8,11},{9,10},{10,... | collective-permute-start | bytes 614408 | tf_op jit(solution)/shard_map/ppermute | solution.py:452
  51.1 15.5 %collective-permute-start.18 = (f32[400,128]{1,0:T(8,128)S(1)}, f32[400,128]{1,0:T(8,128)S(1)}, u32[]{:S(2)}, u32[]{:S(2)}) collective-permute-start(f32[400,128]{1,0:T(8,128)S(1)} %get-tuple-element.91), channel_id=1, source_target_pairs={{0,1},{1,0},{2,3},{3,2},{4,5},{5,4},{6,7},{7,6},{8,9},{9,8},{10,11... | collective-permute-start | bytes 614408 | tf_op jit(solution)/shard_map/ppermute | solution.py:452
  61.0 9.2 %collective-permute-start.10 = (f32[200,128]{1,0:T(8,128)S(1)}, f32[200,128]{1,0:T(8,128)S(1)}, u32[]{:S(2)}, u32[]{:S(2)}) collective-permute-start(f32[200,128]{1,0:T(8,128)S(1)} %get-tuple-element.77), channel_id=1, source_target_pairs={{0,2},{1,3},{2,0},{3,1},{4,6},{5,7},{6,4},{7,5},{8,10},{9,11},{10,... | collective-permute-start | bytes 307208 | tf_op jit(solution)/shard_map/ppermute | solution.py:452
  61.4 8.8 %collective-permute-start.11 = (f32[200,128]{1,0:T(8,128)S(1)}, f32[200,128]{1,0:T(8,128)S(1)}, u32[]{:S(2)}, u32[]{:S(2)}) collective-permute-start(f32[200,128]{1,0:T(8,128)S(1)} %get-tuple-element.78), channel_id=1, source_target_pairs={{0,3},{1,2},{2,1},{3,0},{4,7},{5,6},{6,5},{7,4},{8,11},{9,10},{10,... | collective-permute-start | bytes 307208 | tf_op jit(solution)/shard_map/ppermute | solution.py:452
  61.6 8.7 %collective-permute-start.12 = (f32[200,128]{1,0:T(8,128)S(1)}, f32[200,128]{1,0:T(8,128)S(1)}, u32[]{:S(2)}, u32[]{:S(2)}) collective-permute-start(f32[200,128]{1,0:T(8,128)S(1)} %get-tuple-element.79), channel_id=1, source_target_pairs={{0,1},{1,0},{2,3},{3,2},{4,5},{5,4},{6,7},{7,6},{8,9},{9,8},{10,11... | collective-permute-start | bytes 307208 | tf_op jit(solution)/shard_map/ppermute | solution.py:452
  70.2 10.1 %collective-permute-start.19 = (f32[736,128]{1,0:T(8,128)S(1)}, f32[736,128]{1,0:T(8,128)S(1)}, u32[]{:S(2)}, u32[]{:S(2)}) collective-permute-start(f32[736,128]{1,0:T(8,128)S(1)} %get-tuple-element.99), channel_id=1, source_target_pairs={{0,4},{4,0},{8,12},{12,8},{16,20},{20,16},{24,28},{28,24},{32,36},... | collective-permute-start | bytes 1130504 | tf_op jit(solution)/shard_map/ppermute | solution.py:466
  70.3 20.4 %collective-permute-start.24 = (f32[736,128]{1,0:T(8,128)S(1)}, f32[736,128]{1,0:T(8,128)S(1)}, u32[]{:S(2)}, u32[]{:S(2)}) collective-permute-start(f32[736,128]{1,0:T(8,128)S(1)} %get-tuple-element.105), channel_id=1, source_target_pairs={{0,252},{4,8},{8,4},{12,16},{16,12},{20,24},{24,20},{28,32},{32,28... | collective-permute-start | bytes 1130504 | tf_op jit(solution)/shard_map/ppermute | solution.py:466
  80.4 10.1 %collective-permute-start.20 = (f32[200,128]{1,0:T(8,128)S(1)}, f32[200,128]{1,0:T(8,128)S(1)}, u32[]{:S(2)}, u32[]{:S(2)}) collective-permute-start(f32[200,128]{1,0:T(8,128)S(1)} %get-tuple-element.101), channel_id=1, source_target_pairs={{0,2},{1,3},{2,0},{3,1},{4,6},{5,7},{6,4},{7,5},{8,10},{9,11},{10,... | collective-permute-start | bytes 307208 | tf_op jit(solution)/shard_map/ppermute | solution.py:452
  81.2 9.5 %collective-permute-start.21 = (f32[200,128]{1,0:T(8,128)S(1)}, f32[200,128]{1,0:T(8,128)S(1)}, u32[]{:S(2)}, u32[]{:S(2)}) collective-permute-start(f32[200,128]{1,0:T(8,128)S(1)} %get-tuple-element.102), channel_id=1, source_target_pairs={{0,3},{1,2},{2,1},{3,0},{4,7},{5,6},{6,5},{7,4},{8,11},{9,10},{10,... | collective-permute-start | bytes 307208 | tf_op jit(solution)/shard_map/ppermute | solution.py:452
  81.7 9.0 %collective-permute-start.22 = (f32[200,128]{1,0:T(8,128)S(1)}, f32[200,128]{1,0:T(8,128)S(1)}, u32[]{:S(2)}, u32[]{:S(2)}) collective-permute-start(f32[200,128]{1,0:T(8,128)S(1)} %get-tuple-element.103), channel_id=1, source_target_pairs={{0,1},{1,0},{2,3},{3,2},{4,5},{5,4},{6,7},{7,6},{8,9},{9,8},{10,11... | collective-permute-start | bytes 307208 | tf_op jit(solution)/shard_map/ppermute | solution.py:452
  82.3 16.9 %collective-permute-start.23 = (f32[736,128]{1,0:T(8,128)S(1)}, f32[736,128]{1,0:T(8,128)S(1)}, u32[]{:S(2)}, u32[]{:S(2)}) collective-permute-start(f32[736,128]{1,0:T(8,128)S(1)} %add.68), channel_id=1, source_target_pairs={{0,252},{4,8},{8,4},{12,16},{16,12},{20,24},{24,20},{28,32},{32,28... | collective-permute-start | bytes 1130504 | tf_op jit(solution)/shard_map/ppermute | solution.py:466
  90.8 9.9 %collective-permute-start.25 = (f32[736,128]{1,0:T(8,128)S(1)}, f32[736,128]{1,0:T(8,128)S(1)}, u32[]{:S(2)}, u32[]{:S(2)}) collective-permute-start(f32[736,128]{1,0:T(8,128)S(1)} %add.70), channel_id=1, source_target_pairs={{0,4},{4,0},{8,12},{12,8},{16,20},{20,16},{24,28},{28,24},{32,36},... | collective-permute-start | bytes 1130504 | tf_op jit(solution)/shard_map/ppermute | solution.py:466

commit v5 on v4

--- a/solution.py
+++ b/solution.py
@@ -17,8 +17,8 @@
 ROWS = LINES * G // LANES
 PAD_ROWS = 736
 GROUPS = ROWS // 9
-TILES = 11
-PAIR_ROWS = 200
+TILES = {1: 11, 2: 21}
+CHUNK_ROWS = {1: 200, 2: 384}
 STEP = 24
 DEPTH = 80
 SCREENING = 0.09
@@ -80,9 +80,9 @@
 
 
 def screened(device):
-    lanes = jnp.arange(TILES * LANES, dtype=jnp.int32)
+    lanes = jnp.arange(TILES[2] * LANES, dtype=jnp.int32)
     first = wavenumber(jnp.arange(G, dtype=jnp.int32))
-    second = wavenumber(jnp.minimum(device * PLANES + lanes // G, G - 1))
+    second = wavenumber(device * PLANES + lanes // G % PLANES)
     third = wavenumber(lanes % G)
     squared = first[:, None] ** 2 + (second**2)[None, :] + (third**2)[None, :]
     scaled = squared / (4.0 * SCREENING * SCREENING)
@@ -227,19 +227,18 @@
     line_passes(work, lines, len(pairs))
     column_passes(work, columns, len(pairs))
     lane = lane_index(PLANES)
-    for index in range(len(pairs)):
-        for out, step in zip(outs, STEPS):
-            first = (place[1] ^ step) * PLANES + index * LINES
-
-            def load(line, first=first):
-                return work[pl.ds(first + line, PLANES, stride=G), :]
-
-            def store(tile, value, start=index * PAIR_ROWS, out=out):
-                out[start + tile * PLANES : start + (tile + 1) * PLANES, :] = value
-
-            pack(PLANES, load, store, lane)
-            start = index * PAIR_ROWS + TILES * PLANES
-            out[start : start + 2, :] = jnp.zeros((2, LANES), jnp.float32)
+    for out, step in zip(outs, STEPS):
+        first = (place[1] ^ step) * PLANES
+
+        def load(line, first=first):
+            return work[pl.ds(line // PLANES * LINES + first + line % PLANES, PLANES, stride=G), :]
+
+        def store(tile, value, out=out):
+            out[tile * PLANES : (tile + 1) * PLANES, :] = value
+
+        pack(len(pairs) * PLANES, load, store, lane)
+        start = TILES[len(pairs)] * PLANES
+        out[start:, :] = jnp.zeros((CHUNK_ROWS[len(pairs)] - start, LANES), jnp.float32)
 
 
 def pencil_kernel(count, parts, place, *refs):
@@ -248,29 +247,35 @@
     forward, backward = forward.at[place[1]], backward.at[place[1]]
     lane = lane_index(G)
     energies = [jnp.zeros((G, LANES), jnp.float32) for _ in range(count)]
-    places = [(pair, tile) for tile in range(TILES) for pair in range(count)]
-    for group in range(0, len(places), 2):
-        now = places[group : group + 2]
+    for group in range(0, TILES[count], 2):
+        tiles = range(group, min(group + 2, TILES[count]))
         values = []
-        for pair, tile in now:
-            start = pair * PAIR_ROWS + tile * PLANES
-            values.append(jnp.concatenate([chunk[start : start + PLANES, :] for chunk in chunks], axis=0))
+        for tile in tiles:
+            rows = slice(tile * PLANES, (tile + 1) * PLANES)
+            values.append(jnp.concatenate([chunk[rows, :] for chunk in chunks], axis=0))
         solved = []
-        for (pair, tile), spectral in zip(now, along_columns(values, forward[...])):
+        for tile, spectral in zip(tiles, along_columns(values, forward[...])):
             spectral = spectral[:G]
             solved.append(spectral * kernel[:, tile * LANES : (tile + 1) * LANES])
-            if tile == TILES - 1:
-                spectral = jnp.where(lane < PLANES * G - tile * LANES, spectral, 0.0)
-            energies[pair] = energies[pair] + spectral * solved[-1]
-        for (pair, tile), value in zip(now, along_columns(solved, backward[...])):
-            start = pair * PAIR_ROWS + tile * PLANES
+            energy = spectral * solved[-1]
+            border = PLANES * G - tile * LANES
+            if border >= LANES or count == 1:
+                energies[0] = energies[0] + energy
+            elif border <= 0:
+                energies[1] = energies[1] + energy
+            else:
+                energies[0] = energies[0] + jnp.where(lane < border, energy, 0.0)
+                energies[1] = energies[1] + jnp.where(lane < border, 0.0, energy)
+        for tile, value in zip(tiles, along_columns(solved, backward[...])):
             for index, out in enumerate(outs):
-                out[start : start + PLANES, :] = value[index * STEP : index * STEP + PLANES]
+                out[tile * PLANES : (tile + 1) * PLANES, :] = value[index * STEP : index * STEP + PLANES]
+    for out in outs:
+        out[TILES[count] * PLANES :, :] = jnp.zeros((CHUNK_ROWS[count] - TILES[count] * PLANES, LANES), jnp.float32)
     for pair in range(count):
-        total = jnp.full((2, LANES), jnp.sum(energies[pair]), jnp.float32)
-        start = pair * PAIR_ROWS + TILES * PLANES
+        total = jnp.full((1, LANES), jnp.sum(energies[pair]), jnp.float32)
+        row = TILES[count] * PLANES + pair
         for out in outs:
-            out[start : start + 2, :] = total
+            out[row : row + 1, :] = total
 
 
 def gather_kernel(count, parts, names, shares, place, *refs):
@@ -281,17 +286,16 @@
     added = dict(zip((2, -2), refs[len(names) : -1 - len(shares)]))
     upward = place[0] == 0
     lane = lane_index(PLANES)
-    for pair in range(count):
-        for chunk, step in zip(chunks, STEPS):
-            first = pair * LINES + (place[1] ^ step) * PLANES
-
-            def load(tile, start=pair * PAIR_ROWS, chunk=chunk):
-                return chunk[start + tile * PLANES : start + (tile + 1) * PLANES, :]
-
-            def store(line, value, first=first):
-                work[pl.ds(first + line, PLANES, stride=G), :] = value
-
-            unpack(PLANES, load, store, lane)
+    for chunk, step in zip(chunks, STEPS):
+        first = (place[1] ^ step) * PLANES
+
+        def load(tile, chunk=chunk):
+            return chunk[tile * PLANES : (tile + 1) * PLANES, :]
+
+        def store(line, value, first=first):
+            work[pl.ds(line // PLANES * LINES + first + line % PLANES, PLANES, stride=G), :] = value
+
+        unpack(count * PLANES, load, store, lane)
     column_passes(work, columns, count)
     line_passes(work, lines, count)
     lane = lane_index(GROUPS)
@@ -336,7 +340,7 @@
     for name, share in shares.items():
         total = jnp.zeros((1, LANES), jnp.float32)
         for pair, _ in share:
-            start = pair * PAIR_ROWS + TILES * PLANES
+            start = TILES[count] * PLANES + pair
             for device in range(DEVICES):
                 total = total + device_row(chunks, place, device, start)
         totals[name] = jnp.broadcast_to(total, (PAD_ROWS - ROWS, LANES))
@@ -374,7 +378,7 @@
 
 
 def chunks_of(count, parts):
-    rows = count * PAIR_ROWS
+    rows = CHUNK_ROWS[count]
     if parts == 1:
         return [jax.ShapeDtypeStruct((DEVICES, rows, LANES), jnp.float32)]
     return [jax.ShapeDtypeStruct((rows, LANES), jnp.float32)] * parts
@@ -485,7 +489,7 @@
     close = {0: own, (1, 0): first, (1, 1): second}
     near = spread_pairs(close, [(0, 1), (-1, 1)], tables)
     third, fourth = after((third, fourth), near)
-    wide = {(1, 0): first, (1, 1): second, (2, 0): third, (2, 1): fourth}
+    wide = {(1, 1): second, (1, 0): first, (2, 1): fourth, (2, 0): third}
     far = spread_pairs(wide, [(-1, 2), (-2, 2)], tables)
     none = spread_pairs({0: after(own, far)}, [(0, 0)], tables)
     near = solve_pencils(exchanged(near), 2, tables)

time: 102 us -> 107 us (1.049)
  the two profiles are of different devices: /device:TPU:1 before, /device:TPU:16 now
where the time goes in v5:
time: 107 us; the launch traced here: 106 us
  starting transfers between devices  43.9 us (41%)
  waiting for transfers between devices  38.5 us (36%)
  Pallas kernels  21.7 us (20%)
    ppermute x8, starting transfers between devices, swapped(): return lax.ppermute(value, 'orb', pairs)  30.5 us
    ppermute x18, waiting for transfers between devices, exchanged(): received.append(lax.ppermute(chunk, 'grid', pairs))  21.4 us
    ppermute x8, waiting for transfers between devices, swapped(): return lax.ppermute(value, 'orb', pairs)  17.1 us
    ppermute x18, starting transfers between devices, exchanged(): received.append(lax.ppermute(chunk, 'grid', pairs))  13.4 us
    pallas_call x3, Pallas kernels, gather_shares(): pl.pallas_call(lambda *refs: gather_kernel(count, parts, list(orbitals),...  9.01 us
    pallas_call x3, Pallas kernels, spread_pairs(): pl.pallas_call(lambda *refs: spread_kernel(pairs, list(orbitals), *refs),...  8.21 us
    pallas_call x3, Pallas kernels, solve_pencils(): pl.pallas_call(lambda *refs: pencil_kernel(count, parts, *refs), out_shap...  3.56 us
  transfers between devices with their start and end apart: 26, of which 12 were waited for; matrix products, arithmetic and copies ran while one was open for 1% of the time, Pallas kernels for 20%

profile of v5, /device:TPU:16, one launch (start us, length us, event | category | flops | bytes accessed | tf_op | source)
XLA Modules:
  0.0 106.5 jit_solution(15575095143197108334)
XLA Ops:
  0.6 1.0 copy-done.4
  1.7 2.0 %collective-permute-start.1 = (f32[736,128]{1,0:T(8,128)S(1)}, f32[736,128]{1,0:T(8,128)S(1)}, u32[]{:S(2)}, u32[]{:S(2)}) collective-permute-start(f32[736,128]{1,0:T(8,128)S(1)} %enter.1.refs_1_.refs_7_.own), channel_id=1, source_target_pairs={{0,4},{4,0},{8,12},{12,8},{16,20},{20,16},{24,28},{28,24},{32,36},... | collective-permute-start | bytes 1130504 | tf_op jit(solution)/shard_map/ppermute | solution.py:470
  3.7 6.9 %collective-permute-start = (f32[736,128]{1,0:T(8,128)S(1)}, f32[736,128]{1,0:T(8,128)S(1)}, u32[]{:S(2)}, u32[]{:S(2)}) collective-permute-start(f32[736,128]{1,0:T(8,128)S(1)} %enter.1.refs_1_.refs_7_.own), channel_id=1, source_target_pairs={{0,252},{4,8},{8,4},{12,16},{16,12},{20,24},{24,20},{28,32},{32,28... | collective-permute-start | bytes 1130504 | tf_op jit(solution)/shard_map/ppermute | solution.py:470
  10.6 1.8 %collective-permute-done.1.refs_2_.refs_8_ = f32[736,128]{1,0:T(8,128)S(1)} collective-permute-done((f32[736,128]{1,0:T(8,128)S(1)}, f32[736,128]{1,0:T(8,128)S(1)}, u32[]{:S(2)}, u32[]{:S(2)}) %collective-permute-start.1) | collective-permute-done | bytes 376864 | tf_op jit(solution)/shard_map/ppermute | solution.py:470
  12.4 7.6 %collective-permute-start.2 = (f32[736,128]{1,0:T(8,128)S(1)}, f32[736,128]{1,0:T(8,128)S(1)}, u32[]{:S(2)}, u32[]{:S(2)}) collective-permute-start(f32[736,128]{1,0:T(8,128)S(1)} %collective-permute-done.1.refs_2_.refs_8_), channel_id=1, source_target_pairs={{0,252},{4,8},{8,4},{12,16},{16,12},{20,24},{24,20},{28,32},{32,28... | collective-permute-start | bytes 1130504 | tf_op jit(solution)/shard_map/ppermute | solution.py:470
  20.1 0.1 pad_add_fusion.refs_0_
  20.2 3.1 %spread.3 = (f32[384,128]{1,0:T(8,128)S(1)}, f32[384,128]{1,0:T(8,128)S(1)}, f32[384,128]{1,0:T(8,128)S(1)}, f32[384,128]{1,0:T(8,128)S(1)}) custom-call(s32[2]{0:T(128)S(1)} %pad_add_fusion.refs_0_, f32[736,128]{1,0:T(8,128)S(1)} %enter.1.refs_1_.refs_7_.own, f32[736,128]{1,0:T(8,128)S(1)} %collective-permute-done.1.refs_2_.refs_8_, ...), custom_call_target="tpu_custom_call" | custom-call | tf_op jit(solution)/shard_map/spread/pallas_call | solution.py:392
  23.3 2.3 %collective-permute-start.4 = (f32[384,128]{1,0:T(8,128)S(1)}, f32[384,128]{1,0:T(8,128)S(1)}, u32[]{:S(2)}, u32[]{:S(2)}) collective-permute-start(f32[384,128]{1,0:T(8,128)S(1)} %get-tuple-element.57), channel_id=1, source_target_pairs={{0,2},{1,3},{2,0},{3,1},{4,6},{5,7},{6,4},{7,5},{8,10},{9,11},{10,... | collective-permute-start | bytes 589832 | tf_op jit(solution)/shard_map/ppermute | solution.py:456
  25.6 0.1 collective-permute-start.5
  25.7 0.1 collective-permute-start.6
  25.8 2.3 %collective-permute-done.2.refs_4_.refs_10_ = f32[736,128]{1,0:T(8,128)S(1)} collective-permute-done((f32[736,128]{1,0:T(8,128)S(1)}, f32[736,128]{1,0:T(8,128)S(1)}, u32[]{:S(2)}, u32[]{:S(2)}) %collective-permute-start.2) | collective-permute-done | bytes 376864 | tf_op jit(solution)/shard_map/ppermute | solution.py:470
  28.1 1.3 %collective-permute-done.3.refs_3_.refs_9_ = f32[736,128]{1,0:T(8,128)S(1)} collective-permute-done((f32[736,128]{1,0:T(8,128)S(1)}, f32[736,128]{1,0:T(8,128)S(1)}, u32[]{:S(2)}, u32[]{:S(2)}) %collective-permute-start.3) | collective-permute-done | bytes 376864 | tf_op jit(solution)/shard_map/ppermute | solution.py:470
  29.4 3.2 %spread.4 = (f32[384,128]{1,0:T(8,128)S(1)}, f32[384,128]{1,0:T(8,128)S(1)}, f32[384,128]{1,0:T(8,128)S(1)}, f32[384,128]{1,0:T(8,128)S(1)}) custom-call(s32[2]{0:T(128)S(1)} %pad_add_fusion.refs_0_, f32[736,128]{1,0:T(8,128)S(1)} %collective-permute-done.refs_3_.refs_1_.refs_9_.refs_7_, f32[736,128]{1,0:T(8,128)S(1)} %collective-permute-done.1.refs_2_.refs_8_, ...), custom_call_target="tpu_custom_call" | custom-call | tf_op jit(solution)/shard_map/spread/pallas_call | solution.py:392
  32.6 2.3 %collective-permute-start.13 = (f32[384,128]{1,0:T(8,128)S(1)}, f32[384,128]{1,0:T(8,128)S(1)}, u32[]{:S(2)}, u32[]{:S(2)}) collective-permute-start(f32[384,128]{1,0:T(8,128)S(1)} %get-tuple-element.63), channel_id=1, source_target_pairs={{0,2},{1,3},{2,0},{3,1},{4,6},{5,7},{6,4},{7,5},{8,10},{9,11},{10,... | collective-permute-start | bytes 589832 | tf_op jit(solution)/shard_map/ppermute | solution.py:456
  34.9 0.2 collective-permute-start.15
  35.1 0.4 fusion.refs_5_
  35.5 1.8 %collective-permute-done.5.refs_3_ = f32[384,128]{1,0:T(8,128)S(1)} collective-permute-done((f32[384,128]{1,0:T(8,128)S(1)}, f32[384,128]{1,0:T(8,128)S(1)}, u32[]{:S(2)}, u32[]{:S(2)}) %collective-permute-start.5) | collective-permute-done | bytes 196640 | tf_op jit(solution)/shard_map/ppermute | solution.py:456
  37.3 1.3 %pencils.3 = (f32[384,128]{1,0:T(8,128)S(1)}, f32[384,128]{1,0:T(8,128)S(1)}, f32[384,128]{1,0:T(8,128)S(1)}, f32[384,128]{1,0:T(8,128)S(1)}) custom-call(s32[2]{0:T(128)S(1)} %pad_add_fusion.refs_0_, f32[384,128]{1,0:T(8,128)S(1)} %get-tuple-element.56.refs_1_, f32[384,128]{1,0:T(8,128)S(1)} %collective-permute-done.4.refs_2_, ...), custom_call_target="tpu_custom_call" | custom-call | tf_op jit(solution)/shard_map/pencils/pallas_call | solution.py:405
  38.5 0.8 collective-permute-start.7
  39.4 0.7 collective-permute-start.8
  40.1 1.9 %spread.5 = (f32[200,128]{1,0:T(8,128)S(1)}, f32[200,128]{1,0:T(8,128)S(1)}, f32[200,128]{1,0:T(8,128)S(1)}, f32[200,128]{1,0:T(8,128)S(1)}) custom-call(s32[2]{0:T(128)S(1)} %pad_add_fusion.refs_0_, f32[736,128]{1,0:T(8,128)S(1)} %enter.1.refs_1_.refs_7_.own, bf16[256,256]{1,0:T(8,128)(2,1)S(1)} %copy-done, bf16[80,240]{1,0:T(8,128)(2,1)S(1)} %copy-done.3), custom_call_target="tpu_custom_call" | custom-call | tf_op jit(solution)/shard_map/spread/pallas_call | solution.py:392
  42.0 0.9 collective-permute-start.9
  43.0 2.7 %collective-permute-done.14.refs_3_ = f32[384,128]{1,0:T(8,128)S(1)} collective-permute-done((f32[384,128]{1,0:T(8,128)S(1)}, f32[384,128]{1,0:T(8,128)S(1)}, u32[]{:S(2)}, u32[]{:S(2)}) %collective-permute-start.14) | collective-permute-done | bytes 196640 | tf_op jit(solution)/shard_map/ppermute | solution.py:456
  45.7 1.3 %pencils.5 = (f32[384,128]{1,0:T(8,128)S(1)}, f32[384,128]{1,0:T(8,128)S(1)}, f32[384,128]{1,0:T(8,128)S(1)}, f32[384,128]{1,0:T(8,128)S(1)}) custom-call(s32[2]{0:T(128)S(1)} %pad_add_fusion.refs_0_, f32[384,128]{1,0:T(8,128)S(1)} %get-tuple-element.84.refs_1_, f32[384,128]{1,0:T(8,128)S(1)} %collective-permute-done.13.refs_2_, ...), custom_call_target="tpu_custom_call" | custom-call | tf_op jit(solution)/shard_map/pencils/pallas_call | solution.py:405
  46.9 0.5 collective-permute-start.16
  47.5 1.0 collective-permute-start.17
  48.5 1.6 %collective-permute-done.7.refs_2_ = f32[384,128]{1,0:T(8,128)S(1)} collective-permute-done((f32[384,128]{1,0:T(8,128)S(1)}, f32[384,128]{1,0:T(8,128)S(1)}, u32[]{:S(2)}, u32[]{:S(2)}) %collective-permute-start.7) | collective-permute-done | bytes 196640 | tf_op jit(solution)/shard_map/ppermute | solution.py:456
  50.1 4.0 %collective-permute-done.8.refs_3_ = f32[384,128]{1,0:T(8,128)S(1)} collective-permute-done((f32[384,128]{1,0:T(8,128)S(1)}, f32[384,128]{1,0:T(8,128)S(1)}, u32[]{:S(2)}, u32[]{:S(2)}) %collective-permute-start.8) | collective-permute-done | bytes 196640 | tf_op jit(solution)/shard_map/ppermute | solution.py:456
  54.1 3.4 %gather.3 = (f32[736,128]{1,0:T(8,128)S(1)}, f32[736,128]{1,0:T(8,128)S(1)}, f32[736,128]{1,0:T(8,128)S(1)}) custom-call(s32[2]{0:T(128)S(1)} %pad_add_fusion.refs_0_, f32[384,128]{1,0:T(8,128)S(1)} %get-tuple-element.71.refs_1_, f32[384,128]{1,0:T(8,128)S(1)} %collective-permute-done.7.refs_2_, f32[384,128]{1,0:T(8,128)S(1)} %collective-permute-done.8.refs_3_, ...), custom_call_target="tpu_custom_call" | custom-call | tf_op jit(solution)/shard_map/gather/pallas_call | solution.py:417
  57.5 0.5 collective-permute-start.10
  58.1 1.0 collective-permute-start.11
  59.1 0.7 collective-permute-start.12
  59.8 2.7 %collective-permute-done.17.refs_3_ = f32[384,128]{1,0:T(8,128)S(1)} collective-permute-done((f32[384,128]{1,0:T(8,128)S(1)}, f32[384,128]{1,0:T(8,128)S(1)}, u32[]{:S(2)}, u32[]{:S(2)}) %collective-permute-start.17) | collective-permute-done | bytes 196640 | tf_op jit(solution)/shard_map/ppermute | solution.py:456
  62.5 3.6 %gather.4 = (f32[736,128]{1,0:T(8,128)S(1)}, f32[736,128]{1,0:T(8,128)S(1)}, f32[736,128]{1,0:T(8,128)S(1)}, f32[736,128]{1,0:T(8,128)S(1)}) custom-call(s32[2]{0:T(128)S(1)} %pad_add_fusion.refs_0_, f32[384,128]{1,0:T(8,128)S(1)} %get-tuple-element.92.refs_1_, f32[384,128]{1,0:T(8,128)S(1)} %collective-permute-done.16.refs_2_, ...), custom_call_target="tpu_custom_call" | custom-call | tf_op jit(solution)/shard_map/gather/pallas_call | solution.py:417
  66.1 0.8 collective-permute-done.11.refs_3_
  66.9 6.9 %collective-permute-start.24 = (f32[736,128]{1,0:T(8,128)S(1)}, f32[736,128]{1,0:T(8,128)S(1)}, u32[]{:S(2)}, u32[]{:S(2)}) collective-permute-start(f32[736,128]{1,0:T(8,128)S(1)} %get-tuple-element.105), channel_id=1, source_target_pairs={{0,252},{4,8},{8,4},{12,16},{16,12},{20,24},{24,20},{28,32},{32,28... | collective-permute-start | bytes 1130504 | tf_op jit(solution)/shard_map/ppermute | solution.py:470
  73.8 1.0 pencils.4
  74.8 2.9 %collective-permute-done.19 = f32[736,128]{1,0:T(8,128)S(1)} collective-permute-done((f32[736,128]{1,0:T(8,128)S(1)}, f32[736,128]{1,0:T(8,128)S(1)}, u32[]{:S(2)}, u32[]{:S(2)}) %collective-permute-start.19) | collective-permute-done | bytes 376864 | tf_op jit(solution)/shard_map/ppermute | solution.py:470
  77.7 0.5 collective-permute-start.20
  78.2 0.1 collective-permute-start.21
  78.3 1.5 %collective-permute-start.22 = (f32[200,128]{1,0:T(8,128)S(1)}, f32[200,128]{1,0:T(8,128)S(1)}, u32[]{:S(2)}, u32[]{:S(2)}) collective-permute-start(f32[200,128]{1,0:T(8,128)S(1)} %get-tuple-element.103), channel_id=1, source_target_pairs={{0,1},{1,0},{2,3},{3,2},{4,5},{5,4},{6,7},{7,6},{8,9},{9,8},{10,11... | collective-permute-start | bytes 307208 | tf_op jit(solution)/shard_map/ppermute | solution.py:456
  79.8 0.1 add.77
  79.9 6.9 %collective-permute-start.23 = (f32[736,128]{1,0:T(8,128)S(1)}, f32[736,128]{1,0:T(8,128)S(1)}, u32[]{:S(2)}, u32[]{:S(2)}) collective-permute-start(f32[736,128]{1,0:T(8,128)S(1)} %add.77), channel_id=1, source_target_pairs={{0,252},{4,8},{8,4},{12,16},{16,12},{20,24},{24,20},{28,32},{32,28... | collective-permute-start | bytes 1130504 | tf_op jit(solution)/shard_map/ppermute | solution.py:470
  86.8 7.7 %collective-permute-done.21.refs_3_ = f32[200,128]{1,0:T(8,128)S(1)} collective-permute-done((f32[200,128]{1,0:T(8,128)S(1)}, f32[200,128]{1,0:T(8,128)S(1)}, u32[]{:S(2)}, u32[]{:S(2)}) %collective-permute-start.21) | collective-permute-done | bytes 102432 | tf_op jit(solution)/shard_map/ppermute | solution.py:456
  94.6 0.1 collective-permute-start.25
  94.7 2.0 %gather.5.refs_0_ = f32[736,128]{1,0:T(8,128)S(1)} custom-call(s32[2]{0:T(128)S(1)} %pad_add_fusion.refs_0_, f32[200,128]{1,0:T(8,128)S(1)} %get-tuple-element.100.refs_1_, f32[200,128]{1,0:T(8,128)S(1)} %collective-permute-done.20.refs_2_, f32[200,128]{1,0:T(8,128)S(1)} %collective-permute-done.21.refs_3_, f32[200,128]{1,0:T(8,128)S(1)} %collective-permute-done.22.refs_4_, ...), custom_call_target="tpu_custom_call" | custom-call | tf_op jit(solution)/shard_map/gather/pallas_call | solution.py:417
  96.8 8.8 %collective-permute-done.25.refs_2_ = f32[736,128]{1,0:T(8,128)S(1)} collective-permute-done((f32[736,128]{1,0:T(8,128)S(1)}, f32[736,128]{1,0:T(8,128)S(1)}, u32[]{:S(2)}, u32[]{:S(2)}) %collective-permute-start.25) | collective-permute-done | bytes 376864 | tf_op jit(solution)/shard_map/ppermute | solution.py:470
  105.6 0.8 leave.1
  (32 shorter events, 0.2 us)
Async XLA Ops:
  0.6 1.0 copy-start.4
  1.6 18.5 %copy-start = (bf16[256,256]{1,0:T(8,128)(2,1)S(1)}, bf16[256,256]{1,0:T(8,128)(2,1)}, u32[]{:S(2)}) copy-start(bf16[256,256]{1,0:T(8,128)(2,1)} %constant.72.clone.refs_4_.refs_5_.refs_2_) | copy-start | bytes 393220
  1.6 18.5 %copy-start.3 = (bf16[80,240]{1,0:T(8,128)(2,1)S(1)}, bf16[80,240]{1,0:T(8,128)(2,1)}, u32[]{:S(2)}) copy-start(bf16[80,240]{1,0:T(8,128)(2,1)} %constant.73.clone.refs_5_.refs_6_.refs_3_) | copy-start | bytes 115204
  1.7 10.8 %collective-permute-start.1 = (f32[736,128]{1,0:T(8,128)S(1)}, f32[736,128]{1,0:T(8,128)S(1)}, u32[]{:S(2)}, u32[]{:S(2)}) collective-permute-start(f32[736,128]{1,0:T(8,128)S(1)} %enter.1.refs_1_.refs_7_.own), channel_id=1, source_target_pairs={{0,4},{4,0},{8,12},{12,8},{16,20},{20,16},{24,28},{28,24},{32,36},... | collective-permute-start | bytes 1130504 | tf_op jit(solution)/shard_map/ppermute | solution.py:470
  3.7 16.4 %collective-permute-start = (f32[736,128]{1,0:T(8,128)S(1)}, f32[736,128]{1,0:T(8,128)S(1)}, u32[]{:S(2)}, u32[]{:S(2)}) collective-permute-start(f32[736,128]{1,0:T(8,128)S(1)} %enter.1.refs_1_.refs_7_.own), channel_id=1, source_target_pairs={{0,252},{4,8},{8,4},{12,16},{16,12},{20,24},{24,20},{28,32},{32,28... | collective-permute-start | bytes 1130504 | tf_op jit(solution)/shard_map/ppermute | solution.py:470
  12.4 15.7 %collective-permute-start.2 = (f32[736,128]{1,0:T(8,128)S(1)}, f32[736,128]{1,0:T(8,128)S(1)}, u32[]{:S(2)}, u32[]{:S(2)}) collective-permute-start(f32[736,128]{1,0:T(8,128)S(1)} %collective-permute-done.1.refs_2_.refs_8_), channel_id=1, source_target_pairs={{0,252},{4,8},{8,4},{12,16},{16,12},{20,24},{24,20},{28,32},{32,28... | collective-permute-start | bytes 1130504 | tf_op jit(solution)/shard_map/ppermute | solution.py:470
  20.1 9.4 %collective-permute-start.3 = (f32[736,128]{1,0:T(8,128)S(1)}, f32[736,128]{1,0:T(8,128)S(1)}, u32[]{:S(2)}, u32[]{:S(2)}) collective-permute-start(f32[736,128]{1,0:T(8,128)S(1)} %collective-permute-done.refs_3_.refs_1_.refs_9_.refs_7_), channel_id=1, source_target_pairs={{0,4},{4,0},{8,12},{12,8},{16,20},{20,16},{24,28},{28,24},{32,36},... | collective-permute-start | bytes 1130504 | tf_op jit(solution)/shard_map/ppermute | solution.py:470
  23.3 11.6 %collective-permute-start.4 = (f32[384,128]{1,0:T(8,128)S(1)}, f32[384,128]{1,0:T(8,128)S(1)}, u32[]{:S(2)}, u32[]{:S(2)}) collective-permute-start(f32[384,128]{1,0:T(8,128)S(1)} %get-tuple-element.57), channel_id=1, source_target_pairs={{0,2},{1,3},{2,0},{3,1},{4,6},{5,7},{6,4},{7,5},{8,10},{9,11},{10,... | collective-permute-start | bytes 589832 | tf_op jit(solution)/shard_map/ppermute | solution.py:456
  25.6 11.6 %collective-permute-start.5 = (f32[384,128]{1,0:T(8,128)S(1)}, f32[384,128]{1,0:T(8,128)S(1)}, u32[]{:S(2)}, u32[]{:S(2)}) collective-permute-start(f32[384,128]{1,0:T(8,128)S(1)} %get-tuple-element.58), channel_id=1, source_target_pairs={{0,3},{1,2},{2,1},{3,0},{4,7},{5,6},{6,5},{7,4},{8,11},{9,10},{10,... | collective-permute-start | bytes 589832 | tf_op jit(solution)/shard_map/ppermute | solution.py:456
  25.7 11.5 %collective-permute-start.6 = (f32[384,128]{1,0:T(8,128)S(1)}, f32[384,128]{1,0:T(8,128)S(1)}, u32[]{:S(2)}, u32[]{:S(2)}) collective-permute-start(f32[384,128]{1,0:T(8,128)S(1)} %get-tuple-element.59), channel_id=1, source_target_pairs={{0,1},{1,0},{2,3},{3,2},{4,5},{5,4},{6,7},{7,6},{8,9},{9,8},{10,11... | collective-permute-start | bytes 589832 | tf_op jit(solution)/shard_map/ppermute | solution.py:456
  32.6 9.4 %collective-permute-start.13 = (f32[384,128]{1,0:T(8,128)S(1)}, f32[384,128]{1,0:T(8,128)S(1)}, u32[]{:S(2)}, u32[]{:S(2)}) collective-permute-start(f32[384,128]{1,0:T(8,128)S(1)} %get-tuple-element.63), channel_id=1, source_target_pairs={{0,2},{1,3},{2,0},{3,1},{4,6},{5,7},{6,4},{7,5},{8,10},{9,11},{10,... | collective-permute-start | bytes 589832 | tf_op jit(solution)/shard_map/ppermute | solution.py:456
  34.9 10.8 %collective-permute-start.14 = (f32[384,128]{1,0:T(8,128)S(1)}, f32[384,128]{1,0:T(8,128)S(1)}, u32[]{:S(2)}, u32[]{:S(2)}) collective-permute-start(f32[384,128]{1,0:T(8,128)S(1)} %get-tuple-element.64), channel_id=1, source_target_pairs={{0,3},{1,2},{2,1},{3,0},{4,7},{5,6},{6,5},{7,4},{8,11},{9,10},{10,... | collective-permute-start | bytes 589832 | tf_op jit(solution)/shard_map/ppermute | solution.py:456
  34.9 10.8 %collective-permute-start.15 = (f32[384,128]{1,0:T(8,128)S(1)}, f32[384,128]{1,0:T(8,128)S(1)}, u32[]{:S(2)}, u32[]{:S(2)}) collective-permute-start(f32[384,128]{1,0:T(8,128)S(1)} %get-tuple-element.65), channel_id=1, source_target_pairs={{0,1},{1,0},{2,3},{3,2},{4,5},{5,4},{6,7},{7,6},{8,9},{9,8},{10,11... | collective-permute-start | bytes 589832 | tf_op jit(solution)/shard_map/ppermute | solution.py:456
  35.1 2.2 %copy-start.1 = (bf16[4,96,240]{2,1,0:T(8,128)(2,1)S(1)}, bf16[4,96,240]{2,1,0:T(8,128)(2,1)}, u32[]{:S(2)}) copy-start(bf16[4,96,240]{2,1,0:T(8,128)(2,1)} %constant.75.clone.refs_7_) | copy-start | bytes 552964
  35.1 2.2 %copy-start.2 = (bf16[4,80,240]{2,1,0:T(8,128)(2,1)S(1)}, bf16[4,80,240]{2,1,0:T(8,128)(2,1)}, u32[]{:S(2)}) copy-start(bf16[4,80,240]{2,1,0:T(8,128)(2,1)} %constant.74.clone.refs_6_) | copy-start | bytes 460804
  38.5 11.6 %collective-permute-start.7 = (f32[384,128]{1,0:T(8,128)S(1)}, f32[384,128]{1,0:T(8,128)S(1)}, u32[]{:S(2)}, u32[]{:S(2)}) collective-permute-start(f32[384,128]{1,0:T(8,128)S(1)} %get-tuple-element.72), channel_id=1, source_target_pairs={{0,2},{1,3},{2,0},{3,1},{4,6},{5,7},{6,4},{7,5},{8,10},{9,11},{10,... | collective-permute-start | bytes 589832 | tf_op jit(solution)/shard_map/ppermute | solution.py:456
  39.4 14.7 %collective-permute-start.8 = (f32[384,128]{1,0:T(8,128)S(1)}, f32[384,128]{1,0:T(8,128)S(1)}, u32[]{:S(2)}, u32[]{:S(2)}) collective-permute-start(f32[384,128]{1,0:T(8,128)S(1)} %get-tuple-element.73), channel_id=1, source_target_pairs={{0,3},{1,2},{2,1},{3,0},{4,7},{5,6},{6,5},{7,4},{8,11},{9,10},{10,... | collective-permute-start | bytes 589832 | tf_op jit(solution)/shard_map/ppermute | solution.py:456
  42.0 12.1 %collective-permute-start.9 = (f32[384,128]{1,0:T(8,128)S(1)}, f32[384,128]{1,0:T(8,128)S(1)}, u32[]{:S(2)}, u32[]{:S(2)}) collective-permute-start(f32[384,128]{1,0:T(8,128)S(1)} %get-tuple-element.74), channel_id=1, source_target_pairs={{0,1},{1,0},{2,3},{3,2},{4,5},{5,4},{6,7},{7,6},{8,9},{9,8},{10,11... | collective-permute-start | bytes 589832 | tf_op jit(solution)/shard_map/ppermute | solution.py:456
  46.9 12.2 %collective-permute-start.16 = (f32[384,128]{1,0:T(8,128)S(1)}, f32[384,128]{1,0:T(8,128)S(1)}, u32[]{:S(2)}, u32[]{:S(2)}) collective-permute-start(f32[384,128]{1,0:T(8,128)S(1)} %get-tuple-element.89), channel_id=1, source_target_pairs={{0,2},{1,3},{2,0},{3,1},{4,6},{5,7},{6,4},{7,5},{8,10},{9,11},{10,... | collective-permute-start | bytes 589832 | tf_op jit(solution)/shard_map/ppermute | solution.py:456
  47.5 15.1 %collective-permute-start.17 = (f32[384,128]{1,0:T(8,128)S(1)}, f32[384,128]{1,0:T(8,128)S(1)}, u32[]{:S(2)}, u32[]{:S(2)}) collective-permute-start(f32[384,128]{1,0:T(8,128)S(1)} %get-tuple-element.90), channel_id=1, source_target_pairs={{0,3},{1,2},{2,1},{3,0},{4,7},{5,6},{6,5},{7,4},{8,11},{9,10},{10,... | collective-permute-start | bytes 589832 | tf_op jit(solution)/shard_map/ppermute | solution.py:456
  50.1 12.5 %collective-permute-start.18 = (f32[384,128]{1,0:T(8,128)S(1)}, f32[384,128]{1,0:T(8,128)S(1)}, u32[]{:S(2)}, u32[]{:S(2)}) collective-permute-start(f32[384,128]{1,0:T(8,128)S(1)} %get-tuple-element.91), channel_id=1, source_target_pairs={{0,1},{1,0},{2,3},{3,2},{4,5},{5,4},{6,7},{7,6},{8,9},{9,8},{10,11... | collective-permute-start | bytes 589832 | tf_op jit(solution)/shard_map/ppermute | solution.py:456
  57.5 8.5 %collective-permute-start.10 = (f32[200,128]{1,0:T(8,128)S(1)}, f32[200,128]{1,0:T(8,128)S(1)}, u32[]{:S(2)}, u32[]{:S(2)}) collective-permute-start(f32[200,128]{1,0:T(8,128)S(1)} %get-tuple-element.77), channel_id=1, source_target_pairs={{0,2},{1,3},{2,0},{3,1},{4,6},{5,7},{6,4},{7,5},{8,10},{9,11},{10,... | collective-permute-start | bytes 307208 | tf_op jit(solution)/shard_map/ppermute | solution.py:456
  58.1 8.8 %collective-permute-start.11 = (f32[200,128]{1,0:T(8,128)S(1)}, f32[200,128]{1,0:T(8,128)S(1)}, u32[]{:S(2)}, u32[]{:S(2)}) collective-permute-start(f32[200,128]{1,0:T(8,128)S(1)} %get-tuple-element.78), channel_id=1, source_target_pairs={{0,3},{1,2},{2,1},{3,0},{4,7},{5,6},{6,5},{7,4},{8,11},{9,10},{10,... | collective-permute-start | bytes 307208 | tf_op jit(solution)/shard_map/ppermute | solution.py:456
  59.1 7.8 %collective-permute-start.12 = (f32[200,128]{1,0:T(8,128)S(1)}, f32[200,128]{1,0:T(8,128)S(1)}, u32[]{:S(2)}, u32[]{:S(2)}) collective-permute-start(f32[200,128]{1,0:T(8,128)S(1)} %get-tuple-element.79), channel_id=1, source_target_pairs={{0,1},{1,0},{2,3},{3,2},{4,5},{5,4},{6,7},{7,6},{8,9},{9,8},{10,11... | collective-permute-start | bytes 307208 | tf_op jit(solution)/shard_map/ppermute | solution.py:456
  66.9 10.8 %collective-permute-start.19 = (f32[736,128]{1,0:T(8,128)S(1)}, f32[736,128]{1,0:T(8,128)S(1)}, u32[]{:S(2)}, u32[]{:S(2)}) collective-permute-start(f32[736,128]{1,0:T(8,128)S(1)} %get-tuple-element.99), channel_id=1, source_target_pairs={{0,4},{4,0},{8,12},{12,8},{16,20},{20,16},{24,28},{28,24},{32,36},... | collective-permute-start | bytes 1130504 | tf_op jit(solution)/shard_map/ppermute | solution.py:470
  66.9 27.7 %collective-permute-start.24 = (f32[736,128]{1,0:T(8,128)S(1)}, f32[736,128]{1,0:T(8,128)S(1)}, u32[]{:S(2)}, u32[]{:S(2)}) collective-permute-start(f32[736,128]{1,0:T(8,128)S(1)} %get-tuple-element.105), channel_id=1, source_target_pairs={{0,252},{4,8},{8,4},{12,16},{16,12},{20,24},{24,20},{28,32},{32,28... | collective-permute-start | bytes 1130504 | tf_op jit(solution)/shard_map/ppermute | solution.py:470
  77.7 9.1 %collective-permute-start.20 = (f32[200,128]{1,0:T(8,128)S(1)}, f32[200,128]{1,0:T(8,128)S(1)}, u32[]{:S(2)}, u32[]{:S(2)}) collective-permute-start(f32[200,128]{1,0:T(8,128)S(1)} %get-tuple-element.101), channel_id=1, source_target_pairs={{0,2},{1,3},{2,0},{3,1},{4,6},{5,7},{6,4},{7,5},{8,10},{9,11},{10,... | collective-permute-start | bytes 307208 | tf_op jit(solution)/shard_map/ppermute | solution.py:456
  78.2 16.3 %collective-permute-start.21 = (f32[200,128]{1,0:T(8,128)S(1)}, f32[200,128]{1,0:T(8,128)S(1)}, u32[]{:S(2)}, u32[]{:S(2)}) collective-permute-start(f32[200,128]{1,0:T(8,128)S(1)} %get-tuple-element.102), channel_id=1, source_target_pairs={{0,3},{1,2},{2,1},{3,0},{4,7},{5,6},{6,5},{7,4},{8,11},{9,10},{10,... | collective-permute-start | bytes 307208 | tf_op jit(solution)/shard_map/ppermute | solution.py:456
  78.3 16.3 %collective-permute-start.22 = (f32[200,128]{1,0:T(8,128)S(1)}, f32[200,128]{1,0:T(8,128)S(1)}, u32[]{:S(2)}, u32[]{:S(2)}) collective-permute-start(f32[200,128]{1,0:T(8,128)S(1)} %get-tuple-element.103), channel_id=1, source_target_pairs={{0,1},{1,0},{2,3},{3,2},{4,5},{5,4},{6,7},{7,6},{8,9},{9,8},{10,11... | collective-permute-start | bytes 307208 | tf_op jit(solution)/shard_map/ppermute | solution.py:456
  79.9 16.9 %collective-permute-start.23 = (f32[736,128]{1,0:T(8,128)S(1)}, f32[736,128]{1,0:T(8,128)S(1)}, u32[]{:S(2)}, u32[]{:S(2)}) collective-permute-start(f32[736,128]{1,0:T(8,128)S(1)} %add.77), channel_id=1, source_target_pairs={{0,252},{4,8},{8,4},{12,16},{16,12},{20,24},{24,20},{28,32},{32,28... | collective-permute-start | bytes 1130504 | tf_op jit(solution)/shard_map/ppermute | solution.py:470
  94.6 11.0 %collective-permute-start.25 = (f32[736,128]{1,0:T(8,128)S(1)}, f32[736,128]{1,0:T(8,128)S(1)}, u32[]{:S(2)}, u32[]{:S(2)}) collective-permute-start(f32[736,128]{1,0:T(8,128)S(1)} %add.79), channel_id=1, source_target_pairs={{0,4},{4,0},{8,12},{12,8},{16,20},{20,16},{24,28},{28,24},{32,36},... | collective-permute-start | bytes 1130504 | tf_op jit(solution)/shard_map/ppermute | solution.py:470

commit v6 on v5

--- a/solution.py
+++ b/solution.py
@@ -505,9 +505,9 @@
     one = swapped(after(one, none), 1, 0)
     two = swapped(two, 1, 1)
     none = solve_pencils(none, 1, tables)
-    none = exchanged(after(none, one))
     four = swapped(one + four, 1, 1)
     three = swapped(two + after(three, none), 1, 0)
+    none = exchanged(none)
     kept = kept + four
     (self_share,) = gather_shares(none, 1, {0: own}, {0: [(0, 0)]}, tables)
     residual, intersection = leave(own, self_share, kept, three)

time: 107 us -> 102 us (0.953)
  the two profiles are of different devices: /device:TPU:16 before, /device:TPU:1 now
where the time goes in v6:
time: 102 us
  starting transfers between devices  55.5 us (54%)
  waiting for transfers between devices  22.1 us (22%)
  Pallas kernels  21.6 us (21%)
  local copies, waits for them, and re-layouts  1.58 us (2%)
    ppermute x8, starting transfers between devices, swapped(): return lax.ppermute(value, 'orb', pairs)  36.1 us
    ppermute x18, starting transfers between devices, exchanged(): received.append(lax.ppermute(chunk, 'grid', pairs))  19.4 us
    ppermute x18, waiting for transfers between devices, exchanged(): received.append(lax.ppermute(chunk, 'grid', pairs))  18.7 us
    pallas_call x3, Pallas kernels, gather_shares(): pl.pallas_call(lambda *refs: gather_kernel(count, parts, list(orbitals),...  9.01 us
    pallas_call x3, Pallas kernels, spread_pairs(): pl.pallas_call(lambda *refs: spread_kernel(pairs, list(orbitals), *refs),...  8.2 us
    pallas_call x3, Pallas kernels, solve_pencils(): pl.pallas_call(lambda *refs: pencil_kernel(count, parts, *refs), out_shap...  3.57 us
    ppermute x8, waiting for transfers between devices, swapped(): return lax.ppermute(value, 'orb', pairs)  3.41 us
  transfers between devices with their start and end apart: 26, of which 8 were waited for; matrix products, arithmetic and copies ran while one was open for 1% of the time, Pallas kernels for 20%

profile of v6, /device:TPU:1, one launch (start us, length us, event | category | flops | bytes accessed | tf_op | source)
XLA Modules:
  0.0 102.3 jit_solution(15553249222899436804)
XLA Ops:
  0.6 1.0 copy-done.4
  1.7 2.6 %collective-permute-start.1 = (f32[736,128]{1,0:T(8,128)S(1)}, f32[736,128]{1,0:T(8,128)S(1)}, u32[]{:S(2)}, u32[]{:S(2)}) collective-permute-start(f32[736,128]{1,0:T(8,128)S(1)} %enter.1.refs_1_.refs_7_.own), channel_id=1, source_target_pairs={{0,4},{4,0},{8,12},{12,8},{16,20},{20,16},{24,28},{28,24},{32,36},... | collective-permute-start | bytes 1130504 | tf_op jit(solution)/shard_map/ppermute | solution.py:470
  4.2 9.5 %collective-permute-start = (f32[736,128]{1,0:T(8,128)S(1)}, f32[736,128]{1,0:T(8,128)S(1)}, u32[]{:S(2)}, u32[]{:S(2)}) collective-permute-start(f32[736,128]{1,0:T(8,128)S(1)} %enter.1.refs_1_.refs_7_.own), channel_id=1, source_target_pairs={{0,252},{4,8},{8,4},{12,16},{16,12},{20,24},{24,20},{28,32},{32,28... | collective-permute-start | bytes 1130504 | tf_op jit(solution)/shard_map/ppermute | solution.py:470
  13.7 8.9 %collective-permute-start.2 = (f32[736,128]{1,0:T(8,128)S(1)}, f32[736,128]{1,0:T(8,128)S(1)}, u32[]{:S(2)}, u32[]{:S(2)}) collective-permute-start(f32[736,128]{1,0:T(8,128)S(1)} %collective-permute-done.1.refs_2_.refs_8_), channel_id=1, source_target_pairs={{0,252},{4,8},{8,4},{12,16},{16,12},{20,24},{24,20},{28,32},{32,28... | collective-permute-start | bytes 1130504 | tf_op jit(solution)/shard_map/ppermute | solution.py:470
  22.6 0.1 pad_add_fusion.refs_0_
  22.7 3.1 %spread.3 = (f32[384,128]{1,0:T(8,128)S(1)}, f32[384,128]{1,0:T(8,128)S(1)}, f32[384,128]{1,0:T(8,128)S(1)}, f32[384,128]{1,0:T(8,128)S(1)}) custom-call(s32[2]{0:T(128)S(1)} %pad_add_fusion.refs_0_, f32[736,128]{1,0:T(8,128)S(1)} %enter.1.refs_1_.refs_7_.own, f32[736,128]{1,0:T(8,128)S(1)} %collective-permute-done.1.refs_2_.refs_8_, ...), custom_call_target="tpu_custom_call" | custom-call | tf_op jit(solution)/shard_map/spread/pallas_call | solution.py:392
  25.8 0.5 collective-permute-start.4
  26.4 3.1 %collective-permute-start.5 = (f32[384,128]{1,0:T(8,128)S(1)}, f32[384,128]{1,0:T(8,128)S(1)}, u32[]{:S(2)}, u32[]{:S(2)}) collective-permute-start(f32[384,128]{1,0:T(8,128)S(1)} %get-tuple-element.54), channel_id=1, source_target_pairs={{0,3},{1,2},{2,1},{3,0},{4,7},{5,6},{6,5},{7,4},{8,11},{9,10},{10,... | collective-permute-start | bytes 589832 | tf_op jit(solution)/shard_map/ppermute | solution.py:456
  29.5 0.6 collective-permute-done.2.refs_4_.refs_10_
  30.1 0.9 collective-permute-done.3.refs_3_.refs_9_
  31.0 3.2 %spread.4 = (f32[384,128]{1,0:T(8,128)S(1)}, f32[384,128]{1,0:T(8,128)S(1)}, f32[384,128]{1,0:T(8,128)S(1)}, f32[384,128]{1,0:T(8,128)S(1)}) custom-call(s32[2]{0:T(128)S(1)} %pad_add_fusion.refs_0_, f32[736,128]{1,0:T(8,128)S(1)} %collective-permute-done.refs_3_.refs_1_.refs_9_.refs_7_, f32[736,128]{1,0:T(8,128)S(1)} %collective-permute-done.1.refs_2_.refs_8_, ...), custom_call_target="tpu_custom_call" | custom-call | tf_op jit(solution)/shard_map/spread/pallas_call | solution.py:392
  34.2 0.5 collective-permute-start.16
  34.7 4.0 %collective-permute-start.17 = (f32[384,128]{1,0:T(8,128)S(1)}, f32[384,128]{1,0:T(8,128)S(1)}, u32[]{:S(2)}, u32[]{:S(2)}) collective-permute-start(f32[384,128]{1,0:T(8,128)S(1)} %get-tuple-element.60), channel_id=1, source_target_pairs={{0,3},{1,2},{2,1},{3,0},{4,7},{5,6},{6,5},{7,4},{8,11},{9,10},{10,... | collective-permute-start | bytes 589832 | tf_op jit(solution)/shard_map/ppermute | solution.py:456
  38.7 0.4 fusion.refs_5_
  39.1 0.5 copy-done.1
  39.6 0.1 copy-done.2
  39.7 1.3 %pencils.3 = (f32[384,128]{1,0:T(8,128)S(1)}, f32[384,128]{1,0:T(8,128)S(1)}, f32[384,128]{1,0:T(8,128)S(1)}, f32[384,128]{1,0:T(8,128)S(1)}) custom-call(s32[2]{0:T(128)S(1)} %pad_add_fusion.refs_0_, f32[384,128]{1,0:T(8,128)S(1)} %get-tuple-element.52.refs_1_, f32[384,128]{1,0:T(8,128)S(1)} %collective-permute-done.4.refs_2_, ...), custom_call_target="tpu_custom_call" | custom-call | tf_op jit(solution)/shard_map/pencils/pallas_call | solution.py:405
  41.0 0.5 collective-permute-start.7
  41.4 1.7 %collective-permute-start.8 = (f32[384,128]{1,0:T(8,128)S(1)}, f32[384,128]{1,0:T(8,128)S(1)}, u32[]{:S(2)}, u32[]{:S(2)}) collective-permute-start(f32[384,128]{1,0:T(8,128)S(1)} %get-tuple-element.69), channel_id=1, source_target_pairs={{0,3},{1,2},{2,1},{3,0},{4,7},{5,6},{6,5},{7,4},{8,11},{9,10},{10,... | collective-permute-start | bytes 589832 | tf_op jit(solution)/shard_map/ppermute | solution.py:456
  43.2 1.9 %spread.5 = (f32[200,128]{1,0:T(8,128)S(1)}, f32[200,128]{1,0:T(8,128)S(1)}, f32[200,128]{1,0:T(8,128)S(1)}, f32[200,128]{1,0:T(8,128)S(1)}) custom-call(s32[2]{0:T(128)S(1)} %pad_add_fusion.refs_0_, f32[736,128]{1,0:T(8,128)S(1)} %enter.1.refs_1_.refs_7_.own, bf16[256,256]{1,0:T(8,128)(2,1)S(1)} %copy-done, bf16[80,240]{1,0:T(8,128)(2,1)S(1)} %copy-done.3), custom_call_target="tpu_custom_call" | custom-call | tf_op jit(solution)/shard_map/spread/pallas_call | solution.py:392
  45.1 0.3 collective-permute-start.9
  45.4 3.0 %collective-permute-done.17.refs_3_ = f32[384,128]{1,0:T(8,128)S(1)} collective-permute-done((f32[384,128]{1,0:T(8,128)S(1)}, f32[384,128]{1,0:T(8,128)S(1)}, u32[]{:S(2)}, u32[]{:S(2)}) %collective-permute-start.17) | collective-permute-done | bytes 196640 | tf_op jit(solution)/shard_map/ppermute | solution.py:456
  48.4 1.3 %pencils.5 = (f32[384,128]{1,0:T(8,128)S(1)}, f32[384,128]{1,0:T(8,128)S(1)}, f32[384,128]{1,0:T(8,128)S(1)}, f32[384,128]{1,0:T(8,128)S(1)}) custom-call(s32[2]{0:T(128)S(1)} %pad_add_fusion.refs_0_, f32[384,128]{1,0:T(8,128)S(1)} %get-tuple-element.80.refs_1_, f32[384,128]{1,0:T(8,128)S(1)} %collective-permute-done.16.refs_2_, ...), custom_call_target="tpu_custom_call" | custom-call | tf_op jit(solution)/shard_map/pencils/pallas_call | solution.py:405
  49.7 0.5 collective-permute-start.19
  50.2 0.1 collective-permute-start.20
  50.3 3.0 %collective-permute-start.21 = (f32[384,128]{1,0:T(8,128)S(1)}, f32[384,128]{1,0:T(8,128)S(1)}, u32[]{:S(2)}, u32[]{:S(2)}) collective-permute-start(f32[384,128]{1,0:T(8,128)S(1)} %get-tuple-element.87), channel_id=1, source_target_pairs={{0,1},{1,0},{2,3},{3,2},{4,5},{5,4},{6,7},{7,6},{8,9},{9,8},{10,11... | collective-permute-start | bytes 589832 | tf_op jit(solution)/shard_map/ppermute | solution.py:456
  53.3 3.5 %collective-permute-done.8.refs_3_ = f32[384,128]{1,0:T(8,128)S(1)} collective-permute-done((f32[384,128]{1,0:T(8,128)S(1)}, f32[384,128]{1,0:T(8,128)S(1)}, u32[]{:S(2)}, u32[]{:S(2)}) %collective-permute-start.8) | collective-permute-done | bytes 196640 | tf_op jit(solution)/shard_map/ppermute | solution.py:456
  56.8 3.4 %gather.3 = (f32[736,128]{1,0:T(8,128)S(1)}, f32[736,128]{1,0:T(8,128)S(1)}, f32[736,128]{1,0:T(8,128)S(1)}) custom-call(s32[2]{0:T(128)S(1)} %pad_add_fusion.refs_0_, f32[384,128]{1,0:T(8,128)S(1)} %get-tuple-element.67.refs_1_, f32[384,128]{1,0:T(8,128)S(1)} %collective-permute-done.7.refs_2_, f32[384,128]{1,0:T(8,128)S(1)} %collective-permute-done.8.refs_3_, ...), custom_call_target="tpu_custom_call" | custom-call | tf_op jit(solution)/shard_map/gather/pallas_call | solution.py:417
  60.3 0.5 collective-permute-start.10
  60.8 0.1 collective-permute-start.11
  60.9 1.3 %collective-permute-start.12 = (f32[200,128]{1,0:T(8,128)S(1)}, f32[200,128]{1,0:T(8,128)S(1)}, u32[]{:S(2)}, u32[]{:S(2)}) collective-permute-start(f32[200,128]{1,0:T(8,128)S(1)} %get-tuple-element.75), channel_id=1, source_target_pairs={{0,1},{1,0},{2,3},{3,2},{4,5},{5,4},{6,7},{7,6},{8,9},{9,8},{10,11... | collective-permute-start | bytes 307208 | tf_op jit(solution)/shard_map/ppermute | solution.py:456
  62.2 2.4 %collective-permute-done.20.refs_3_ = f32[384,128]{1,0:T(8,128)S(1)} collective-permute-done((f32[384,128]{1,0:T(8,128)S(1)}, f32[384,128]{1,0:T(8,128)S(1)}, u32[]{:S(2)}, u32[]{:S(2)}) %collective-permute-start.20) | collective-permute-done | bytes 196640 | tf_op jit(solution)/shard_map/ppermute | solution.py:456
  64.6 3.5 %gather.5 = (f32[736,128]{1,0:T(8,128)S(1)}, f32[736,128]{1,0:T(8,128)S(1)}, f32[736,128]{1,0:T(8,128)S(1)}, f32[736,128]{1,0:T(8,128)S(1)}) custom-call(s32[2]{0:T(128)S(1)} %pad_add_fusion.refs_0_, f32[384,128]{1,0:T(8,128)S(1)} %get-tuple-element.88.refs_1_, f32[384,128]{1,0:T(8,128)S(1)} %collective-permute-done.19.refs_2_, ...), custom_call_target="tpu_custom_call" | custom-call | tf_op jit(solution)/shard_map/gather/pallas_call | solution.py:417
  68.2 0.2 collective-permute-start.22
  68.4 7.7 %collective-permute-start.24 = (f32[736,128]{1,0:T(8,128)S(1)}, f32[736,128]{1,0:T(8,128)S(1)}, u32[]{:S(2)}, u32[]{:S(2)}) collective-permute-start(f32[736,128]{1,0:T(8,128)S(1)} %get-tuple-element.97), channel_id=1, source_target_pairs={{0,252},{4,8},{8,4},{12,16},{16,12},{20,24},{24,20},{28,32},{32,28... | collective-permute-start | bytes 1130504 | tf_op jit(solution)/shard_map/ppermute | solution.py:470
  76.1 1.0 %pencils.4 = (f32[200,128]{1,0:T(8,128)S(1)}, f32[200,128]{1,0:T(8,128)S(1)}, f32[200,128]{1,0:T(8,128)S(1)}, f32[200,128]{1,0:T(8,128)S(1)}) custom-call(s32[2]{0:T(128)S(1)} %pad_add_fusion.refs_0_, f32[200,128]{1,0:T(8,128)S(1)} %get-tuple-element.72.refs_1_, f32[200,128]{1,0:T(8,128)S(1)} %collective-permute-done.10.refs_2_, ...), custom_call_target="tpu_custom_call" | custom-call | tf_op jit(solution)/shard_map/pencils/pallas_call | solution.py:405
  77.1 1.8 %collective-permute-done.22 = f32[736,128]{1,0:T(8,128)S(1)} collective-permute-done((f32[736,128]{1,0:T(8,128)S(1)}, f32[736,128]{1,0:T(8,128)S(1)}, u32[]{:S(2)}, u32[]{:S(2)}) %collective-permute-start.22) | collective-permute-done | bytes 376864 | tf_op jit(solution)/shard_map/ppermute | solution.py:470
  79.0 0.1 add.77
  79.1 7.1 %collective-permute-start.23 = (f32[736,128]{1,0:T(8,128)S(1)}, f32[736,128]{1,0:T(8,128)S(1)}, u32[]{:S(2)}, u32[]{:S(2)}) collective-permute-start(f32[736,128]{1,0:T(8,128)S(1)} %add.77), channel_id=1, source_target_pairs={{0,252},{4,8},{8,4},{12,16},{16,12},{20,24},{24,20},{28,32},{32,28... | collective-permute-start | bytes 1130504 | tf_op jit(solution)/shard_map/ppermute | solution.py:470
  86.2 0.1 add.79
  86.3 0.1 collective-permute-start.25
  86.4 0.2 collective-permute-start.13
  86.6 3.0 %collective-permute-start.14 = (f32[200,128]{1,0:T(8,128)S(1)}, f32[200,128]{1,0:T(8,128)S(1)}, u32[]{:S(2)}, u32[]{:S(2)}) collective-permute-start(f32[200,128]{1,0:T(8,128)S(1)} %get-tuple-element.78), channel_id=1, source_target_pairs={{0,3},{1,2},{2,1},{3,0},{4,7},{5,6},{6,5},{7,4},{8,11},{9,10},{10,... | collective-permute-start | bytes 307208 | tf_op jit(solution)/shard_map/ppermute | solution.py:456
  89.6 7.5 %collective-permute-done.13.refs_2_ = f32[200,128]{1,0:T(8,128)S(1)} collective-permute-done((f32[200,128]{1,0:T(8,128)S(1)}, f32[200,128]{1,0:T(8,128)S(1)}, u32[]{:S(2)}, u32[]{:S(2)}) %collective-permute-start.13) | collective-permute-done | bytes 102432 | tf_op jit(solution)/shard_map/ppermute | solution.py:456
  97.1 2.2 %collective-permute-done.14.refs_3_ = f32[200,128]{1,0:T(8,128)S(1)} collective-permute-done((f32[200,128]{1,0:T(8,128)S(1)}, f32[200,128]{1,0:T(8,128)S(1)}, u32[]{:S(2)}, u32[]{:S(2)}) %collective-permute-start.14) | collective-permute-done | bytes 102432 | tf_op jit(solution)/shard_map/ppermute | solution.py:456
  99.3 2.0 %gather.4.refs_0_ = f32[736,128]{1,0:T(8,128)S(1)} custom-call(s32[2]{0:T(128)S(1)} %pad_add_fusion.refs_0_, f32[200,128]{1,0:T(8,128)S(1)} %get-tuple-element.76.refs_1_, f32[200,128]{1,0:T(8,128)S(1)} %collective-permute-done.13.refs_2_, f32[200,128]{1,0:T(8,128)S(1)} %collective-permute-done.14.refs_3_, f32[200,128]{1,0:T(8,128)S(1)} %collective-permute-done.15.refs_4_, ...), custom_call_target="tpu_custom_call" | custom-call | tf_op jit(solution)/shard_map/gather/pallas_call | solution.py:417
  101.4 0.1 add.78.refs_1_
  101.4 0.8 leave.1
  (32 shorter events, 0.2 us)
Async XLA Ops:
  0.6 1.0 copy-start.4
  1.6 21.1 %copy-start = (bf16[256,256]{1,0:T(8,128)(2,1)S(1)}, bf16[256,256]{1,0:T(8,128)(2,1)}, u32[]{:S(2)}) copy-start(bf16[256,256]{1,0:T(8,128)(2,1)} %constant.72.clone.refs_4_.refs_5_.refs_2_) | copy-start | bytes 393220
  1.6 21.0 %copy-start.3 = (bf16[80,240]{1,0:T(8,128)(2,1)S(1)}, bf16[80,240]{1,0:T(8,128)(2,1)}, u32[]{:S(2)}) copy-start(bf16[80,240]{1,0:T(8,128)(2,1)} %constant.73.clone.refs_5_.refs_6_.refs_3_) | copy-start | bytes 115204
  1.7 12.0 %collective-permute-start.1 = (f32[736,128]{1,0:T(8,128)S(1)}, f32[736,128]{1,0:T(8,128)S(1)}, u32[]{:S(2)}, u32[]{:S(2)}) collective-permute-start(f32[736,128]{1,0:T(8,128)S(1)} %enter.1.refs_1_.refs_7_.own), channel_id=1, source_target_pairs={{0,4},{4,0},{8,12},{12,8},{16,20},{20,16},{24,28},{28,24},{32,36},... | collective-permute-start | bytes 1130504 | tf_op jit(solution)/shard_map/ppermute | solution.py:470
  4.2 18.4 %collective-permute-start = (f32[736,128]{1,0:T(8,128)S(1)}, f32[736,128]{1,0:T(8,128)S(1)}, u32[]{:S(2)}, u32[]{:S(2)}) collective-permute-start(f32[736,128]{1,0:T(8,128)S(1)} %enter.1.refs_1_.refs_7_.own), channel_id=1, source_target_pairs={{0,252},{4,8},{8,4},{12,16},{16,12},{20,24},{24,20},{28,32},{32,28... | collective-permute-start | bytes 1130504 | tf_op jit(solution)/shard_map/ppermute | solution.py:470
  13.7 16.4 %collective-permute-start.2 = (f32[736,128]{1,0:T(8,128)S(1)}, f32[736,128]{1,0:T(8,128)S(1)}, u32[]{:S(2)}, u32[]{:S(2)}) collective-permute-start(f32[736,128]{1,0:T(8,128)S(1)} %collective-permute-done.1.refs_2_.refs_8_), channel_id=1, source_target_pairs={{0,252},{4,8},{8,4},{12,16},{16,12},{20,24},{24,20},{28,32},{32,28... | collective-permute-start | bytes 1130504 | tf_op jit(solution)/shard_map/ppermute | solution.py:470
  22.6 8.4 %collective-permute-start.3 = (f32[736,128]{1,0:T(8,128)S(1)}, f32[736,128]{1,0:T(8,128)S(1)}, u32[]{:S(2)}, u32[]{:S(2)}) collective-permute-start(f32[736,128]{1,0:T(8,128)S(1)} %collective-permute-done.refs_3_.refs_1_.refs_9_.refs_7_), channel_id=1, source_target_pairs={{0,4},{4,0},{8,12},{12,8},{16,20},{20,16},{24,28},{28,24},{32,36},... | collective-permute-start | bytes 1130504 | tf_op jit(solution)/shard_map/ppermute | solution.py:470
  25.8 12.8 %collective-permute-start.4 = (f32[384,128]{1,0:T(8,128)S(1)}, f32[384,128]{1,0:T(8,128)S(1)}, u32[]{:S(2)}, u32[]{:S(2)}) collective-permute-start(f32[384,128]{1,0:T(8,128)S(1)} %get-tuple-element.53), channel_id=1, source_target_pairs={{0,2},{1,3},{2,0},{3,1},{4,6},{5,7},{6,4},{7,5},{8,10},{9,11},{10,... | collective-permute-start | bytes 589832 | tf_op jit(solution)/shard_map/ppermute | solution.py:456
  26.4 12.8 %collective-permute-start.5 = (f32[384,128]{1,0:T(8,128)S(1)}, f32[384,128]{1,0:T(8,128)S(1)}, u32[]{:S(2)}, u32[]{:S(2)}) collective-permute-start(f32[384,128]{1,0:T(8,128)S(1)} %get-tuple-element.54), channel_id=1, source_target_pairs={{0,3},{1,2},{2,1},{3,0},{4,7},{5,6},{6,5},{7,4},{8,11},{9,10},{10,... | collective-permute-start | bytes 589832 | tf_op jit(solution)/shard_map/ppermute | solution.py:456
  29.5 9.6 %collective-permute-start.6 = (f32[384,128]{1,0:T(8,128)S(1)}, f32[384,128]{1,0:T(8,128)S(1)}, u32[]{:S(2)}, u32[]{:S(2)}) collective-permute-start(f32[384,128]{1,0:T(8,128)S(1)} %get-tuple-element.55), channel_id=1, source_target_pairs={{0,1},{1,0},{2,3},{3,2},{4,5},{5,4},{6,7},{7,6},{8,9},{9,8},{10,11... | collective-permute-start | bytes 589832 | tf_op jit(solution)/shard_map/ppermute | solution.py:456
  34.2 10.9 %collective-permute-start.16 = (f32[384,128]{1,0:T(8,128)S(1)}, f32[384,128]{1,0:T(8,128)S(1)}, u32[]{:S(2)}, u32[]{:S(2)}) collective-permute-start(f32[384,128]{1,0:T(8,128)S(1)} %get-tuple-element.59), channel_id=1, source_target_pairs={{0,2},{1,3},{2,0},{3,1},{4,6},{5,7},{6,4},{7,5},{8,10},{9,11},{10,... | collective-permute-start | bytes 589832 | tf_op jit(solution)/shard_map/ppermute | solution.py:456
  34.7 13.7 %collective-permute-start.17 = (f32[384,128]{1,0:T(8,128)S(1)}, f32[384,128]{1,0:T(8,128)S(1)}, u32[]{:S(2)}, u32[]{:S(2)}) collective-permute-start(f32[384,128]{1,0:T(8,128)S(1)} %get-tuple-element.60), channel_id=1, source_target_pairs={{0,3},{1,2},{2,1},{3,0},{4,7},{5,6},{6,5},{7,4},{8,11},{9,10},{10,... | collective-permute-start | bytes 589832 | tf_op jit(solution)/shard_map/ppermute | solution.py:456
  38.7 9.7 %collective-permute-start.18 = (f32[384,128]{1,0:T(8,128)S(1)}, f32[384,128]{1,0:T(8,128)S(1)}, u32[]{:S(2)}, u32[]{:S(2)}) collective-permute-start(f32[384,128]{1,0:T(8,128)S(1)} %get-tuple-element.61), channel_id=1, source_target_pairs={{0,1},{1,0},{2,3},{3,2},{4,5},{5,4},{6,7},{7,6},{8,9},{9,8},{10,11... | collective-permute-start | bytes 589832 | tf_op jit(solution)/shard_map/ppermute | solution.py:456
  38.7 0.9 copy-start.1
  38.7 1.0 copy-start.2
  41.0 9.3 %collective-permute-start.7 = (f32[384,128]{1,0:T(8,128)S(1)}, f32[384,128]{1,0:T(8,128)S(1)}, u32[]{:S(2)}, u32[]{:S(2)}) collective-permute-start(f32[384,128]{1,0:T(8,128)S(1)} %get-tuple-element.68), channel_id=1, source_target_pairs={{0,2},{1,3},{2,0},{3,1},{4,6},{5,7},{6,4},{7,5},{8,10},{9,11},{10,... | collective-permute-start | bytes 589832 | tf_op jit(solution)/shard_map/ppermute | solution.py:456
  41.4 15.4 %collective-permute-start.8 = (f32[384,128]{1,0:T(8,128)S(1)}, f32[384,128]{1,0:T(8,128)S(1)}, u32[]{:S(2)}, u32[]{:S(2)}) collective-permute-start(f32[384,128]{1,0:T(8,128)S(1)} %get-tuple-element.69), channel_id=1, source_target_pairs={{0,3},{1,2},{2,1},{3,0},{4,7},{5,6},{6,5},{7,4},{8,11},{9,10},{10,... | collective-permute-start | bytes 589832 | tf_op jit(solution)/shard_map/ppermute | solution.py:456
  45.1 11.7 %collective-permute-start.9 = (f32[384,128]{1,0:T(8,128)S(1)}, f32[384,128]{1,0:T(8,128)S(1)}, u32[]{:S(2)}, u32[]{:S(2)}) collective-permute-start(f32[384,128]{1,0:T(8,128)S(1)} %get-tuple-element.70), channel_id=1, source_target_pairs={{0,1},{1,0},{2,3},{3,2},{4,5},{5,4},{6,7},{7,6},{8,9},{9,8},{10,11... | collective-permute-start | bytes 589832 | tf_op jit(solution)/shard_map/ppermute | solution.py:456
  49.7 11.2 %collective-permute-start.19 = (f32[384,128]{1,0:T(8,128)S(1)}, f32[384,128]{1,0:T(8,128)S(1)}, u32[]{:S(2)}, u32[]{:S(2)}) collective-permute-start(f32[384,128]{1,0:T(8,128)S(1)} %get-tuple-element.85), channel_id=1, source_target_pairs={{0,2},{1,3},{2,0},{3,1},{4,6},{5,7},{6,4},{7,5},{8,10},{9,11},{10,... | collective-permute-start | bytes 589832 | tf_op jit(solution)/shard_map/ppermute | solution.py:456
  50.2 14.5 %collective-permute-start.20 = (f32[384,128]{1,0:T(8,128)S(1)}, f32[384,128]{1,0:T(8,128)S(1)}, u32[]{:S(2)}, u32[]{:S(2)}) collective-permute-start(f32[384,128]{1,0:T(8,128)S(1)} %get-tuple-element.86), channel_id=1, source_target_pairs={{0,3},{1,2},{2,1},{3,0},{4,7},{5,6},{6,5},{7,4},{8,11},{9,10},{10,... | collective-permute-start | bytes 589832 | tf_op jit(solution)/shard_map/ppermute | solution.py:456
  50.3 14.3 %collective-permute-start.21 = (f32[384,128]{1,0:T(8,128)S(1)}, f32[384,128]{1,0:T(8,128)S(1)}, u32[]{:S(2)}, u32[]{:S(2)}) collective-permute-start(f32[384,128]{1,0:T(8,128)S(1)} %get-tuple-element.87), channel_id=1, source_target_pairs={{0,1},{1,0},{2,3},{3,2},{4,5},{5,4},{6,7},{7,6},{8,9},{9,8},{10,11... | collective-permute-start | bytes 589832 | tf_op jit(solution)/shard_map/ppermute | solution.py:456
  60.3 7.9 %collective-permute-start.10 = (f32[200,128]{1,0:T(8,128)S(1)}, f32[200,128]{1,0:T(8,128)S(1)}, u32[]{:S(2)}, u32[]{:S(2)}) collective-permute-start(f32[200,128]{1,0:T(8,128)S(1)} %get-tuple-element.73), channel_id=1, source_target_pairs={{0,2},{1,3},{2,0},{3,1},{4,6},{5,7},{6,4},{7,5},{8,10},{9,11},{10,... | collective-permute-start | bytes 307208 | tf_op jit(solution)/shard_map/ppermute | solution.py:456
  60.8 7.4 %collective-permute-start.11 = (f32[200,128]{1,0:T(8,128)S(1)}, f32[200,128]{1,0:T(8,128)S(1)}, u32[]{:S(2)}, u32[]{:S(2)}) collective-permute-start(f32[200,128]{1,0:T(8,128)S(1)} %get-tuple-element.74), channel_id=1, source_target_pairs={{0,3},{1,2},{2,1},{3,0},{4,7},{5,6},{6,5},{7,4},{8,11},{9,10},{10,... | collective-permute-start | bytes 307208 | tf_op jit(solution)/shard_map/ppermute | solution.py:456
  60.9 7.3 %collective-permute-start.12 = (f32[200,128]{1,0:T(8,128)S(1)}, f32[200,128]{1,0:T(8,128)S(1)}, u32[]{:S(2)}, u32[]{:S(2)}) collective-permute-start(f32[200,128]{1,0:T(8,128)S(1)} %get-tuple-element.75), channel_id=1, source_target_pairs={{0,1},{1,0},{2,3},{3,2},{4,5},{5,4},{6,7},{7,6},{8,9},{9,8},{10,11... | collective-permute-start | bytes 307208 | tf_op jit(solution)/shard_map/ppermute | solution.py:456
  68.2 10.8 %collective-permute-start.22 = (f32[736,128]{1,0:T(8,128)S(1)}, f32[736,128]{1,0:T(8,128)S(1)}, u32[]{:S(2)}, u32[]{:S(2)}) collective-permute-start(f32[736,128]{1,0:T(8,128)S(1)} %get-tuple-element.95), channel_id=1, source_target_pairs={{0,4},{4,0},{8,12},{12,8},{16,20},{20,16},{24,28},{28,24},{32,36},... | collective-permute-start | bytes 1130504 | tf_op jit(solution)/shard_map/ppermute | solution.py:470
  68.4 17.8 %collective-permute-start.24 = (f32[736,128]{1,0:T(8,128)S(1)}, f32[736,128]{1,0:T(8,128)S(1)}, u32[]{:S(2)}, u32[]{:S(2)}) collective-permute-start(f32[736,128]{1,0:T(8,128)S(1)} %get-tuple-element.97), channel_id=1, source_target_pairs={{0,252},{4,8},{8,4},{12,16},{16,12},{20,24},{24,20},{28,32},{32,28... | collective-permute-start | bytes 1130504 | tf_op jit(solution)/shard_map/ppermute | solution.py:470
  79.1 22.3 %collective-permute-start.23 = (f32[736,128]{1,0:T(8,128)S(1)}, f32[736,128]{1,0:T(8,128)S(1)}, u32[]{:S(2)}, u32[]{:S(2)}) collective-permute-start(f32[736,128]{1,0:T(8,128)S(1)} %add.77), channel_id=1, source_target_pairs={{0,252},{4,8},{8,4},{12,16},{16,12},{20,24},{24,20},{28,32},{32,28... | collective-permute-start | bytes 1130504 | tf_op jit(solution)/shard_map/ppermute | solution.py:470
  86.3 15.2 %collective-permute-start.25 = (f32[736,128]{1,0:T(8,128)S(1)}, f32[736,128]{1,0:T(8,128)S(1)}, u32[]{:S(2)}, u32[]{:S(2)}) collective-permute-start(f32[736,128]{1,0:T(8,128)S(1)} %add.79), channel_id=1, source_target_pairs={{0,4},{4,0},{8,12},{12,8},{16,20},{20,16},{24,28},{28,24},{32,36},... | collective-permute-start | bytes 1130504 | tf_op jit(solution)/shard_map/ppermute | solution.py:470
  86.4 10.8 %collective-permute-start.13 = (f32[200,128]{1,0:T(8,128)S(1)}, f32[200,128]{1,0:T(8,128)S(1)}, u32[]{:S(2)}, u32[]{:S(2)}) collective-permute-start(f32[200,128]{1,0:T(8,128)S(1)} %get-tuple-element.77), channel_id=1, source_target_pairs={{0,2},{1,3},{2,0},{3,1},{4,6},{5,7},{6,4},{7,5},{8,10},{9,11},{10,... | collective-permute-start | bytes 307208 | tf_op jit(solution)/shard_map/ppermute | solution.py:456
  86.6 12.8 %collective-permute-start.14 = (f32[200,128]{1,0:T(8,128)S(1)}, f32[200,128]{1,0:T(8,128)S(1)}, u32[]{:S(2)}, u32[]{:S(2)}) collective-permute-start(f32[200,128]{1,0:T(8,128)S(1)} %get-tuple-element.78), channel_id=1, source_target_pairs={{0,3},{1,2},{2,1},{3,0},{4,7},{5,6},{6,5},{7,4},{8,11},{9,10},{10,... | collective-permute-start | bytes 307208 | tf_op jit(solution)/shard_map/ppermute | solution.py:456
  89.6 9.7 %collective-permute-start.15 = (f32[200,128]{1,0:T(8,128)S(1)}, f32[200,128]{1,0:T(8,128)S(1)}, u32[]{:S(2)}, u32[]{:S(2)}) collective-permute-start(f32[200,128]{1,0:T(8,128)S(1)} %get-tuple-element.79), channel_id=1, source_target_pairs={{0,1},{1,0},{2,3},{3,2},{4,5},{5,4},{6,7},{7,6},{8,9},{9,8},{10,11... | collective-permute-start | bytes 307208 | tf_op jit(solution)/shard_map/ppermute | solution.py:456

commit v7 on v4

--- a/solution.py
+++ b/solution.py
@@ -485,7 +485,7 @@
     close = {0: own, (1, 0): first, (1, 1): second}
     near = spread_pairs(close, [(0, 1), (-1, 1)], tables)
     third, fourth = after((third, fourth), near)
-    wide = {(1, 0): first, (1, 1): second, (2, 0): third, (2, 1): fourth}
+    wide = {(1, 1): second, (1, 0): first, (2, 1): fourth, (2, 0): third}
     far = spread_pairs(wide, [(-1, 2), (-2, 2)], tables)
     none = spread_pairs({0: after(own, far)}, [(0, 0)], tables)
     near = solve_pencils(exchanged(near), 2, tables)

time: 102 us -> 102 us (level)
  no operation moved by 1% of the time
where the time goes in v7:
time: 102 us; the launch traced here: 101 us
  starting transfers between devices  54.3 us (53%)
  waiting for transfers between devices  23.1 us (23%)
  Pallas kernels  21.7 us (21%)
  local copies, waits for them, and re-layouts  1.23 us (1%)
    ppermute x8, starting transfers between devices, swapped(): return lax.ppermute(value, 'orb', pairs)  36.5 us
    ppermute x18, starting transfers between devices, exchanged(): received.append(lax.ppermute(chunk, 'grid', pairs))  17.7 us
    ppermute x18, waiting for transfers between devices, exchanged(): received.append(lax.ppermute(chunk, 'grid', pairs))  12 us
    ppermute x8, waiting for transfers between devices, swapped(): return lax.ppermute(value, 'orb', pairs)  11.1 us
    pallas_call x3, Pallas kernels, gather_shares(): pl.pallas_call(lambda *refs: gather_kernel(count, parts, list(orbitals),...  9.04 us
    pallas_call x3, Pallas kernels, spread_pairs(): pl.pallas_call(lambda *refs: spread_kernel(pairs, list(orbitals), *refs),...  8.18 us
    pallas_call x3, Pallas kernels, solve_pencils(): pl.pallas_call(lambda *refs: pencil_kernel(count, parts, *refs), out_shap...  3.58 us
  transfers between devices with their start and end apart: 26, of which 11 were waited for; matrix products, arithmetic and copies ran while one was open for 0% of the time, Pallas kernels for 20%

profile of v7, /device:TPU:1, one launch (start us, length us, event | category | flops | bytes accessed | tf_op | source)
XLA Modules:
  0.0 101.5 jit_solution(5728503702313795815)
XLA Ops:
  0.6 1.0 copy-done.4
  1.7 2.6 %collective-permute-start.1 = (f32[736,128]{1,0:T(8,128)S(1)}, f32[736,128]{1,0:T(8,128)S(1)}, u32[]{:S(2)}, u32[]{:S(2)}) collective-permute-start(f32[736,128]{1,0:T(8,128)S(1)} %enter.1.refs_1_.refs_7_.own), channel_id=1, source_target_pairs={{0,4},{4,0},{8,12},{12,8},{16,20},{20,16},{24,28},{28,24},{32,36},... | collective-permute-start | bytes 1130504 | tf_op jit(solution)/shard_map/ppermute | solution.py:466
  4.2 9.5 %collective-permute-start = (f32[736,128]{1,0:T(8,128)S(1)}, f32[736,128]{1,0:T(8,128)S(1)}, u32[]{:S(2)}, u32[]{:S(2)}) collective-permute-start(f32[736,128]{1,0:T(8,128)S(1)} %enter.1.refs_1_.refs_7_.own), channel_id=1, source_target_pairs={{0,252},{4,8},{8,4},{12,16},{16,12},{20,24},{24,20},{28,32},{32,28... | collective-permute-start | bytes 1130504 | tf_op jit(solution)/shard_map/ppermute | solution.py:466
  13.7 8.9 %collective-permute-start.2 = (f32[736,128]{1,0:T(8,128)S(1)}, f32[736,128]{1,0:T(8,128)S(1)}, u32[]{:S(2)}, u32[]{:S(2)}) collective-permute-start(f32[736,128]{1,0:T(8,128)S(1)} %collective-permute-done.1.refs_2_.refs_8_), channel_id=1, source_target_pairs={{0,252},{4,8},{8,4},{12,16},{16,12},{20,24},{24,20},{28,32},{32,28... | collective-permute-start | bytes 1130504 | tf_op jit(solution)/shard_map/ppermute | solution.py:466
  22.7 3.1 %spread.3 = (f32[400,128]{1,0:T(8,128)S(1)}, f32[400,128]{1,0:T(8,128)S(1)}, f32[400,128]{1,0:T(8,128)S(1)}, f32[400,128]{1,0:T(8,128)S(1)}) custom-call(s32[2]{0:T(128)S(1)} %pad_add_fusion.refs_0_, f32[736,128]{1,0:T(8,128)S(1)} %enter.1.refs_1_.refs_7_.own, f32[736,128]{1,0:T(8,128)S(1)} %collective-permute-done.1.refs_2_.refs_8_, ...), custom_call_target="tpu_custom_call" | custom-call | tf_op jit(solution)/shard_map/spread/pallas_call | solution.py:388
  25.8 0.5 collective-permute-start.4
  26.3 3.1 %collective-permute-start.5 = (f32[400,128]{1,0:T(8,128)S(1)}, f32[400,128]{1,0:T(8,128)S(1)}, u32[]{:S(2)}, u32[]{:S(2)}) collective-permute-start(f32[400,128]{1,0:T(8,128)S(1)} %get-tuple-element.58), channel_id=1, source_target_pairs={{0,3},{1,2},{2,1},{3,0},{4,7},{5,6},{6,5},{7,4},{8,11},{9,10},{10,... | collective-permute-start | bytes 614408 | tf_op jit(solution)/shard_map/ppermute | solution.py:452
  29.5 0.7 collective-permute-done.2.refs_4_.refs_10_
  30.1 0.9 collective-permute-done.3.refs_3_.refs_9_
  31.0 3.1 %spread.4 = (f32[400,128]{1,0:T(8,128)S(1)}, f32[400,128]{1,0:T(8,128)S(1)}, f32[400,128]{1,0:T(8,128)S(1)}, f32[400,128]{1,0:T(8,128)S(1)}) custom-call(s32[2]{0:T(128)S(1)} %pad_add_fusion.refs_0_, f32[736,128]{1,0:T(8,128)S(1)} %collective-permute-done.refs_3_.refs_1_.refs_9_.refs_7_, f32[736,128]{1,0:T(8,128)S(1)} %collective-permute-done.1.refs_2_.refs_8_, ...), custom_call_target="tpu_custom_call" | custom-call | tf_op jit(solution)/shard_map/spread/pallas_call | solution.py:388
  34.2 0.5 collective-permute-start.13
  34.7 4.0 %collective-permute-start.14 = (f32[400,128]{1,0:T(8,128)S(1)}, f32[400,128]{1,0:T(8,128)S(1)}, u32[]{:S(2)}, u32[]{:S(2)}) collective-permute-start(f32[400,128]{1,0:T(8,128)S(1)} %get-tuple-element.64), channel_id=1, source_target_pairs={{0,3},{1,2},{2,1},{3,0},{4,7},{5,6},{6,5},{7,4},{8,11},{9,10},{10,... | collective-permute-start | bytes 614408 | tf_op jit(solution)/shard_map/ppermute | solution.py:452
  38.7 0.2 fusion.refs_5_
  38.9 0.5 collective-permute-done.5.refs_3_
  39.5 0.1 copy-done.1
  39.6 0.1 copy-done.2
  39.7 1.3 %pencils.3 = (f32[400,128]{1,0:T(8,128)S(1)}, f32[400,128]{1,0:T(8,128)S(1)}, f32[400,128]{1,0:T(8,128)S(1)}, f32[400,128]{1,0:T(8,128)S(1)}) custom-call(s32[2]{0:T(128)S(1)} %pad_add_fusion.refs_0_, f32[400,128]{1,0:T(8,128)S(1)} %get-tuple-element.56.refs_1_, f32[400,128]{1,0:T(8,128)S(1)} %collective-permute-done.4.refs_2_, ...), custom_call_target="tpu_custom_call" | custom-call | tf_op jit(solution)/shard_map/pencils/pallas_call | solution.py:401
  40.9 0.5 collective-permute-start.7
  41.4 1.7 %collective-permute-start.8 = (f32[400,128]{1,0:T(8,128)S(1)}, f32[400,128]{1,0:T(8,128)S(1)}, u32[]{:S(2)}, u32[]{:S(2)}) collective-permute-start(f32[400,128]{1,0:T(8,128)S(1)} %get-tuple-element.73), channel_id=1, source_target_pairs={{0,3},{1,2},{2,1},{3,0},{4,7},{5,6},{6,5},{7,4},{8,11},{9,10},{10,... | collective-permute-start | bytes 614408 | tf_op jit(solution)/shard_map/ppermute | solution.py:452
  43.2 1.9 %spread.5 = (f32[200,128]{1,0:T(8,128)S(1)}, f32[200,128]{1,0:T(8,128)S(1)}, f32[200,128]{1,0:T(8,128)S(1)}, f32[200,128]{1,0:T(8,128)S(1)}) custom-call(s32[2]{0:T(128)S(1)} %pad_add_fusion.refs_0_, f32[736,128]{1,0:T(8,128)S(1)} %enter.1.refs_1_.refs_7_.own, bf16[256,256]{1,0:T(8,128)(2,1)S(1)} %copy-done, bf16[80,240]{1,0:T(8,128)(2,1)S(1)} %copy-done.3), custom_call_target="tpu_custom_call" | custom-call | tf_op jit(solution)/shard_map/spread/pallas_call | solution.py:388
  45.1 0.3 collective-permute-start.9
  45.4 3.3 %collective-permute-done.14.refs_3_ = f32[400,128]{1,0:T(8,128)S(1)} collective-permute-done((f32[400,128]{1,0:T(8,128)S(1)}, f32[400,128]{1,0:T(8,128)S(1)}, u32[]{:S(2)}, u32[]{:S(2)}) %collective-permute-start.14) | collective-permute-done | bytes 204832 | tf_op jit(solution)/shard_map/ppermute | solution.py:452
  48.7 1.3 %pencils.5 = (f32[400,128]{1,0:T(8,128)S(1)}, f32[400,128]{1,0:T(8,128)S(1)}, f32[400,128]{1,0:T(8,128)S(1)}, f32[400,128]{1,0:T(8,128)S(1)}) custom-call(s32[2]{0:T(128)S(1)} %pad_add_fusion.refs_0_, f32[400,128]{1,0:T(8,128)S(1)} %get-tuple-element.84.refs_1_, f32[400,128]{1,0:T(8,128)S(1)} %collective-permute-done.13.refs_2_, ...), custom_call_target="tpu_custom_call" | custom-call | tf_op jit(solution)/shard_map/pencils/pallas_call | solution.py:401
  50.0 0.5 collective-permute-start.16
  50.5 0.1 collective-permute-start.17
  50.6 0.5 collective-permute-done.7.refs_2_
  51.1 2.7 %collective-permute-start.18 = (f32[400,128]{1,0:T(8,128)S(1)}, f32[400,128]{1,0:T(8,128)S(1)}, u32[]{:S(2)}, u32[]{:S(2)}) collective-permute-start(f32[400,128]{1,0:T(8,128)S(1)} %get-tuple-element.91), channel_id=1, source_target_pairs={{0,1},{1,0},{2,3},{3,2},{4,5},{5,4},{6,7},{7,6},{8,9},{9,8},{10,11... | collective-permute-start | bytes 614408 | tf_op jit(solution)/shard_map/ppermute | solution.py:452
  53.8 3.7 %collective-permute-done.8.refs_3_ = f32[400,128]{1,0:T(8,128)S(1)} collective-permute-done((f32[400,128]{1,0:T(8,128)S(1)}, f32[400,128]{1,0:T(8,128)S(1)}, u32[]{:S(2)}, u32[]{:S(2)}) %collective-permute-start.8) | collective-permute-done | bytes 204832 | tf_op jit(solution)/shard_map/ppermute | solution.py:452
  57.5 3.4 %gather.3 = (f32[736,128]{1,0:T(8,128)S(1)}, f32[736,128]{1,0:T(8,128)S(1)}, f32[736,128]{1,0:T(8,128)S(1)}) custom-call(s32[2]{0:T(128)S(1)} %pad_add_fusion.refs_0_, f32[400,128]{1,0:T(8,128)S(1)} %get-tuple-element.71.refs_1_, f32[400,128]{1,0:T(8,128)S(1)} %collective-permute-done.7.refs_2_, f32[400,128]{1,0:T(8,128)S(1)} %collective-permute-done.8.refs_3_, ...), custom_call_target="tpu_custom_call" | custom-call | tf_op jit(solution)/shard_map/gather/pallas_call | solution.py:413
  61.0 0.5 collective-permute-start.10
  61.4 0.1 collective-permute-start.11
  61.6 1.3 %collective-permute-start.12 = (f32[200,128]{1,0:T(8,128)S(1)}, f32[200,128]{1,0:T(8,128)S(1)}, u32[]{:S(2)}, u32[]{:S(2)}) collective-permute-start(f32[200,128]{1,0:T(8,128)S(1)} %get-tuple-element.79), channel_id=1, source_target_pairs={{0,1},{1,0},{2,3},{3,2},{4,5},{5,4},{6,7},{7,6},{8,9},{9,8},{10,11... | collective-permute-start | bytes 307208 | tf_op jit(solution)/shard_map/ppermute | solution.py:452
  62.9 3.7 %collective-permute-done.17.refs_3_ = f32[400,128]{1,0:T(8,128)S(1)} collective-permute-done((f32[400,128]{1,0:T(8,128)S(1)}, f32[400,128]{1,0:T(8,128)S(1)}, u32[]{:S(2)}, u32[]{:S(2)}) %collective-permute-start.17) | collective-permute-done | bytes 204832 | tf_op jit(solution)/shard_map/ppermute | solution.py:452
  66.6 3.6 %gather.4 = (f32[736,128]{1,0:T(8,128)S(1)}, f32[736,128]{1,0:T(8,128)S(1)}, f32[736,128]{1,0:T(8,128)S(1)}, f32[736,128]{1,0:T(8,128)S(1)}) custom-call(s32[2]{0:T(128)S(1)} %pad_add_fusion.refs_0_, f32[400,128]{1,0:T(8,128)S(1)} %get-tuple-element.92.refs_1_, f32[400,128]{1,0:T(8,128)S(1)} %collective-permute-done.16.refs_2_, ...), custom_call_target="tpu_custom_call" | custom-call | tf_op jit(solution)/shard_map/gather/pallas_call | solution.py:413
  70.2 0.1 collective-permute-start.19
  70.3 7.2 %collective-permute-start.24 = (f32[736,128]{1,0:T(8,128)S(1)}, f32[736,128]{1,0:T(8,128)S(1)}, u32[]{:S(2)}, u32[]{:S(2)}) collective-permute-start(f32[736,128]{1,0:T(8,128)S(1)} %get-tuple-element.105), channel_id=1, source_target_pairs={{0,252},{4,8},{8,4},{12,16},{16,12},{20,24},{24,20},{28,32},{32,28... | collective-permute-start | bytes 1130504 | tf_op jit(solution)/shard_map/ppermute | solution.py:466
  77.5 1.0 %pencils.4 = (f32[200,128]{1,0:T(8,128)S(1)}, f32[200,128]{1,0:T(8,128)S(1)}, f32[200,128]{1,0:T(8,128)S(1)}, f32[200,128]{1,0:T(8,128)S(1)}) custom-call(s32[2]{0:T(128)S(1)} %pad_add_fusion.refs_0_, f32[200,128]{1,0:T(8,128)S(1)} %get-tuple-element.76.refs_1_, f32[200,128]{1,0:T(8,128)S(1)} %collective-permute-done.10.refs_2_, ...), custom_call_target="tpu_custom_call" | custom-call | tf_op jit(solution)/shard_map/pencils/pallas_call | solution.py:401
  78.6 1.8 %collective-permute-done.19 = f32[736,128]{1,0:T(8,128)S(1)} collective-permute-done((f32[736,128]{1,0:T(8,128)S(1)}, f32[736,128]{1,0:T(8,128)S(1)}, u32[]{:S(2)}, u32[]{:S(2)}) %collective-permute-start.19) | collective-permute-done | bytes 376864 | tf_op jit(solution)/shard_map/ppermute | solution.py:466
  80.4 0.9 collective-permute-start.20
  81.2 0.4 collective-permute-start.21
  81.7 0.5 collective-permute-start.22
  82.3 8.2 %collective-permute-start.23 = (f32[736,128]{1,0:T(8,128)S(1)}, f32[736,128]{1,0:T(8,128)S(1)}, u32[]{:S(2)}, u32[]{:S(2)}) collective-permute-start(f32[736,128]{1,0:T(8,128)S(1)} %add.68), channel_id=1, source_target_pairs={{0,252},{4,8},{8,4},{12,16},{16,12},{20,24},{24,20},{28,32},{32,28... | collective-permute-start | bytes 1130504 | tf_op jit(solution)/shard_map/ppermute | solution.py:466
  90.5 0.2 collective-permute-done.21.refs_3_
  90.8 0.1 collective-permute-start.25
  90.9 2.0 %gather.5.refs_0_ = f32[736,128]{1,0:T(8,128)S(1)} custom-call(s32[2]{0:T(128)S(1)} %pad_add_fusion.refs_0_, f32[200,128]{1,0:T(8,128)S(1)} %get-tuple-element.100.refs_1_, f32[200,128]{1,0:T(8,128)S(1)} %collective-permute-done.20.refs_2_, f32[200,128]{1,0:T(8,128)S(1)} %collective-permute-done.21.refs_3_, f32[200,128]{1,0:T(8,128)S(1)} %collective-permute-done.22.refs_4_, ...), custom_call_target="tpu_custom_call" | custom-call | tf_op jit(solution)/shard_map/gather/pallas_call | solution.py:413
  92.9 6.2 %collective-permute-done.23 = f32[736,128]{1,0:T(8,128)S(1)} collective-permute-done((f32[736,128]{1,0:T(8,128)S(1)}, f32[736,128]{1,0:T(8,128)S(1)}, u32[]{:S(2)}, u32[]{:S(2)}) %collective-permute-start.23) | collective-permute-done | bytes 376864 | tf_op jit(solution)/shard_map/ppermute | solution.py:466
  99.2 1.5 %collective-permute-done.25.refs_2_ = f32[736,128]{1,0:T(8,128)S(1)} collective-permute-done((f32[736,128]{1,0:T(8,128)S(1)}, f32[736,128]{1,0:T(8,128)S(1)}, u32[]{:S(2)}, u32[]{:S(2)}) %collective-permute-start.25) | collective-permute-done | bytes 376864 | tf_op jit(solution)/shard_map/ppermute | solution.py:466
  100.6 0.8 leave.1
  (32 shorter events, 0.3 us)
Async XLA Ops:
  0.6 1.0 copy-start.4
  1.6 21.1 %copy-start = (bf16[256,256]{1,0:T(8,128)(2,1)S(1)}, bf16[256,256]{1,0:T(8,128)(2,1)}, u32[]{:S(2)}) copy-start(bf16[256,256]{1,0:T(8,128)(2,1)} %constant.68.clone.refs_4_.refs_5_.refs_2_) | copy-start | bytes 393220
  1.6 21.0 %copy-start.3 = (bf16[80,240]{1,0:T(8,128)(2,1)S(1)}, bf16[80,240]{1,0:T(8,128)(2,1)}, u32[]{:S(2)}) copy-start(bf16[80,240]{1,0:T(8,128)(2,1)} %constant.69.clone.refs_5_.refs_6_.refs_3_) | copy-start | bytes 115204
  1.7 12.0 %collective-permute-start.1 = (f32[736,128]{1,0:T(8,128)S(1)}, f32[736,128]{1,0:T(8,128)S(1)}, u32[]{:S(2)}, u32[]{:S(2)}) collective-permute-start(f32[736,128]{1,0:T(8,128)S(1)} %enter.1.refs_1_.refs_7_.own), channel_id=1, source_target_pairs={{0,4},{4,0},{8,12},{12,8},{16,20},{20,16},{24,28},{28,24},{32,36},... | collective-permute-start | bytes 1130504 | tf_op jit(solution)/shard_map/ppermute | solution.py:466
  4.2 18.4 %collective-permute-start = (f32[736,128]{1,0:T(8,128)S(1)}, f32[736,128]{1,0:T(8,128)S(1)}, u32[]{:S(2)}, u32[]{:S(2)}) collective-permute-start(f32[736,128]{1,0:T(8,128)S(1)} %enter.1.refs_1_.refs_7_.own), channel_id=1, source_target_pairs={{0,252},{4,8},{8,4},{12,16},{16,12},{20,24},{24,20},{28,32},{32,28... | collective-permute-start | bytes 1130504 | tf_op jit(solution)/shard_map/ppermute | solution.py:466
  13.7 16.4 %collective-permute-start.2 = (f32[736,128]{1,0:T(8,128)S(1)}, f32[736,128]{1,0:T(8,128)S(1)}, u32[]{:S(2)}, u32[]{:S(2)}) collective-permute-start(f32[736,128]{1,0:T(8,128)S(1)} %collective-permute-done.1.refs_2_.refs_8_), channel_id=1, source_target_pairs={{0,252},{4,8},{8,4},{12,16},{16,12},{20,24},{24,20},{28,32},{32,28... | collective-permute-start | bytes 1130504 | tf_op jit(solution)/shard_map/ppermute | solution.py:466
  22.6 8.4 %collective-permute-start.3 = (f32[736,128]{1,0:T(8,128)S(1)}, f32[736,128]{1,0:T(8,128)S(1)}, u32[]{:S(2)}, u32[]{:S(2)}) collective-permute-start(f32[736,128]{1,0:T(8,128)S(1)} %collective-permute-done.refs_3_.refs_1_.refs_9_.refs_7_), channel_id=1, source_target_pairs={{0,4},{4,0},{8,12},{12,8},{16,20},{20,16},{24,28},{28,24},{32,36},... | collective-permute-start | bytes 1130504 | tf_op jit(solution)/shard_map/ppermute | solution.py:466
  25.8 12.8 %collective-permute-start.4 = (f32[400,128]{1,0:T(8,128)S(1)}, f32[400,128]{1,0:T(8,128)S(1)}, u32[]{:S(2)}, u32[]{:S(2)}) collective-permute-start(f32[400,128]{1,0:T(8,128)S(1)} %get-tuple-element.57), channel_id=1, source_target_pairs={{0,2},{1,3},{2,0},{3,1},{4,6},{5,7},{6,4},{7,5},{8,10},{9,11},{10,... | collective-permute-start | bytes 614408 | tf_op jit(solution)/shard_map/ppermute | solution.py:452
  26.3 13.1 %collective-permute-start.5 = (f32[400,128]{1,0:T(8,128)S(1)}, f32[400,128]{1,0:T(8,128)S(1)}, u32[]{:S(2)}, u32[]{:S(2)}) collective-permute-start(f32[400,128]{1,0:T(8,128)S(1)} %get-tuple-element.58), channel_id=1, source_target_pairs={{0,3},{1,2},{2,1},{3,0},{4,7},{5,6},{6,5},{7,4},{8,11},{9,10},{10,... | collective-permute-start | bytes 614408 | tf_op jit(solution)/shard_map/ppermute | solution.py:452
  29.5 10.0 %collective-permute-start.6 = (f32[400,128]{1,0:T(8,128)S(1)}, f32[400,128]{1,0:T(8,128)S(1)}, u32[]{:S(2)}, u32[]{:S(2)}) collective-permute-start(f32[400,128]{1,0:T(8,128)S(1)} %get-tuple-element.59), channel_id=1, source_target_pairs={{0,1},{1,0},{2,3},{3,2},{4,5},{5,4},{6,7},{7,6},{8,9},{9,8},{10,11... | collective-permute-start | bytes 614408 | tf_op jit(solution)/shard_map/ppermute | solution.py:452
  34.2 10.9 %collective-permute-start.13 = (f32[400,128]{1,0:T(8,128)S(1)}, f32[400,128]{1,0:T(8,128)S(1)}, u32[]{:S(2)}, u32[]{:S(2)}) collective-permute-start(f32[400,128]{1,0:T(8,128)S(1)} %get-tuple-element.63), channel_id=1, source_target_pairs={{0,2},{1,3},{2,0},{3,1},{4,6},{5,7},{6,4},{7,5},{8,10},{9,11},{10,... | collective-permute-start | bytes 614408 | tf_op jit(solution)/shard_map/ppermute | solution.py:452
  34.7 14.1 %collective-permute-start.14 = (f32[400,128]{1,0:T(8,128)S(1)}, f32[400,128]{1,0:T(8,128)S(1)}, u32[]{:S(2)}, u32[]{:S(2)}) collective-permute-start(f32[400,128]{1,0:T(8,128)S(1)} %get-tuple-element.64), channel_id=1, source_target_pairs={{0,3},{1,2},{2,1},{3,0},{4,7},{5,6},{6,5},{7,4},{8,11},{9,10},{10,... | collective-permute-start | bytes 614408 | tf_op jit(solution)/shard_map/ppermute | solution.py:452
  38.7 10.1 %collective-permute-start.15 = (f32[400,128]{1,0:T(8,128)S(1)}, f32[400,128]{1,0:T(8,128)S(1)}, u32[]{:S(2)}, u32[]{:S(2)}) collective-permute-start(f32[400,128]{1,0:T(8,128)S(1)} %get-tuple-element.65), channel_id=1, source_target_pairs={{0,1},{1,0},{2,3},{3,2},{4,5},{5,4},{6,7},{7,6},{8,9},{9,8},{10,11... | collective-permute-start | bytes 614408 | tf_op jit(solution)/shard_map/ppermute | solution.py:452
  38.7 0.9 copy-start.1
  38.7 1.0 copy-start.2
  40.9 10.1 %collective-permute-start.7 = (f32[400,128]{1,0:T(8,128)S(1)}, f32[400,128]{1,0:T(8,128)S(1)}, u32[]{:S(2)}, u32[]{:S(2)}) collective-permute-start(f32[400,128]{1,0:T(8,128)S(1)} %get-tuple-element.72), channel_id=1, source_target_pairs={{0,2},{1,3},{2,0},{3,1},{4,6},{5,7},{6,4},{7,5},{8,10},{9,11},{10,... | collective-permute-start | bytes 614408 | tf_op jit(solution)/shard_map/ppermute | solution.py:452
  41.4 16.1 %collective-permute-start.8 = (f32[400,128]{1,0:T(8,128)S(1)}, f32[400,128]{1,0:T(8,128)S(1)}, u32[]{:S(2)}, u32[]{:S(2)}) collective-permute-start(f32[400,128]{1,0:T(8,128)S(1)} %get-tuple-element.73), channel_id=1, source_target_pairs={{0,3},{1,2},{2,1},{3,0},{4,7},{5,6},{6,5},{7,4},{8,11},{9,10},{10,... | collective-permute-start | bytes 614408 | tf_op jit(solution)/shard_map/ppermute | solution.py:452
  45.1 12.4 %collective-permute-start.9 = (f32[400,128]{1,0:T(8,128)S(1)}, f32[400,128]{1,0:T(8,128)S(1)}, u32[]{:S(2)}, u32[]{:S(2)}) collective-permute-start(f32[400,128]{1,0:T(8,128)S(1)} %get-tuple-element.74), channel_id=1, source_target_pairs={{0,1},{1,0},{2,3},{3,2},{4,5},{5,4},{6,7},{7,6},{8,9},{9,8},{10,11... | collective-permute-start | bytes 614408 | tf_op jit(solution)/shard_map/ppermute | solution.py:452
  50.0 11.5 %collective-permute-start.16 = (f32[400,128]{1,0:T(8,128)S(1)}, f32[400,128]{1,0:T(8,128)S(1)}, u32[]{:S(2)}, u32[]{:S(2)}) collective-permute-start(f32[400,128]{1,0:T(8,128)S(1)} %get-tuple-element.89), channel_id=1, source_target_pairs={{0,2},{1,3},{2,0},{3,1},{4,6},{5,7},{6,4},{7,5},{8,10},{9,11},{10,... | collective-permute-start | bytes 614408 | tf_op jit(solution)/shard_map/ppermute | solution.py:452
  50.5 16.1 %collective-permute-start.17 = (f32[400,128]{1,0:T(8,128)S(1)}, f32[400,128]{1,0:T(8,128)S(1)}, u32[]{:S(2)}, u32[]{:S(2)}) collective-permute-start(f32[400,128]{1,0:T(8,128)S(1)} %get-tuple-element.90), channel_id=1, source_target_pairs={{0,3},{1,2},{2,1},{3,0},{4,7},{5,6},{6,5},{7,4},{8,11},{9,10},{10,... | collective-permute-start | bytes 614408 | tf_op jit(solution)/shard_map/ppermute | solution.py:452
  51.1 15.5 %collective-permute-start.18 = (f32[400,128]{1,0:T(8,128)S(1)}, f32[400,128]{1,0:T(8,128)S(1)}, u32[]{:S(2)}, u32[]{:S(2)}) collective-permute-start(f32[400,128]{1,0:T(8,128)S(1)} %get-tuple-element.91), channel_id=1, source_target_pairs={{0,1},{1,0},{2,3},{3,2},{4,5},{5,4},{6,7},{7,6},{8,9},{9,8},{10,11... | collective-permute-start | bytes 614408 | tf_op jit(solution)/shard_map/ppermute | solution.py:452
  61.0 9.2 %collective-permute-start.10 = (f32[200,128]{1,0:T(8,128)S(1)}, f32[200,128]{1,0:T(8,128)S(1)}, u32[]{:S(2)}, u32[]{:S(2)}) collective-permute-start(f32[200,128]{1,0:T(8,128)S(1)} %get-tuple-element.77), channel_id=1, source_target_pairs={{0,2},{1,3},{2,0},{3,1},{4,6},{5,7},{6,4},{7,5},{8,10},{9,11},{10,... | collective-permute-start | bytes 307208 | tf_op jit(solution)/shard_map/ppermute | solution.py:452
  61.4 8.8 %collective-permute-start.11 = (f32[200,128]{1,0:T(8,128)S(1)}, f32[200,128]{1,0:T(8,128)S(1)}, u32[]{:S(2)}, u32[]{:S(2)}) collective-permute-start(f32[200,128]{1,0:T(8,128)S(1)} %get-tuple-element.78), channel_id=1, source_target_pairs={{0,3},{1,2},{2,1},{3,0},{4,7},{5,6},{6,5},{7,4},{8,11},{9,10},{10,... | collective-permute-start | bytes 307208 | tf_op jit(solution)/shard_map/ppermute | solution.py:452
  61.6 8.7 %collective-permute-start.12 = (f32[200,128]{1,0:T(8,128)S(1)}, f32[200,128]{1,0:T(8,128)S(1)}, u32[]{:S(2)}, u32[]{:S(2)}) collective-permute-start(f32[200,128]{1,0:T(8,128)S(1)} %get-tuple-element.79), channel_id=1, source_target_pairs={{0,1},{1,0},{2,3},{3,2},{4,5},{5,4},{6,7},{7,6},{8,9},{9,8},{10,11... | collective-permute-start | bytes 307208 | tf_op jit(solution)/shard_map/ppermute | solution.py:452
  70.2 10.1 %collective-permute-start.19 = (f32[736,128]{1,0:T(8,128)S(1)}, f32[736,128]{1,0:T(8,128)S(1)}, u32[]{:S(2)}, u32[]{:S(2)}) collective-permute-start(f32[736,128]{1,0:T(8,128)S(1)} %get-tuple-element.99), channel_id=1, source_target_pairs={{0,4},{4,0},{8,12},{12,8},{16,20},{20,16},{24,28},{28,24},{32,36},... | collective-permute-start | bytes 1130504 | tf_op jit(solution)/shard_map/ppermute | solution.py:466
  70.3 20.4 %collective-permute-start.24 = (f32[736,128]{1,0:T(8,128)S(1)}, f32[736,128]{1,0:T(8,128)S(1)}, u32[]{:S(2)}, u32[]{:S(2)}) collective-permute-start(f32[736,128]{1,0:T(8,128)S(1)} %get-tuple-element.105), channel_id=1, source_target_pairs={{0,252},{4,8},{8,4},{12,16},{16,12},{20,24},{24,20},{28,32},{32,28... | collective-permute-start | bytes 1130504 | tf_op jit(solution)/shard_map/ppermute | solution.py:466
  80.4 10.1 %collective-permute-start.20 = (f32[200,128]{1,0:T(8,128)S(1)}, f32[200,128]{1,0:T(8,128)S(1)}, u32[]{:S(2)}, u32[]{:S(2)}) collective-permute-start(f32[200,128]{1,0:T(8,128)S(1)} %get-tuple-element.101), channel_id=1, source_target_pairs={{0,2},{1,3},{2,0},{3,1},{4,6},{5,7},{6,4},{7,5},{8,10},{9,11},{10,... | collective-permute-start | bytes 307208 | tf_op jit(solution)/shard_map/ppermute | solution.py:452
  81.2 9.5 %collective-permute-start.21 = (f32[200,128]{1,0:T(8,128)S(1)}, f32[200,128]{1,0:T(8,128)S(1)}, u32[]{:S(2)}, u32[]{:S(2)}) collective-permute-start(f32[200,128]{1,0:T(8,128)S(1)} %get-tuple-element.102), channel_id=1, source_target_pairs={{0,3},{1,2},{2,1},{3,0},{4,7},{5,6},{6,5},{7,4},{8,11},{9,10},{10,... | collective-permute-start | bytes 307208 | tf_op jit(solution)/shard_map/ppermute | solution.py:452
  81.7 9.0 %collective-permute-start.22 = (f32[200,128]{1,0:T(8,128)S(1)}, f32[200,128]{1,0:T(8,128)S(1)}, u32[]{:S(2)}, u32[]{:S(2)}) collective-permute-start(f32[200,128]{1,0:T(8,128)S(1)} %get-tuple-element.103), channel_id=1, source_target_pairs={{0,1},{1,0},{2,3},{3,2},{4,5},{5,4},{6,7},{7,6},{8,9},{9,8},{10,11... | collective-permute-start | bytes 307208 | tf_op jit(solution)/shard_map/ppermute | solution.py:452
  82.3 16.9 %collective-permute-start.23 = (f32[736,128]{1,0:T(8,128)S(1)}, f32[736,128]{1,0:T(8,128)S(1)}, u32[]{:S(2)}, u32[]{:S(2)}) collective-permute-start(f32[736,128]{1,0:T(8,128)S(1)} %add.68), channel_id=1, source_target_pairs={{0,252},{4,8},{8,4},{12,16},{16,12},{20,24},{24,20},{28,32},{32,28... | collective-permute-start | bytes 1130504 | tf_op jit(solution)/shard_map/ppermute | solution.py:466
  90.8 9.9 %collective-permute-start.25 = (f32[736,128]{1,0:T(8,128)S(1)}, f32[736,128]{1,0:T(8,128)S(1)}, u32[]{:S(2)}, u32[]{:S(2)}) collective-permute-start(f32[736,128]{1,0:T(8,128)S(1)} %add.70), channel_id=1, source_target_pairs={{0,4},{4,0},{8,12},{12,8},{16,20},{20,16},{24,28},{28,24},{32,36},... | collective-permute-start | bytes 1130504 | tf_op jit(solution)/shard_map/ppermute | solution.py:466
